TPU v7x, 32 devices: a whole 2x2x4 slice. The times are simulated.
32 devices in a mesh: dp: 4 (over y, core), mp: 8 (over z, x).
Axes of the slice: x: 2, y: 2, z: 4, core: 2. Of those that a mesh axis runs over, the one named last changes fastest.
Arguments:
- hidden_in: bfloat16 [8, 512, 768], P('dp', 'mp'), may hold values from -6 to 6
- cotangent: bfloat16 [8, 512, 768], P('dp', 'mp'), may hold values from -6 to 6
- lengths: int32 [8], P('dp'), may hold values from 64 to 512, as said below
- teacher_attn_in: bfloat16 [768, 2304], P(('dp', 'mp')), may hold values from -0.21875 to 0.21875
- teacher_attn_out: bfloat16 [768, 768], P(None, ('dp', 'mp')), may hold values from -2.5 to 2.5
- teacher_ffn_in: bfloat16 [768, 3072], P('dp', 'mp'), may hold values from -0.21875 to 0.21875
- teacher_ffn_out: bfloat16 [3072, 768], P('mp', 'dp'), may hold values from -0.109375 to 0.109375
- teacher_shifts: bfloat16 [7680], P(('dp', 'mp')), may hold values from -3 to 3
- teacher_gains: bfloat16 [1536], P(('dp', 'mp')), may hold values from 0.25 to 1.75
- student_attn_in: bfloat16 [768, 1152], P(('dp', 'mp')), may hold values from -0.21875 to 0.21875
- student_attn_out: bfloat16 [384, 768], P(None, ('dp', 'mp')), may hold values from -3.5 to 3.5
- student_ffn_in: bfloat16 [768, 1536], P('dp', 'mp'), may hold values from -0.21875 to 0.21875
- student_ffn_out: bfloat16 [1536, 768], P('mp', 'dp'), may hold values from -0.15625 to 0.15625
- student_shifts: bfloat16 [5376], P(('dp', 'mp')), may hold values from -3 to 3
- student_gains: bfloat16 [1536], P(('dp', 'mp')), may hold values from 0.25 to 1.75
Outputs:
- out: bfloat16 [8, 512, 768], P('dp', 'mp')
- grad_hidden: float32 [8, 512, 768], P('dp', 'mp')
- grad_teacher_attn_in: float32 [768, 2304], P(('dp', 'mp'))
- grad_teacher_attn_out: float32 [768, 768], P(None, ('dp', 'mp'))
- grad_teacher_ffn_in: float32 [768, 3072], P('dp', 'mp')
- grad_teacher_ffn_out: float32 [3072, 768], P('mp', 'dp')
- grad_teacher_shifts: float32 [7680], P(('dp', 'mp'))
- grad_teacher_gains: float32 [1536], P(('dp', 'mp'))
- grad_student_attn_in: float32 [768, 1152], P(('dp', 'mp'))
- grad_student_attn_out: float32 [384, 768], P(None, ('dp', 'mp'))
- grad_student_ffn_in: float32 [768, 1536], P('dp', 'mp')
- grad_student_ffn_out: float32 [1536, 768], P('mp', 'dp')
- grad_student_shifts: float32 [5376], P(('dp', 'mp'))
- grad_student_gains: float32 [1536], P(('dp', 'mp'))
Inputs may be any that keep to these rules, and one draw needn't show every extreme that they name: `lengths`: each length lies between 64 and 512; in every aligned block of 2 rows at least one row has length 512.
All inputs are finite; a program needn't handle non-finite values.
Results may differ from a plain program's by a relative error of at most 0.028.
Values may be sent and summed in bfloat16 or wider, within the bound.
A program may use at most 192 MiB of HBM per device.

v0:
```python
import jax
import jax.numpy as jnp
from jax import lax
from jax.sharding import PartitionSpec as P

HEAD = 64


EPSILON = 1e-06
NEGATIVE = -1e30


def layer_norm(values, gain, shift):
    centered = values - jnp.mean(values, axis=-1, keepdims=True)
    variance = jnp.mean(centered * centered, axis=-1, keepdims=True)
    return centered * lax.rsqrt(variance + EPSILON) * gain + shift


def smooth_gate(pre_act):
    return jax.nn.gelu(pre_act, approximate=False)


def split_shifts(shifts, head_width, model_width, hidden_width):
    spans_list = [
        head_width,
        head_width,
        model_width,
        model_width,
        hidden_width,
        model_width,
        model_width,
    ]
    pieces = []
    offset = 0
    for length in spans_list:
        pieces.append(shifts[offset : offset + length])
        offset = offset + length
    return pieces


def to_heads(values):
    return values.reshape(values.shape[0], values.shape[1], values.shape[2] // HEAD, HEAD)


def score_block(queries, all_keys, valid_keys):
    raw = jnp.einsum(
        "rqhd,rkhd->rhqk", to_heads(queries), to_heads(all_keys), preferred_element_type=jnp.float32
    )
    return jnp.where(valid_keys[:, None, None, :], raw * 0.125, NEGATIVE)


def fetch(attn_in, attn_out, ffn_in, ffn_out, shifts, gains):
    whole_in, whole_out, whole_shifts, whole_gains = (
        lax.all_gather(attn_in, ("dp", "mp"), axis=0, tiled=True),
        lax.all_gather(attn_out, ("dp", "mp"), axis=1, tiled=True),
        lax.all_gather(shifts, ("dp", "mp"), axis=0, tiled=True),
        lax.all_gather(gains, ("dp", "mp"), axis=0, tiled=True),
    )
    ffn_first, ffn_second = (
        lax.all_gather(ffn_in, "dp", axis=0, tiled=True),
        lax.all_gather(ffn_out, "dp", axis=1, tiled=True),
    )
    return (
        whole_in,
        whole_out,
        ffn_first,
        ffn_second,
        whole_shifts.astype(jnp.float32),
        whole_gains.astype(jnp.float32),
    )


def forward_layer(hidden, params, valid_keys):
    attn_in, attn_out, ffn_first, ffn_second, shifts, gains = params
    model_width = hidden.shape[-1]
    head_width = attn_in.shape[1] // 3
    hidden_width = shifts.shape[0] - 2 * head_width - 4 * model_width
    pieces = split_shifts(shifts, head_width, model_width, hidden_width)
    bias_query, bias_value, bias_output, shift_one, bias_up, bias_down, shift_two = pieces
    hidden_low = hidden.astype(jnp.bfloat16)
    projected = jnp.einsum("rsd,de->rse", hidden_low, attn_in, preferred_element_type=jnp.float32)
    queries = (projected[..., :head_width] + bias_query).astype(jnp.bfloat16)
    local_keys = projected[..., head_width : 2 * head_width].astype(jnp.bfloat16)
    local_values = (projected[..., 2 * head_width :] + bias_value).astype(jnp.bfloat16)
    all_keys, all_values = (
        lax.all_gather(local_keys, "mp", axis=1, tiled=True),
        lax.all_gather(local_values, "mp", axis=1, tiled=True),
    )
    scores = score_block(queries, all_keys, valid_keys)
    row_max = jnp.max(scores, axis=-1, keepdims=True)
    exponent = jnp.exp(scores - row_max)
    row_total = jnp.sum(exponent, axis=-1, keepdims=True)
    log_total = row_max + jnp.log(row_total)
    weights_low = (exponent / row_total).astype(jnp.bfloat16)
    mixed = jnp.einsum(
        "rhqk,rkhd->rqhd", weights_low, to_heads(all_values), preferred_element_type=jnp.float32
    )
    context = mixed.reshape(queries.shape).astype(jnp.bfloat16)
    branch = (
        jnp.einsum("rsh,hd->rsd", context, attn_out, preferred_element_type=jnp.float32)
        + bias_output
    )
    summed_one = hidden + branch
    normed_one = layer_norm(summed_one, gains[:model_width], shift_one)
    normed_low = normed_one.astype(jnp.bfloat16)
    ffn_tokens = lax.all_gather(normed_low, "mp", axis=1, tiled=True)
    local_hidden = ffn_first.shape[1]
    bias_part = lax.dynamic_slice_in_dim(bias_up, lax.axis_index("mp") * local_hidden, local_hidden)
    pre_act = (
        jnp.einsum("rsd,df->rsf", ffn_tokens, ffn_first, preferred_element_type=jnp.float32)
        + bias_part
    )
    act_low = smooth_gate(pre_act).astype(jnp.bfloat16)
    down_terms = jnp.einsum("rsf,fd->rsd", act_low, ffn_second, preferred_element_type=jnp.float32)
    ffn_down = lax.psum_scatter(
        down_terms.astype(jnp.bfloat16), "mp", scatter_dimension=1, tiled=True
    ).astype(jnp.float32)
    summed_two = normed_one + ffn_down + bias_down
    result = layer_norm(summed_two, gains[model_width:], shift_two)
    key_store = (all_keys, all_values)
    kept = (
        hidden_low,
        queries,
        key_store,
        log_total,
        context,
        summed_one,
        ffn_tokens,
        pre_act,
        act_low,
        summed_two,
    )
    return (result, kept)


def backward_layer(grad_out, kept, params, valid_keys):
    attn_in, attn_out, ffn_first, ffn_second, shifts, gains = params
    (
        hidden_low,
        queries,
        key_store,
        log_total,
        context,
        summed_one,
        ffn_tokens,
        pre_act,
        act_low,
        summed_two,
    ) = kept
    model_width = summed_one.shape[-1]
    head_width = attn_in.shape[1] // 3
    hidden_width = shifts.shape[0] - 2 * head_width - 4 * model_width
    pieces = split_shifts(shifts, head_width, model_width, hidden_width)
    bias_query, bias_value, bias_output, shift_one, bias_up, bias_down, shift_two = pieces
    sum_axes = (0, 1)
    unused_two, norm_two_back = jax.vjp(layer_norm, summed_two, gains[model_width:], shift_two)
    grad_two, grad_gain_two, grad_shift_two = norm_two_back(grad_out)
    grad_down = grad_two.astype(jnp.bfloat16)
    grad_bias_down = jnp.sum(grad_down.astype(jnp.float32), axis=sum_axes)
    grad_tokens = lax.all_gather(grad_down, "mp", axis=1, tiled=True)
    grad_act = jnp.einsum(
        "rsd,fd->rsf", grad_tokens, ffn_second, preferred_element_type=jnp.float32
    )
    grad_second = jnp.einsum(
        "rsf,rsd->fd", act_low, grad_tokens, preferred_element_type=jnp.float32
    )
    unused_gate, gate_back = jax.vjp(smooth_gate, pre_act)
    grad_pre = gate_back(grad_act)[0].astype(jnp.bfloat16)
    grad_bias_part = jnp.sum(grad_pre.astype(jnp.float32), axis=sum_axes)
    grad_first = jnp.einsum("rsd,rsf->df", ffn_tokens, grad_pre, preferred_element_type=jnp.float32)
    back_terms = jnp.einsum("rsf,df->rsd", grad_pre, ffn_first, preferred_element_type=jnp.float32)
    grad_normed = lax.psum_scatter(
        back_terms.astype(jnp.bfloat16), "mp", scatter_dimension=1, tiled=True
    ).astype(jnp.float32)
    blank_bias = jnp.zeros((hidden_width,), jnp.float32)
    grad_bias_up = lax.dynamic_update_slice_in_dim(
        blank_bias, grad_bias_part, lax.axis_index("mp") * ffn_first.shape[1], 0
    )
    grad_normed = grad_normed + grad_two
    unused_one, norm_one_back = jax.vjp(layer_norm, summed_one, gains[:model_width], shift_one)
    grad_one, grad_gain_one, grad_shift_one = norm_one_back(grad_normed)
    grad_branch = grad_one.astype(jnp.bfloat16)
    grad_bias_output = jnp.sum(grad_branch.astype(jnp.float32), axis=sum_axes)
    grad_attn_out = jnp.einsum(
        "rsh,rsd->hd", context, grad_branch, preferred_element_type=jnp.float32
    )
    grad_context = jnp.einsum(
        "rsd,hd->rsh", grad_branch, attn_out, preferred_element_type=jnp.float32
    ).astype(jnp.bfloat16)
    stored_keys, stored_values = key_store
    all_keys, all_values = (stored_keys, stored_values)
    weights = jnp.exp(score_block(queries, all_keys, valid_keys) - log_total)
    context_heads = to_heads(grad_context)
    grad_weights = jnp.einsum(
        "rqhd,rkhd->rhqk", context_heads, to_heads(all_values), preferred_element_type=jnp.float32
    )
    inner_sum = jnp.sum(weights * grad_weights, axis=-1, keepdims=True)
    grad_raw = (0.125 * weights * (grad_weights - inner_sum)).astype(jnp.bfloat16)
    grad_queries = jnp.einsum(
        "rhqk,rkhd->rqhd", grad_raw, to_heads(all_keys), preferred_element_type=jnp.float32
    )
    grad_queries = grad_queries.reshape(queries.shape).astype(jnp.bfloat16)
    weights_low = weights.astype(jnp.bfloat16)
    value_terms = jnp.einsum(
        "rhqk,rqhd->rkhd", weights_low, context_heads, preferred_element_type=jnp.float32
    )
    key_terms = jnp.einsum(
        "rhqk,rqhd->rkhd", grad_raw, to_heads(queries), preferred_element_type=jnp.float32
    )
    key_terms = key_terms.reshape(all_keys.shape)
    value_terms = value_terms.reshape(all_values.shape)
    grad_keys, grad_values = (
        lax.psum_scatter(
            key_terms.astype(jnp.bfloat16), "mp", scatter_dimension=1, tiled=True
        ).astype(jnp.float32),
        lax.psum_scatter(
            value_terms.astype(jnp.bfloat16), "mp", scatter_dimension=1, tiled=True
        ).astype(jnp.float32),
    )
    grad_values_low = grad_values.astype(jnp.bfloat16)
    grad_projected = jnp.concatenate(
        [grad_queries, grad_keys.astype(jnp.bfloat16), grad_values_low], axis=-1
    )
    grad_attn_in = jnp.einsum(
        "rsd,rse->de", hidden_low, grad_projected, preferred_element_type=jnp.float32
    )
    grad_hidden = grad_one + jnp.einsum(
        "rse,de->rsd", grad_projected, attn_in, preferred_element_type=jnp.float32
    )
    grad_bias_query = jnp.sum(grad_queries.astype(jnp.float32), axis=sum_axes)
    grad_bias_value = jnp.sum(grad_values_low.astype(jnp.float32), axis=sum_axes)
    grad_shifts = jnp.concatenate(
        [
            grad_bias_query,
            grad_bias_value,
            grad_bias_output,
            grad_shift_one,
            grad_bias_up,
            grad_bias_down,
            grad_shift_two,
        ]
    )
    grad_gains = jnp.concatenate([grad_gain_one, grad_gain_two])
    return (
        grad_hidden,
        (grad_attn_in, grad_attn_out, grad_first, grad_second, grad_shifts, grad_gains),
    )


def reduce_grads(grads):
    grad_attn_in, grad_attn_out, grad_first, grad_second, grad_shifts, grad_gains = grads
    total_in, total_out, total_shifts, total_gains = (
        lax.psum_scatter(grad_attn_in, ("dp", "mp"), scatter_dimension=0, tiled=True),
        lax.psum_scatter(grad_attn_out, ("dp", "mp"), scatter_dimension=1, tiled=True),
        lax.psum_scatter(grad_shifts, ("dp", "mp"), scatter_dimension=0, tiled=True),
        lax.psum_scatter(grad_gains, ("dp", "mp"), scatter_dimension=0, tiled=True),
    )
    total_first, total_second = (
        lax.psum_scatter(
            grad_first.astype(jnp.bfloat16), "dp", scatter_dimension=0, tiled=True
        ).astype(jnp.float32),
        lax.psum_scatter(
            grad_second.astype(jnp.bfloat16), "dp", scatter_dimension=1, tiled=True
        ).astype(jnp.float32),
    )
    return (total_in, total_out, total_first, total_second, total_shifts, total_gains)


def body(
    hidden_in,
    cotangent,
    lengths,
    teacher_attn_in,
    teacher_attn_out,
    teacher_ffn_in,
    teacher_ffn_out,
    teacher_shifts,
    teacher_gains,
    student_attn_in,
    student_attn_out,
    student_ffn_in,
    student_ffn_out,
    student_shifts,
    student_gains,
):
    span_len = hidden_in.shape[1] * lax.axis_size("mp")
    positions = jnp.arange(span_len)
    valid_keys = positions[None, :] < lengths[:, None]
    teacher = fetch(
        teacher_attn_in,
        teacher_attn_out,
        teacher_ffn_in,
        teacher_ffn_out,
        teacher_shifts,
        teacher_gains,
    )
    student = fetch(
        student_attn_in,
        student_attn_out,
        student_ffn_in,
        student_ffn_out,
        student_shifts,
        student_gains,
    )
    middle, teacher_kept = forward_layer(hidden_in.astype(jnp.float32), teacher, valid_keys)
    final, student_kept = forward_layer(middle, student, valid_keys)
    grad_middle, student_grads = backward_layer(
        cotangent.astype(jnp.float32), student_kept, student, valid_keys
    )
    grad_input, teacher_grads = backward_layer(grad_middle, teacher_kept, teacher, valid_keys)
    teacher_totals = reduce_grads(teacher_grads)
    student_totals = reduce_grads(student_grads)
    return (final.astype(jnp.bfloat16), grad_input) + teacher_totals + student_totals


def solution(mesh):
    in_specs = (
        P("dp", "mp", None),
        P("dp", "mp", None),
        P("dp"),
        P(("dp", "mp"), None),
        P(None, ("dp", "mp")),
        P("dp", "mp"),
        P("mp", "dp"),
        P(("dp", "mp")),
        P(("dp", "mp")),
        P(("dp", "mp"), None),
        P(None, ("dp", "mp")),
        P("dp", "mp"),
        P("mp", "dp"),
        P(("dp", "mp")),
        P(("dp", "mp")),
    )
    out_specs = (
        P("dp", "mp", None),
        P("dp", "mp", None),
        P(("dp", "mp"), None),
        P(None, ("dp", "mp")),
        P("dp", "mp"),
        P("mp", "dp"),
        P(("dp", "mp")),
        P(("dp", "mp")),
        P(("dp", "mp"), None),
        P(None, ("dp", "mp")),
        P("dp", "mp"),
        P("mp", "dp"),
        P(("dp", "mp")),
        P(("dp", "mp")),
    )
    return jax.shard_map(body, mesh=mesh, in_specs=in_specs, out_specs=out_specs, check_vma=False)
```

profile of v0, /device:TPU:0, one launch (start us, length us, event | category | flops | bytes accessed | tf_op | source)
XLA Modules:
  0.0 1676.0 jit_solution(16617810036594969817)
XLA Ops:
  11.4 43.0 %all-reduce.11 = (bf16[7680]{0:T(1024)(128)(2,1)S(1)}, bf16[1536]{0:T(1024)(128)(2,1)S(1)}, bf16[5376]{0:T(1024)(128)(2,1)}, bf16[1536]{0:T(1024)(128)(2,1)}) all-reduce(bf16[7680]{0:T(1024)(128)(2,1)S(1)} %dynamic-update-slice, bf16[1536]{0:T(1024)(128)(2,1)S(1)} %dynamic-update-slice.1, ...), channel_id=1, replica_groups=mesh['dp'=4,'mp'=8] {'dp','mp'}, use_global_device_ids=true, to_apply=%add | all-reduce | flops 16128 | bytes 64512
  55.0 19.1 %all-gather.10.cloned.1.call-done = bf16[768,2304]{1,0:T(8,128)(2,1)} async-done(((bf16[24,2304]{1,0:T(8,128)(2,1)}), bf16[768,2304]{1,0:T(8,128)(2,1)}) %all-gather.10.cloned.1.call-update) | async-done | bytes 3538960 | tf_op jit(solution)/shard_map/all_gather | solution.py:54
  74.1 2.8 fusion.2
  79.9 40.8 %all-gather.12.cloned.1.call-done = bf16[2,512,768]{2,1,0:T(8,128)(2,1)} async-done(((bf16[2,64,768]{2,1,0:T(8,128)(2,1)}), bf16[2,512,768]{2,1,0:T(8,128)(2,1)}) %all-gather.12.cloned.1.call-update) | async-done | bytes 1572880 | tf_op jit(solution)/shard_map/all_gather | solution.py:87
  123.4 43.2 %all-gather.14.cloned.1.call-done = bf16[2,512,768]{2,1,0:T(8,128)(2,1)} async-done(((bf16[2,64,768]{2,1,0:T(8,128)(2,1)}), bf16[2,512,768]{2,1,0:T(8,128)(2,1)}) %all-gather.14.cloned.1.call-update) | async-done | bytes 1572880 | tf_op jit(solution)/shard_map/all_gather | solution.py:86
  174.5 47.9 %all-gather.16.cloned.1.call-done = bf16[768,768]{0,1:T(8,128)(2,1)} async-done(((bf16[768,24]{0,1:T(8,128)(2,1)}), bf16[768,768]{0,1:T(8,128)(2,1)}) %all-gather.16.cloned.1.call-update) | async-done | bytes 1179664 | tf_op jit(solution)/shard_map/all_gather | solution.py:55
  226.2 8.0 all_gather.67
  234.3 8.1 all_gather.68
  242.3 27.0 %all-gather.18.cloned.1.call-done = bf16[2,512,768]{2,1,0:T(8,128)(2,1)} async-done(((bf16[2,64,768]{2,1,0:T(8,128)(2,1)}), bf16[2,512,768]{2,1,0:T(8,128)(2,1)}) %all-gather.18.cloned.1.call-update) | async-done | bytes 1572880 | tf_op jit(solution)/shard_map/all_gather | solution.py:106
  269.3 2.9 fusion.65
  272.3 4.5 multiply_convert_fusion.2
  282.5 75.5 %all_gather.73 = bf16[384,768]{0,1:T(8,128)(2,1)} all-gather(bf16[384,24]{0,1:T(8,128)(2,1)S(1)} %copy-done.76), channel_id=1, replica_groups=mesh['dp'=4,'mp'=8] {'dp','mp'}, dimensions={1}, use_global_device_ids=true | all-gather | bytes 608256 | tf_op jit(solution)/shard_map/all_gather | solution.py:55
  360.8 41.6 %all-gather.20.cloned.1.call-done = bf16[768,1152]{1,0:T(8,128)(2,1)} async-done(((bf16[24,1152]{1,0:T(8,128)(2,1)}), bf16[768,1152]{1,0:T(8,128)(2,1)}) %all-gather.20.cloned.1.call-update) | async-done | bytes 1769488 | tf_op jit(solution)/shard_map/all_gather | solution.py:54
  406.4 34.3 %all_gather.71 = bf16[2,512,384]{2,1,0:T(8,128)(2,1)} all-gather(bf16[2,64,384]{2,1,0:T(8,128)(2,1)S(1)} %get-tuple-element.107), channel_id=1, replica_groups=mesh['dp'=4,'mp'=8] {'mp'}, dimensions={1}, use_global_device_ids=true | all-gather | bytes 884736 | tf_op jit(solution)/shard_map/all_gather | solution.py:87
  444.6 34.2 %all_gather.72 = bf16[2,512,384]{2,1,0:T(8,128)(2,1)} all-gather(bf16[2,64,384]{2,1,0:T(8,128)(2,1)} %slice.141), channel_id=1, replica_groups=mesh['dp'=4,'mp'=8] {'mp'}, dimensions={1}, use_global_device_ids=true | all-gather | bytes 884736 | tf_op jit(solution)/shard_map/all_gather | solution.py:86
  491.0 7.7 all_gather.76
  498.7 7.6 all_gather.77
  506.3 23.8 %all-gather.22.cloned.1.call-done = bf16[2,512,768]{2,1,0:T(8,128)(2,1)} async-done(((bf16[2,64,768]{2,1,0:T(8,128)(2,1)}), bf16[2,512,768]{2,1,0:T(8,128)(2,1)}) %all-gather.22.cloned.1.call-update) | async-done | bytes 1572880 | tf_op jit(solution)/shard_map/all_gather | solution.py:106
  533.4 2.7 multiply_convert_fusion.3
  538.7 63.8 %reduce-scatter.27.cloned.1.call-done = bf16[2,64,768]{2,1,0:T(8,128)(2,1)} async-done(((bf16[2,512,768]{2,1,0:T(8,128)(2,1)}), bf16[2,64,768]{2,1,0:T(8,128)(2,1)}) %reduce-scatter.27.cloned.1.call-update) | async-done | bytes 196624 | tf_op jit(solution)/shard_map/reduce_scatter | solution.py:115
  609.0 43.2 %all-gather.24.cloned.1.call-done = bf16[2,512,768]{2,1,0:T(8,128)(2,1)} async-done(((bf16[2,64,768]{2,1,0:T(8,128)(2,1)}), bf16[2,512,768]{2,1,0:T(8,128)(2,1)}) %all-gather.24.cloned.1.call-update) | async-done | bytes 1572880 | tf_op jit(solution)/shard_map/all_gather | solution.py:160
  652.2 3.5 convert_reduce_fusion.1
  659.1 63.1 %reduce-scatter.29.cloned.1.call-done = bf16[2,64,768]{2,1,0:T(8,128)(2,1)} async-done(((bf16[2,512,768]{2,1,0:T(8,128)(2,1)}), bf16[2,64,768]{2,1,0:T(8,128)(2,1)}) %reduce-scatter.29.cloned.1.call-update) | async-done | bytes 196624 | tf_op jit(solution)/shard_map/reduce_scatter | solution.py:172
  738.8 2.9 convolution_convert_fusion.6
  750.6 49.5 %reduce-scatter.31.cloned.1.call-done = bf16[2,64,384]{2,1,0:T(8,128)(2,1)} async-done(((bf16[2,512,384]{2,1,0:T(8,128)(2,1)}), bf16[2,64,384]{2,1,0:T(8,128)(2,1)}) %reduce-scatter.31.cloned.1.call-update) | async-done | bytes 98320 | tf_op jit(solution)/shard_map/reduce_scatter | solution.py:213
  801.6 63.3 %reduce-scatter.33.cloned.1.call-done = bf16[2,64,384]{2,1,0:T(8,128)(2,1)} async-done(((bf16[2,512,384]{2,1,0:T(8,128)(2,1)}), bf16[2,64,384]{2,1,0:T(8,128)(2,1)}) %reduce-scatter.33.cloned.1.call-update) | async-done | bytes 98320 | tf_op jit(solution)/shard_map/reduce_scatter | solution.py:216
  866.4 3.0 multiply_reduce_fusion.3
  871.9 43.3 %all-gather.26.cloned.1.call-done = bf16[2,512,768]{2,1,0:T(8,128)(2,1)} async-done(((bf16[2,64,768]{2,1,0:T(8,128)(2,1)}), bf16[2,512,768]{2,1,0:T(8,128)(2,1)}) %all-gather.26.cloned.1.call-update) | async-done | bytes 1572880 | tf_op jit(solution)/shard_map/all_gather | solution.py:160
  915.1 4.6 convert_reduce_fusion
  923.6 63.0 %reduce-scatter.35.cloned.1.call-done = bf16[2,64,768]{2,1,0:T(8,128)(2,1)} async-done(((bf16[2,512,768]{2,1,0:T(8,128)(2,1)}), bf16[2,64,768]{2,1,0:T(8,128)(2,1)}) %reduce-scatter.35.cloned.1.call-update) | async-done | bytes 196624 | tf_op jit(solution)/shard_map/reduce_scatter | solution.py:172
  1004.1 2.8 convolution_convert_fusion
  1007.0 2.7 copy.104
  1012.2 2.8 fusion.22
  1015.1 3.6 fusion.20
  1031.4 36.6 %reduce-scatter.37.cloned.1.call-done = bf16[2,64,768]{2,1,0:T(8,128)(2,1)} async-done(((bf16[2,512,768]{2,1,0:T(8,128)(2,1)}), bf16[2,64,768]{2,1,0:T(8,128)(2,1)}) %reduce-scatter.37.cloned.1.call-update) | async-done | bytes 196624 | tf_op jit(solution)/shard_map/reduce_scatter | solution.py:213
  1069.0 66.5 %reduce-scatter.39.cloned.1.call-done = bf16[2,64,768]{2,1,0:T(8,128)(2,1)} async-done(((bf16[2,512,768]{2,1,0:T(8,128)(2,1)}), bf16[2,64,768]{2,1,0:T(8,128)(2,1)}) %reduce-scatter.39.cloned.1.call-update) | async-done | bytes 196624 | tf_op jit(solution)/shard_map/reduce_scatter | solution.py:216
  1136.4 4.1 convolution_bitcast_fusion
  1140.5 8.1 copy.118
  1149.6 8.0 reduce-scatter.51.cloned.1.call-done
  1160.8 20.1 %reduce-scatter.47.cloned.1.call-done = bf16[192,192]{1,0:T(8,128)(2,1)} async-done(((bf16[768,192]{1,0:T(8,128)(2,1)}), bf16[192,192]{1,0:T(8,128)(2,1)}) %reduce-scatter.47.cloned.1.call-update) | async-done | bytes 73744 | tf_op jit(solution)/shard_map/reduce_scatter | solution.py:259
  1193.4 11.9 reduce-scatter.43.cloned.1.call-done
  1207.0 23.0 %reduce-scatter.45.cloned.1.call-done = bf16[384,192]{0,1:T(8,128)(2,1)} async-done(((bf16[384,768]{0,1:T(8,128)(2,1)}), bf16[384,192]{0,1:T(8,128)(2,1)}) %reduce-scatter.45.cloned.1.call-update) | async-done | bytes 147472 | tf_op jit(solution)/shard_map/reduce_scatter | solution.py:262
  1243.1 40.8 %all-reduce.10 = (f32[7680]{0:T(1024)}, f32[1536]{0:T(1024)S(1)}, f32[5376]{0:T(1024)}, f32[1536]{0:T(1024)S(1)}) all-reduce(f32[7680]{0:T(1024)} %get-tuple-element.150, f32[1536]{0:T(1024)} %get-tuple-element.148, f32[5376]{0:T(1024)} %get-tuple-element.151, ...), channel_id=14, replica_groups=mesh['dp'=4,'mp'=8] {'dp','mp'}, use_global_device_ids=true, to_apply=%region_41.42.clone | all-reduce | flops 16128 | bytes 129024
  1287.8 3.2 fusion.28
  1291.0 40.9 %reduce-scatter.55.cloned.1.call-done = f32[384,24]{0,1:T(8,128)} async-done(((f32[384,768]{0,1:T(8,128)}), f32[384,24]{0,1:T(8,128)}) %reduce-scatter.55.cloned.1.call-update) | async-done | bytes 36880
  1331.9 108.1 %reduce-scatter.53.cloned.1.call-done = f32[24,1152]{1,0:T(8,128)} async-done(((f32[768,1152]{1,0:T(8,128)}), f32[24,1152]{1,0:T(8,128)}) %reduce-scatter.53.cloned.1.call-update) | async-done | bytes 110608
  1440.0 103.7 %reduce-scatter.41.cloned.1.call-done = f32[768,24]{0,1:T(8,128)} async-done(((f32[768,768]{0,1:T(8,128)}), f32[768,24]{0,1:T(8,128)}) %reduce-scatter.41.cloned.1.call-update) | async-done | bytes 73744 | tf_op jit(solution)/shard_map/reduce_scatter | solution.py:254
  1543.7 125.4 %reduce-scatter.49.cloned.1.call-done = f32[24,2304]{1,0:T(8,128)} async-done(((f32[768,2304]{1,0:T(8,128)}), f32[24,2304]{1,0:T(8,128)}) %reduce-scatter.49.cloned.1.call-update) | async-done | bytes 221200
  (381 shorter events, 170.5 us)
Async XLA Ops:
  7.2 66.9 %all-gather.10.cloned.1.call-start = ((), (), s32[]{:S(2)}) async-start(), calls=%async_computation.16 | async-start | bytes 3649536 | tf_op jit(solution)/shard_map/all_gather | solution.py:54
  7.9 112.8 %all-gather.12.cloned.1.call-start = ((), (), s32[]{:S(2)}) async-start(), calls=%async_computation.17 | async-start | bytes 1769472 | tf_op jit(solution)/shard_map/all_gather | solution.py:87
  55.0 169.7 %copy-start.64 = (f32[768]{0:T(1024)}, f32[768]{0:T(1024)S(1)}, u32[]{:S(2)}) copy-start(f32[768]{0:T(1024)S(1)} %get-tuple-element.111) | copy-start | bytes 9220
  55.0 347.4 %copy-start.57 = (f32[768]{0:T(1024)}, f32[768]{0:T(1024)S(1)}, u32[]{:S(2)}) copy-start(f32[768]{0:T(1024)S(1)} %get-tuple-element.109) | copy-start | bytes 9220
  77.6 88.9 %all-gather.14.cloned.1.call-start = ((), (), s32[]{:S(2)}) async-start(), calls=%async_computation.18 | async-start | bytes 1769472 | tf_op jit(solution)/shard_map/all_gather | solution.py:86
  78.4 144.0 %all-gather.16.cloned.1.call-start = ((), (), s32[]{:S(2)}) async-start(), calls=%async_computation.19 | async-start | bytes 1216512 | tf_op jit(solution)/shard_map/all_gather | solution.py:55
  79.0 190.4 %all-gather.18.cloned.1.call-start = ((), (), s32[]{:S(2)}) async-start(), calls=%async_computation.20 | async-start | bytes 1769472 | tf_op jit(solution)/shard_map/all_gather | solution.py:106
  79.7 278.3 %copy-start.51 = (f32[768]{0:T(1024)}, f32[768]{0:T(1024)S(1)}, u32[]{:S(2)}) copy-start(f32[768]{0:T(1024)S(1)} %get-tuple-element.124) | copy-start | bytes 9220
  79.7 789.7 %copy-start.49 = (f32[768]{0:T(1024)}, f32[768]{0:T(1024)S(1)}, u32[]{:S(2)}) copy-start(f32[768]{0:T(1024)S(1)} %get-tuple-element.123) | copy-start | bytes 9220
  79.9 89.2 %copy-start.16 = (bf16[2,64,768]{1,2,0:T(8,128)(2,1)}, bf16[2,64,768]{1,2,0:T(8,128)(2,1)S(1)}, u32[]{:S(2)}) copy-start(bf16[2,64,768]{1,2,0:T(8,128)(2,1)S(1)} %copy.122) | copy-start | bytes 589828
  172.7 49.7 %copy-start.28 = (bf16[2,64,768]{2,1,0:T(8,128)(2,1)S(1)}, bf16[2,64,768]{2,1,0:T(8,128)(2,1)}, u32[]{:S(2)}) copy-start(bf16[2,64,768]{2,1,0:T(8,128)(2,1)} %param.15) | copy-start | bytes 589828
  172.7 49.7 %copy-start.77 = (f32[768]{0:T(1024)S(1)}, f32[768]{0:T(1024)}, u32[]{:S(2)}) copy-start(f32[768]{0:T(1024)} %get-tuple-element.112) | copy-start | bytes 9220
  224.4 9.8 copy-start.48
  224.5 47.8 %copy-start.68 = (f32[2,64]{1,0:T(2,128)}, f32[2,64]{1,0:T(2,128)S(1)}, u32[]{:S(2)}) copy-start(f32[2,64]{1,0:T(2,128)S(1)} %broadcast_multiply_fusion.3) | copy-start | bytes 1540
  224.7 47.6 %copy-start.74 = (f32[2,64]{1,0:T(2,128)}, f32[2,64]{1,0:T(2,128)S(1)}, u32[]{:S(2)}) copy-start(f32[2,64]{1,0:T(2,128)S(1)} %fusion.73) | copy-start | bytes 1540
  226.1 131.9 %reduce-scatter.25.cloned.1.call-start = ((), (), s32[]{:S(2)}) async-start(), calls=%async_computation.21 | async-start | bytes 1769472 | tf_op jit(solution)/shard_map/reduce_scatter | solution.py:115
  279.9 122.5 %all-gather.20.cloned.1.call-start = ((), (), s32[]{:S(2)}) async-start(), calls=%async_computation.22 | async-start | bytes 1824768 | tf_op jit(solution)/shard_map/all_gather | solution.py:54
  280.6 249.4 %all-gather.22.cloned.1.call-start = ((), (), s32[]{:S(2)}) async-start(), calls=%async_computation.23 | async-start | bytes 1769472 | tf_op jit(solution)/shard_map/all_gather | solution.py:106
  359.4 44.9 %copy-start.60 = (f32[2,64]{1,0:T(2,128)}, f32[2,64]{1,0:T(2,128)S(1)}, u32[]{:S(2)}) copy-start(f32[2,64]{1,0:T(2,128)S(1)} %broadcast_multiply_fusion.2) | copy-start | bytes 1540
  485.1 47.4 %copy-start.69 = (f32[2,64]{1,0:T(2,128)}, f32[2,64]{1,0:T(2,128)S(1)}, u32[]{:S(2)}) copy-start(f32[2,64]{1,0:T(2,128)S(1)} %broadcast_multiply_fusion.1) | copy-start | bytes 1540
  485.8 46.7 %copy-start.75 = (f32[2,64]{1,0:T(2,128)}, f32[2,64]{1,0:T(2,128)S(1)}, u32[]{:S(2)}) copy-start(f32[2,64]{1,0:T(2,128)S(1)} %fusion.75) | copy-start | bytes 1540
  486.7 115.8 %reduce-scatter.27.cloned.1.call-start = ((), (), s32[]{:S(2)}) async-start(), calls=%async_computation.24 | async-start | bytes 1769472 | tf_op jit(solution)/shard_map/reduce_scatter | solution.py:115
  536.8 65.7 %copy-start.67 = (f32[768]{0:T(1024)S(1)}, f32[768]{0:T(1024)}, u32[]{:S(2)}) copy-start(f32[768]{0:T(1024)} %get-tuple-element.117) | copy-start | bytes 9220
  538.7 65.5 %copy-start.65 = (f32[768]{0:T(1024)S(1)}, f32[768]{0:T(1024)}, u32[]{:S(2)}) copy-start(f32[768]{0:T(1024)} %get-tuple-element.121) | copy-start | bytes 9220
  538.7 113.5 %all-gather.24.cloned.1.call-start = ((), (), s32[]{:S(2)}) async-start(), calls=%async_computation.25 | async-start | bytes 1769472 | tf_op jit(solution)/shard_map/all_gather | solution.py:160
  606.8 48.9 %copy-start.84 = (f32[2,64]{1,0:T(2,128)}, f32[2,64]{1,0:T(2,128)S(1)}, u32[]{:S(2)}) copy-start(f32[2,64]{1,0:T(2,128)S(1)} %negate_multiply_fusion.5) | copy-start | bytes 1540
  609.0 113.3 %reduce-scatter.29.cloned.1.call-start = ((), (), s32[]{:S(2)}) async-start(), calls=%async_computation.26 | async-start | bytes 1769472 | tf_op jit(solution)/shard_map/reduce_scatter | solution.py:172
  658.3 141.7 %reduce-scatter.31.cloned.1.call-start = ((), (), s32[]{:S(2)}) async-start(), calls=%async_computation.27 | async-start | bytes 884736 | tf_op jit(solution)/shard_map/reduce_scatter | solution.py:213
  738.5 126.4 %reduce-scatter.33.cloned.1.call-start = ((), (), s32[]{:S(2)}) async-start(), calls=%async_computation.28 | async-start | bytes 884736 | tf_op jit(solution)/shard_map/reduce_scatter | solution.py:216
  744.0 122.4 %copy-start.62 = (f32[2,64]{1,0:T(2,128)S(1)}, f32[2,64]{1,0:T(2,128)}, u32[]{:S(2)}) copy-start(f32[2,64]{1,0:T(2,128)} %copy-done.60) | copy-start | bytes 1540
  744.0 122.4 %copy-start.71 = (f32[2,64]{1,0:T(2,128)S(1)}, f32[2,64]{1,0:T(2,128)}, u32[]{:S(2)}) copy-start(f32[2,64]{1,0:T(2,128)} %fusion.74) | copy-start | bytes 1540
  744.0 171.1 %all-gather.26.cloned.1.call-start = ((), (), s32[]{:S(2)}) async-start(), calls=%async_computation.29 | async-start | bytes 1769472 | tf_op jit(solution)/shard_map/all_gather | solution.py:160
  871.8 114.8 %reduce-scatter.35.cloned.1.call-start = ((), (), s32[]{:S(2)}) async-start(), calls=%async_computation.30 | async-start | bytes 1769472 | tf_op jit(solution)/shard_map/reduce_scatter | solution.py:172
  922.8 145.2 %reduce-scatter.37.cloned.1.call-start = ((), (), s32[]{:S(2)}) async-start(), calls=%async_computation.31 | async-start | bytes 1769472 | tf_op jit(solution)/shard_map/reduce_scatter | solution.py:213
  986.7 6.5 copy-start.15
  1004.1 131.4 %reduce-scatter.39.cloned.1.call-start = ((), (), s32[]{:S(2)}) async-start(), calls=%async_computation.32 | async-start | bytes 1769472 | tf_op jit(solution)/shard_map/reduce_scatter | solution.py:216
  1009.7 147.9 %reduce-scatter.51.cloned.1.call-start = ((), (), s32[]{:S(2)}) async-start(), calls=%async_computation.38 | async-start | bytes 491520
  1012.1 168.8 %reduce-scatter.47.cloned.1.call-start = ((), (), s32[]{:S(2)}) async-start(), calls=%async_computation.36 | async-start | bytes 491520 | tf_op jit(solution)/shard_map/reduce_scatter | solution.py:259
  1015.0 190.3 %reduce-scatter.43.cloned.1.call-start = ((), (), s32[]{:S(2)}) async-start(), calls=%async_computation.34 | async-start | bytes 737280 | tf_op jit(solution)/shard_map/reduce_scatter | solution.py:259
  1018.8 211.2 %reduce-scatter.45.cloned.1.call-start = ((), (), s32[]{:S(2)}) async-start(), calls=%async_computation.35 | async-start | bytes 737280 | tf_op jit(solution)/shard_map/reduce_scatter | solution.py:262
  1020.7 311.1 %reduce-scatter.55.cloned.1.call-start = ((), (), s32[]{:S(2)}) async-start(), calls=%async_computation.40 | async-start | bytes 1216512
  1022.3 417.7 %reduce-scatter.53.cloned.1.call-start = ((), (), s32[]{:S(2)}) async-start(), calls=%async_computation.39 | async-start | bytes 3649536
  1025.2 518.5 %reduce-scatter.41.cloned.1.call-start = ((), (), s32[]{:S(2)}) async-start(), calls=%async_computation.33 | async-start | bytes 2433024 | tf_op jit(solution)/shard_map/reduce_scatter | solution.py:254
  1028.2 640.8 %reduce-scatter.49.cloned.1.call-start = ((), (), s32[]{:S(2)}) async-start(), calls=%async_computation.37 | async-start | bytes 7299072
  1030.8 105.6 %copy-start.29 = (bf16[2,64,768]{2,1,0:T(8,128)(2,1)S(1)}, bf16[2,64,768]{2,1,0:T(8,128)(2,1)}, u32[]{:S(2)}) copy-start(bf16[2,64,768]{2,1,0:T(8,128)(2,1)} %param.15) | copy-start | bytes 589828
  1148.5 40.1 %copy-start.79 = (f32[768]{0:T(1024)S(1)}, f32[768]{0:T(1024)}, u32[]{:S(2)}) copy-start(f32[768]{0:T(1024)} %get-tuple-element.66) | copy-start | bytes 9220
  1148.5 42.7 %copy-start.78 = (f32[768]{0:T(1024)S(1)}, f32[768]{0:T(1024)}, u32[]{:S(2)}) copy-start(f32[768]{0:T(1024)} %get-tuple-element.80) | copy-start | bytes 9220
  1148.5 139.2 %copy-start.2 = (bf16[768,2304]{1,0:T(8,128)(2,1)S(1)}, bf16[768,2304]{1,0:T(8,128)(2,1)}, u32[]{:S(2)}) copy-start(bf16[768,2304]{1,0:T(8,128)(2,1)} %all-gather.10.cloned.1.call-done) | copy-start | bytes 10616836
  (70 other events, 138.1 us)
Sparse Core Ops, SparseCore 0:
  11.0 63.0 all-gather.9
  77.7 42.9 all-gather.11
  123.5 42.9 all-gather.13
  169.4 52.9 all-gather.15
  226.2 43.1 all-gather.17
  280.0 64.3 reduce-scatter.24
  347.7 54.6 all-gather.19
  486.8 43.2 all-gather.21
  538.8 63.6 reduce-scatter.26
  609.1 43.1 all-gather.23
  658.5 63.7 reduce-scatter.28
  738.6 61.3 reduce-scatter.30
  803.4 61.4 reduce-scatter.32
  871.9 43.1 all-gather.25
  923.0 63.6 reduce-scatter.34
  1004.2 63.7 reduce-scatter.36
  1071.7 63.7 reduce-scatter.38
  1137.8 19.7 reduce-scatter.50
  1160.1 20.8 reduce-scatter.46
  1183.3 22.0 reduce-scatter.42
  1207.9 22.0 reduce-scatter.44
  1235.6 96.1 reduce-scatter.54
  1337.9 102.0 reduce-scatter.52
  1445.7 97.9 reduce-scatter.40
  1550.9 118.1 reduce-scatter.48
where the time goes:
time: 1690 us; the launch traced here: 1680 us
  waiting for transfers between devices  1180 us (70%)
  blocking collectives  259 us (15%)
  local copies, waits for them, and re-layouts  96.8 us (6%)
  matrix products  78.8 us (5%)
  other arithmetic  45.2 us (3%)
    unnamed x29, waiting for transfers between devices  285 us
    reduce_scatter x2, waiting for transfers between devices, backward_layer(): lax.psum_scatter(value_terms.astype(jnp.bfloat16), 'mp', scatter_dimensio...  130 us
    reduce_scatter x2, waiting for transfers between devices, backward_layer(): lax.psum_scatter(back_terms.astype(jnp.bfloat16), 'mp', scatter_dimension...  126 us
    reduce_scatter x1, waiting for transfers between devices, reduce_grads(): lax.psum_scatter(grad_attn_out, ('dp', 'mp'), scatter_dimension=1, tiled=...  104 us
    all_gather x2, waiting for transfers between devices, backward_layer(): grad_tokens = lax.all_gather(grad_down, 'mp', axis=1, tiled=True)  86.5 us
    reduce_scatter x2, waiting for transfers between devices, backward_layer(): lax.psum_scatter(key_terms.astype(jnp.bfloat16), 'mp', scatter_dimension=...  86.1 us
    unnamed x2, blocking collectives  83.8 us
    all_gather x1, blocking collectives, fetch(): lax.all_gather(attn_out, ('dp', 'mp'), axis=1, tiled=True)  75.5 us
  transfers between devices with their start and end apart: 25, of which 24 were waited for; matrix products, arithmetic and copies ran while one was open for 7% of the time, Pallas kernels for 0%

commit v1 on v0

--- a/solution.py
+++ b/solution.py
@@ -1,6 +1,11 @@
+import functools
+import types
+
 import jax
 import jax.numpy as jnp
 from jax import lax
+from jax.experimental import pallas as pl
+from jax.experimental.pallas import tpu as pltpu
 from jax.sharding import PartitionSpec as P
 
 HEAD = 64
@@ -266,7 +271,965 @@
     return (total_in, total_out, total_first, total_second, total_shifts, total_gains)
 
 
-def body(
+BF = jnp.bfloat16
+F32 = jnp.float32
+MESH = pl.DeviceIdType.MESH
+SIDE = 2
+DEPTH = 4
+PARTNERS = 9
+
+
+def mm(left, right, left_dim, right_dim):
+    return lax.dot_general(
+        left, right, (((left_dim,), (right_dim,)), ((), ())), preferred_element_type=F32
+    )
+
+
+def rowsum(values):
+    return jnp.sum(values, axis=0, keepdims=True)
+
+
+def normalize(values):
+    centered = values - jnp.mean(values, axis=-1, keepdims=True)
+    variance = jnp.mean(centered * centered, axis=-1, keepdims=True)
+    scale = lax.rsqrt(variance + EPSILON)
+    return centered * scale, scale
+
+
+def normalize_back(grad, normed, scale):
+    along = jnp.mean(grad * normed, axis=-1, keepdims=True)
+    return scale * (grad - jnp.mean(grad, axis=-1, keepdims=True) - normed * along)
+
+
+def layer_sizes(model, heads_width, hidden):
+    half = heads_width // 2
+    start = 3 * half // 128 * 128
+    return types.SimpleNamespace(
+        hc=half,
+        heads=half // HEAD,
+        wide=4 * half,
+        start=start,
+        pad=3 * half - start,
+        nr=hidden // 16,
+        nc=hidden // 2,
+        zb=model * 8 // hidden,
+    )
+
+
+def vec_rows(model, sizes):
+    rows, at = {}, 0
+    for name, length in (
+        ("qv", 4 * sizes.hc),
+        ("bo", model),
+        ("beta1", model),
+        ("b1", 2 * sizes.nc),
+        ("b2", model),
+        ("beta2", model),
+        ("g1", model),
+        ("g2", model),
+    ):
+        rows[name] = at
+        at += length // model
+    return rows, at
+
+
+def fused_kernel(dims, names, *refs):
+    r = types.SimpleNamespace(**dict(zip(names, refs)))
+    model, tok, seq, layers = dims.model, dims.tok, dims.seq, dims.layers
+    half_lanes = model // 2
+    dp, mp = lax.axis_index("dp"), lax.axis_index("mp")
+    y, c = dp // SIDE, lax.rem(dp, SIDE)
+    z, x = mp // SIDE, lax.rem(mp, SIDE)
+
+    def device(c, x, y, z):
+        return {"dp": y * SIDE + c, "mp": z * SIDE + x}
+
+    sib = device(1 - c, x, y, z)
+    xn, yn = device(c, 1 - x, y, z), device(c, x, 1 - y, z)
+    zdev = [device(c, x, y, lax.rem(z + d, DEPTH)) for d in range(1, DEPTH)]
+    zpair = z + 1 - 2 * lax.rem(z, 2)
+    zn = device(c, x, y, zpair)
+    zfar = device(c, x, y, lax.rem(z + 2, DEPTH))
+
+    bar = pltpu.get_barrier_semaphore()
+    for step in range(1, DEPTH * SIDE):
+        other = lax.rem(mp + step, DEPTH * SIDE)
+        pl.semaphore_signal(bar, inc=1, device_id={"dp": dp, "mp": other}, device_id_type=MESH)
+    pl.semaphore_signal(bar, inc=1, device_id=sib, device_id_type=MESH)
+    pl.semaphore_signal(bar, inc=1, device_id=yn, device_id_type=MESH)
+    pl.semaphore_wait(bar, PARTNERS)
+
+    sent = []
+
+    def remote(src, dst, send, recv, dev):
+        return pltpu.make_async_remote_copy(
+            src_ref=src, dst_ref=dst, send_sem=send, recv_sem=recv, device_id=dev, device_id_type=MESH
+        )
+
+    def push(src, dst, send, recv, dev):
+        copy = remote(src, dst, send, recv, dev)
+        copy.start()
+        sent.append(copy)
+
+    def arrived(dst, recv, send):
+        remote(dst, dst, send, recv, sib).wait_recv()
+
+    row_core = z // 2
+    mine = c == row_core
+    half = lax.rem(z, 2)
+
+    def spread(src, land, sends, recvs):
+        block = 2 * lax.rem(z, 2) + x
+        target = 2 * c + z // 2
+        for j in range(2):
+            local = (x == j) & (z == target)
+            copy = remote(src.at[j], land.at[block], sends.at[j], recvs.at[block], device(c, j, y, target))
+            pl.when(local)(pltpu.make_async_copy(src.at[j], land.at[block], recvs.at[block]).start)
+            pl.when(jnp.logical_not(local))(copy.start)
+
+    def spread_done(src, land, sends, recvs, on_chip_send, on_chip_recv):
+        target = 2 * c + z // 2
+        for j in range(2):
+            local = (x == j) & (z == target)
+            copy = remote(src.at[j], land.at[0], sends.at[j], recvs.at[0], sib)
+            pl.when(jnp.logical_not(local))(copy.wait_send)
+        whole = remote(land, land, on_chip_send, on_chip_recv, sib)
+
+        @pl.when(mine)
+        def _():
+            for block in range(4):
+                arrived(land.at[block], recvs.at[block], sends.at[0])
+            whole.start()
+            whole.wait_send()
+
+        @pl.when(jnp.logical_not(mine))
+        def _():
+            whole.wait_recv()
+
+    def collect(src, land, sends, recvs):
+        @pl.when(mine)
+        def _():
+            for block in range(4):
+                z_to, x_to = 2 * half + block // 2, block % 2
+                local = (x == x_to) & (z == z_to)
+                slot = land.at[x]
+                copy = remote(
+                    src.at[block], slot, sends.at[block], recvs.at[x], device(c, x_to, y, z_to)
+                )
+                pl.when(local)(pltpu.make_async_copy(src.at[block], slot, recvs.at[x]).start)
+                pl.when(jnp.logical_not(local))(copy.start)
+
+    def collect_done(src, land, sends, recvs):
+        for j in range(2):
+            arrived(land.at[j], recvs.at[j], sends.at[0])
+
+        @pl.when(mine)
+        def _():
+            for block in range(4):
+                z_to, x_to = 2 * half + block // 2, block % 2
+                local = (x == x_to) & (z == z_to)
+                copy = remote(src.at[block], src.at[block], sends.at[block], recvs.at[0], sib)
+                pl.when(jnp.logical_not(local))(copy.wait_send)
+
+    chunks = dims.chunks
+
+    def unit(i, grads, z_slice, x_at, y_at):
+        kind, layer, which, part = chunks[i]
+        if kind == "A":
+            ref = r.ga0 if layer == 0 else r.ga1
+            return ref.at[y_at, z_slice, x_at, :, pl.ds(part * model, model)]
+        ref = (r.dw0, r.dw1)[layer] if grads else (r.w0, r.w1)[layer]
+        lanes = pl.ds(pl.multiple_of(y_at * half_lanes, 128), half_lanes)
+        return ref.at[which, z_slice, x_at, pl.ds(part * dims.rows, dims.rows), lanes]
+
+    every, first, second = pl.ds(0, DEPTH), pl.ds(0, 2), pl.ds(2, 2)
+
+    def gather_z(i):
+        own = unit(i, False, pl.ds(z, 1), x, y)
+        for d in range(1, DEPTH):
+            push(own, own, r.gs.at[i, d - 1], r.gr.at[i, d - 1], zdev[d - 1])
+
+    def gather_xy(i):
+        for d in range(1, DEPTH):
+            got = unit(i, False, pl.ds(lax.rem(z + DEPTH - d, DEPTH), 1), x, y)
+            arrived(got, r.gr.at[i, d - 1], r.gs.at[i, d - 1])
+        own = unit(i, False, every, x, y)
+        push(own, own, r.gs.at[i, 3], r.gr.at[i, 3], xn)
+        push(own, own, r.gs.at[i, 4], r.gr.at[i, 4], yn)
+
+    def gather_on(i):
+        arrived(unit(i, False, every, 1 - x, y), r.gr.at[i, 3], r.gs.at[i, 3])
+        arrived(unit(i, False, every, x, 1 - y), r.gr.at[i, 4], r.gs.at[i, 4])
+        over_x = unit(i, False, first, x, 1 - y)
+        over_y = unit(i, False, second, 1 - x, y)
+        push(over_x, over_x, r.gs.at[i, 5], r.gr.at[i, 5], xn)
+        push(over_y, over_y, r.gs.at[i, 6], r.gr.at[i, 6], yn)
+
+    def gather_end(i):
+        arrived(unit(i, False, first, 1 - x, 1 - y), r.gr.at[i, 5], r.gs.at[i, 5])
+        arrived(unit(i, False, second, 1 - x, 1 - y), r.gr.at[i, 6], r.gs.at[i, 6])
+
+    def slots(i):
+        kind, layer, which, part = chunks[i]
+        at = dims.slot[i]
+        if kind == "A":
+            return r.raa.at[at], r.rba.at[at], r.rca.at[at]
+        return r.raf.at[at], r.rbf.at[at], r.rcf.at[at]
+
+    def add_into(ref, extra):
+        total = ref[...].astype(F32)
+        for more in extra:
+            total = total + more[...].astype(F32)
+        ref[...] = total.astype(BF)
+
+    def reduce_a(i):
+        ra, rb, rc = slots(i)
+        push(unit(i, True, first, 1 - x, 1 - y), ra.at[0], r.ss.at[i, 5], r.sr.at[i, 5], xn)
+        push(unit(i, True, second, 1 - x, 1 - y), ra.at[1], r.ss.at[i, 6], r.sr.at[i, 6], yn)
+
+    def reduce_b(i):
+        ra, rb, rc = slots(i)
+        arrived(ra.at[0], r.sr.at[i, 5], r.ss.at[i, 5])
+        add_into(unit(i, True, first, x, 1 - y), [ra.at[0]])
+        arrived(ra.at[1], r.sr.at[i, 6], r.ss.at[i, 6])
+        add_into(unit(i, True, second, 1 - x, y), [ra.at[1]])
+        push(unit(i, True, every, 1 - x, y), rb.at[0], r.ss.at[i, 3], r.sr.at[i, 3], xn)
+        push(unit(i, True, every, x, 1 - y), rb.at[1], r.ss.at[i, 4], r.sr.at[i, 4], yn)
+
+    def reduce_c(i):
+        ra, rb, rc = slots(i)
+        arrived(rb.at[0], r.sr.at[i, 3], r.ss.at[i, 3])
+        arrived(rb.at[1], r.sr.at[i, 4], r.ss.at[i, 4])
+        add_into(unit(i, True, every, x, y), [rb.at[0], rb.at[1]])
+        for d in range(1, DEPTH):
+            src = unit(i, True, pl.ds(lax.rem(z + d, DEPTH), 1), x, y)
+            push(src, rc.at[pl.ds(d - 1, 1)], r.ss.at[i, d - 1], r.sr.at[i, d - 1], zdev[d - 1])
+
+    def reduce_end(i):
+        kind, layer, which, part = chunks[i]
+        at = dims.slot[i]
+        ra, rb, rc = slots(i)
+        total = unit(i, True, pl.ds(z, 1), x, y)[...].astype(F32)[0]
+        for d in range(1, DEPTH):
+            arrived(rc.at[pl.ds(d - 1, 1)], r.sr.at[i, d - 1], r.ss.at[i, d - 1])
+            total = total + rc[d - 1].astype(F32)
+        if kind == "A":
+            out = (r.da0, r.da1)[layer]
+            rows = total.shape[0] // 2
+            out[c, :, part * model : (part + 1) * model] = jnp.where(c == 0, total[:rows], total[rows:])
+            r.fsa[at] = jnp.where(c == 0, total[rows:], total[:rows])
+            push(r.fsa.at[at], r.fra.at[at], r.fs.at[i], r.fr.at[i], sib)
+        else:
+            out = (r.df0, r.df1)[layer]
+            rows = pl.ds(part * dims.rows, dims.rows)
+            out[c, which, rows, :] = total
+            push(out.at[c, which, rows, :], r.frf.at[at], r.fs.at[i], r.fr.at[i], sib)
+
+    def reduce_out(i):
+        kind, layer, which, part = chunks[i]
+        at = dims.slot[i]
+        if kind == "A":
+            arrived(r.fra.at[at], r.fr.at[i], r.fs.at[i])
+            (r.da0, r.da1)[layer][1 - c, :, part * model : (part + 1) * model] = r.fra[at]
+        else:
+            arrived(r.frf.at[at], r.fr.at[i], r.fs.at[i])
+            rows = pl.ds(part * dims.rows, dims.rows)
+            (r.df0, r.df1)[layer][1 - c, which, rows, :] = r.frf[at]
+
+    def total_step(work, land, step, sends, recvs):
+        dev = (sib, xn, yn, zn, zfar)[step]
+        push(work.at[step], land.at[step], sends.at[step], recvs.at[step], dev)
+
+    def total_add(work, land, step, sends, recvs):
+        arrived(land.at[step], recvs.at[step], sends.at[step])
+        work[step + 1] = work[step] + land[step]
+
+    exchanges = []
+
+    def exchange(part):
+        slot = len(exchanges) % 2
+        r.xs[slot] = part.astype(BF)
+        copy = remote(r.xs.at[slot], r.xr.at[slot], r.es.at[slot], r.er.at[slot], sib)
+        copy.start()
+        exchanges.append(copy)
+
+        def finish():
+            copy.wait()
+            return r.xs[slot].astype(F32) + r.xr[slot].astype(F32)
+
+        return finish
+
+    def vec_row(row):
+        return r.vw[5, row : row + 1, :]
+
+    def layer_vecs(at):
+        sizes, rows, base = layers[at], dims.rows_of[at], dims.base[at]
+        if sizes.hc * 2 == model:
+            qv = r.vw[5, pl.ds(base + rows["qv"] + c, 1), :]
+        else:
+            both = vec_row(base + rows["qv"])
+            qv = jnp.where(c == 0, both[:, : 2 * sizes.hc], both[:, 2 * sizes.hc :])
+        span = sizes.nc // model
+        b1 = [r.vw[5, pl.ds(base + rows["b1"] + c * span + s, 1), :] for s in range(span)]
+        found = types.SimpleNamespace(bq=qv[:, : sizes.hc], bv=qv[:, sizes.hc :], b1=b1)
+        for name in ("bo", "beta1", "b2", "beta2", "g1", "g2"):
+            setattr(found, name, vec_row(base + rows[name]))
+        return found
+
+    kept = [
+        types.SimpleNamespace(
+            **{
+                name: getattr(r, f"{name}{at}")
+                for name in ("xb", "q", "kv", "a", "ctx", "n1", "s1", "hb", "g", "gp", "n2", "s2")
+            }
+        )
+        for at in range(2)
+    ]
+    wa = (r.wa0, r.wa1)
+    weights = (r.w0, r.w1)
+
+    def order_rows(at, part):
+        gathered, whole = (r.ga0, r.ga1)[at], wa[at]
+        cols = slice(part * model, (part + 1) * model)
+        rows = gathered.shape[3] // 2
+        span = DEPTH * 2 * rows
+        for y_at in range(SIDE):
+            for z_at in range(DEPTH):
+                left = gathered[y_at, z_at, 0, :, cols].astype(F32)
+                right = gathered[y_at, z_at, 1, :, cols].astype(F32)
+                for core in range(SIDE):
+                    own = slice(core * rows, (core + 1) * rows)
+                    both = jnp.concatenate([left[own], right[own]], axis=0).astype(BF)
+                    begin = (y_at * SIDE + core) * span + z_at * 2 * rows
+                    whole[begin : begin + 2 * rows, cols] = both
+
+    def store_grad_rows(at, y_at, value, cols):
+        blocks = (r.ga0, r.ga1)[at]
+        rows = blocks.shape[3] // 2
+        span = DEPTH * 2 * rows
+        for z_at in range(DEPTH):
+            for x_at in range(SIDE):
+                begin = (z_at * 2 + x_at) * rows
+                both = [value[begin : begin + rows], value[span + begin : span + begin + rows]]
+                blocks[y_at, z_at, x_at, :, cols] = jnp.concatenate(both, axis=0).astype(BF)
+
+    def send_kv(at):
+        kv = kept[at].kv
+        push(kv.at[half], kv.at[half], r.ks.at[at], r.kr.at[at], zn)
+
+    def wait_kv(at):
+        kv = kept[at].kv
+        arrived(kv.at[1 - half], r.kr.at[at], r.ks.at[at])
+
+    def head_kv(at, h):
+        sizes, kv = layers[at], kept[at].kv
+        k = kv[:, :, h * HEAD : (h + 1) * HEAD].reshape(seq, HEAD)
+        v = kv[:, :, sizes.hc + h * HEAD : sizes.hc + (h + 1) * HEAD].reshape(seq, HEAD)
+        return k, v
+
+    def attention(at):
+        sizes, keep = layers[at], kept[at]
+        lane = lax.broadcasted_iota(jnp.int32, (1, model), 1)
+        row = (y * SIDE + row_core) * 2 + x
+        length = jnp.sum(jnp.where(lane == row, vec_row(dims.length_row), 0.0), axis=1, keepdims=True)
+        valid = lax.broadcasted_iota(jnp.int32, (1, seq), 1).astype(F32) < length
+        for h in range(sizes.heads):
+            q = keep.q[:, h * HEAD : (h + 1) * HEAD]
+            k, v = head_kv(at, h)
+            scores = jnp.where(valid, mm(q, k, 1, 1) * 0.125, NEGATIVE)
+            exponent = jnp.exp(scores - jnp.max(scores, axis=1, keepdims=True))
+            low = (exponent / jnp.sum(exponent, axis=1, keepdims=True)).astype(BF)
+            keep.a[h] = low
+            begin = sizes.pad + h * HEAD
+            keep.ctx[:, begin : begin + HEAD] = mm(low, v, 1, 0).astype(BF)
+
+    def attention_back(at, grad_ctx):
+        sizes, keep = layers[at], kept[at]
+        dkv, gp = (r.dkv0, r.dkv1)[at], (r.dp0, r.dp1)[at]
+        for h in range(sizes.heads):
+            q = keep.q[:, h * HEAD : (h + 1) * HEAD]
+            k, v = head_kv(at, h)
+            begin = sizes.pad + h * HEAD
+            dc = grad_ctx[:, begin : begin + HEAD]
+            low = keep.a[h]
+            a = low.astype(F32)
+            da = mm(dc, v, 1, 1)
+            inner = jnp.sum(a * da, axis=1, keepdims=True)
+            ds = (0.125 * a * (da - inner)).astype(BF)
+            gp[:, h * HEAD : (h + 1) * HEAD] = mm(ds, k, 1, 0).astype(BF)
+            dk = mm(ds, q, 0, 0).astype(BF).reshape(2, tok, HEAD)
+            dv = mm(low, dc, 0, 0).astype(BF).reshape(2, tok, HEAD)
+            dkv[:, :, h * HEAD : (h + 1) * HEAD] = dk
+            dkv[:, :, sizes.hc + h * HEAD : sizes.hc + (h + 1) * HEAD] = dv
+
+    def block(at, which, b):
+        sizes = layers[at]
+        w = weights[at][which, b * sizes.zb : (b + 1) * sizes.zb]
+        return w.reshape(model, model)
+
+    def up(at, vecs):
+        sizes, keep = layers[at], kept[at]
+        for b in range(sizes.nc // model):
+            cols = slice(b * model, (b + 1) * model)
+            u = mm(keep.hb[...], block(at, 0, b), 1, 1) + vecs.b1[b]
+            phi = 0.5 * (1.0 + lax.erf(u * 0.7071067811865476))
+            keep.g[:, cols] = (u * phi).astype(BF)
+            density = jnp.exp(u * u * -0.5) * 0.3989422804014327
+            keep.gp[:, cols] = (phi + u * density).astype(BF)
+
+    def down(at):
+        sizes, keep = layers[at], kept[at]
+        total = None
+        for b in range(sizes.nc // model):
+            term = mm(keep.g[:, b * model : (b + 1) * model], block(at, 1, b), 1, 0)
+            total = term if total is None else total + term
+        return total
+
+    def weight_grad(at, which, left, right):
+        sizes = layers[at]
+        dw = (r.dw0, r.dw1)[at]
+        span = model // 2
+        zb = sizes.zb // 2
+        for b in range(sizes.nc // span):
+            value = mm(left[:, b * span : (b + 1) * span], right[...], 0, 0).astype(BF)
+            dw[which, b * zb : (b + 1) * zb] = value.reshape(zb, 2, sizes.nr, model)
+
+    spread(r.hid, r.xin, r.hs, r.hr)
+    push(r.vec, r.vl.at[0], r.vs.at[0], r.vr.at[0], sib)
+    push(r.pa0.at[1 - c], r.ar0, r.is_.at[0], r.ir.at[0], sib)
+    push(r.pf0.at[1 - c], r.fr0, r.is_.at[1], r.ir.at[1], sib)
+    push(r.pa1.at[1 - c], r.ar1, r.is_.at[2], r.ir.at[2], sib)
+    push(r.pf1.at[1 - c], r.fr1, r.is_.at[3], r.ir.at[3], sib)
+
+    def prepare_a(at):
+        own_ref, land, blocks = (r.pa0, r.pa1)[at], (r.ar0, r.ar1)[at], (r.ga0, r.ga1)[at]
+        arrived(land, r.ir.at[2 * at], r.is_.at[2 * at])
+        own, other = own_ref[c], land[...]
+        both = [jnp.where(c == 0, own, other), jnp.where(c == 0, other, own)]
+        blocks[y, z, x] = jnp.concatenate(both, axis=0).astype(BF)
+
+    def prepare_f(at):
+        own_ref, land = (r.pf0, r.pf1)[at], (r.fr0, r.fr1)[at]
+        arrived(land, r.ir.at[2 * at + 1], r.is_.at[2 * at + 1])
+        lanes = pl.ds(pl.multiple_of(y * half_lanes, 128), half_lanes)
+        weights[at][:, z, x, :, lanes] = own_ref[c] + land[...]
+
+    prepare_a(0)
+    gather_z(0)
+    gather_z(1)
+    prepare_f(0)
+    gather_z(2)
+    arrived(r.vl.at[0], r.vr.at[0], r.vs.at[0])
+    r.vw[1] = r.vec[...] + r.vl[0]
+    total_step(r.vw, r.vl, 1, r.vs, r.vr)
+    spread_done(r.hid, r.xin, r.hs, r.hr, r.os.at[0], r.os.at[1])
+    gather_xy(0)
+    gather_z(3)
+    total_add(r.vw, r.vl, 1, r.vs, r.vr)
+    total_step(r.vw, r.vl, 2, r.vs, r.vr)
+    prepare_a(1)
+    prepare_f(1)
+    gather_xy(1)
+    gather_on(0)
+    gather_z(4)
+    total_add(r.vw, r.vl, 2, r.vs, r.vr)
+    total_step(r.vw, r.vl, 3, r.vs, r.vr)
+    gather_xy(2)
+    gather_on(1)
+    gather_z(5)
+    total_add(r.vw, r.vl, 3, r.vs, r.vr)
+    total_step(r.vw, r.vl, 4, r.vs, r.vr)
+    gather_end(0)
+    total_add(r.vw, r.vl, 4, r.vs, r.vr)
+    vecs = [layer_vecs(0), layer_vecs(1)]
+
+    def project(at, hidden_low, parts):
+        sizes, keep = layers[at], kept[at]
+        for part in parts:
+            order_rows(at, part)
+        if sizes.wide == model:
+            p = mm(hidden_low, wa[at][...], 1, 0)
+            keep.q[...] = (p[:, : sizes.hc] + vecs[at].bq).astype(BF)
+            keep.kv[half, :, : sizes.hc] = p[:, sizes.hc : 2 * sizes.hc].astype(BF)
+            keep.kv[half, :, sizes.hc :] = (p[:, 2 * sizes.hc : 3 * sizes.hc] + vecs[at].bv).astype(BF)
+        elif parts == (0,):
+            p = mm(hidden_low, wa[at][:, : 2 * sizes.hc], 1, 0)
+            keep.q[...] = (p[:, : sizes.hc] + vecs[at].bq).astype(BF)
+            keep.kv[half, :, : sizes.hc] = p[:, sizes.hc :].astype(BF)
+        else:
+            p = mm(hidden_low, wa[at][:, 2 * sizes.hc : 3 * sizes.hc], 1, 0)
+            keep.kv[half, :, sizes.hc :] = (p + vecs[at].bv).astype(BF)
+
+    def attend_out(at):
+        return mm(kept[at].ctx[...], wa[at][:, layers[at].start :], 1, 1)
+
+    def norm_one(at, base, branch):
+        keep, v = kept[at], vecs[at]
+        normed, scale = normalize(base + branch + v.bo)
+        keep.n1[...] = normed
+        keep.s1[...] = scale
+        result = normed * v.g1 + v.beta1
+        keep.hb[...] = result.astype(BF)
+        return result
+
+    def norm_two(at, base, branch):
+        keep, v = kept[at], vecs[at]
+        normed, scale = normalize(base + branch + v.b2)
+        keep.n2[...] = normed
+        keep.s2[...] = scale
+        return normed * v.g2 + v.beta2
+
+    if layers[1].pad:
+        kept[1].ctx[...] = jnp.zeros_like(kept[1].ctx)
+        r.dp1[...] = jnp.zeros_like(r.dp1)
+    kept[0].xb[...] = r.xin[...].reshape(tok, model)
+    project(0, kept[0].xb[...], (0,))
+    gather_xy(3)
+    gather_on(2)
+    gather_z(6)
+    gather_end(1)
+    project(0, kept[0].xb[...], (1,))
+    send_kv(0)
+    spread(r.cot, r.cin, r.cs, r.cr)
+    gather_xy(4)
+    gather_on(3)
+    gather_z(7)
+    gather_end(2)
+    wait_kv(0)
+    attention(0)
+    wait_branch = exchange(attend_out(0))
+    gather_xy(5)
+    gather_on(4)
+    gather_z(8)
+    gather_end(3)
+    normed = norm_one(0, kept[0].xb[...].astype(F32), wait_branch())
+    up(0, vecs[0])
+    gather_xy(6)
+    gather_on(5)
+    gather_end(4)
+    spread_done(r.cot, r.cin, r.cs, r.cr, r.os.at[2], r.os.at[3])
+    gather_xy(7)
+    gather_on(6)
+    gather_end(5)
+    wait_branch = exchange(down(0))
+    gather_xy(8)
+    gather_on(7)
+    gather_end(6)
+    middle = norm_two(0, normed, wait_branch())
+    kept[1].xb[...] = middle.astype(BF)
+    project(1, kept[1].xb[...], (0,))
+    send_kv(1)
+    wait_kv(1)
+    attention(1)
+    wait_branch = exchange(attend_out(1))
+    gather_on(8)
+    gather_end(7)
+    normed = norm_one(1, middle, wait_branch())
+    up(1, vecs[1])
+    gather_end(8)
+    wait_branch = exchange(down(1))
+    final = norm_two(1, normed, wait_branch())
+    r.oblk[...] = final.astype(BF).reshape(r.oblk.shape)
+    collect(r.oblk, r.oland, r.ys, r.yr)
+    for copy in sent:
+        copy.wait_send()
+    sent.clear()
+
+    r.vw[0] = jnp.zeros_like(r.vw[0])
+    once = jnp.where(c == 0, 1.0, 0.0)
+
+    def put_vec(at, name, value):
+        row = dims.base[at] + dims.rows_of[at][name]
+        r.vw[0, row : row + 1, :] = value * once
+
+    def back_two(at, grad):
+        keep, v = kept[at], vecs[at]
+        n2 = keep.n2[...]
+        put_vec(at, "g2", rowsum(grad * n2))
+        put_vec(at, "beta2", rowsum(grad))
+        dz2 = normalize_back(grad * v.g2, n2, keep.s2[...])
+        r.eo[...] = dz2.astype(BF)
+        put_vec(at, "b2", rowsum(r.eo[...].astype(F32)))
+        return dz2
+
+    def back_up(at):
+        sizes, keep = layers[at], kept[at]
+        base = dims.base[at] + dims.rows_of[at]["b1"]
+        span = sizes.nc // model
+        for b in range(span):
+            cols = slice(b * model, (b + 1) * model)
+            dg = mm(r.eo[...], block(at, 1, b), 1, 1)
+            du = (dg * keep.gp[:, cols].astype(F32)).astype(BF)
+            keep.g[:, cols] = du
+            r.vw[0, pl.ds(base + c * span + b, 1), :] = rowsum(du.astype(F32))
+
+    def back_in(at):
+        sizes, keep = layers[at], kept[at]
+        total = None
+        for b in range(sizes.nc // model):
+            term = mm(keep.g[:, b * model : (b + 1) * model], block(at, 0, b), 1, 0)
+            total = term if total is None else total + term
+        return total
+
+    def back_one(at, grad):
+        keep, v = kept[at], vecs[at]
+        n1 = keep.n1[...]
+        put_vec(at, "g1", rowsum(grad * n1))
+        put_vec(at, "beta1", rowsum(grad))
+        dz1 = normalize_back(grad * v.g1, n1, keep.s1[...])
+        r.eo[...] = dz1.astype(BF)
+        put_vec(at, "bo", rowsum(r.eo[...].astype(F32)))
+        grad_ctx = mm(r.eo[...], wa[at][:, layers[at].start :], 1, 0).astype(BF)
+        return dz1, grad_ctx
+
+    def send_dkv(at):
+        dkv, land = (r.dkv0, r.dkv1)[at], (r.dkr0, r.dkr1)[at]
+        push(dkv.at[1 - half], land, r.ks.at[2 + at], r.kr.at[2 + at], zn)
+
+    def take_dkv(at):
+        sizes = layers[at]
+        dkv, land, gp = (r.dkv0, r.dkv1)[at], (r.dkr0, r.dkr1)[at], (r.dp0, r.dp1)[at]
+        arrived(land, r.kr.at[2 + at], r.ks.at[2 + at])
+        total = (dkv[half].astype(F32) + land[...].astype(F32)).astype(BF)
+        gp[:, sizes.hc : 3 * sizes.hc] = total
+        qsum = rowsum(gp[:, : sizes.hc].astype(F32))
+        vsum = rowsum(total[:, sizes.hc :].astype(F32))
+        both = jnp.concatenate([qsum, vsum], axis=1)
+        row = dims.base[at] + dims.rows_of[at]["qv"]
+        if 2 * sizes.hc == model:
+            r.vw[0, pl.ds(row + c, 1), :] = both
+        else:
+            blank = jnp.zeros_like(both)
+            left, right = jnp.where(c == 0, both, blank), jnp.where(c == 0, blank, both)
+            r.vw[0, row : row + 1, :] = jnp.concatenate([left, right], axis=1)
+
+    def projection_grad(at, part):
+        sizes, keep, gp = layers[at], kept[at], (r.dp0, r.dp1)[at]
+        begin, end = part * model, (part + 1) * model
+        for y_at in range(SIDE):
+            rows = slice(y_at * half_lanes, (y_at + 1) * half_lanes)
+            pieces = []
+            xb = keep.xb[:, rows]
+            split = min(end, sizes.start)
+            if begin < split:
+                pieces.append(mm(xb, gp[:, begin:split], 0, 0))
+            if end > sizes.start:
+                value = mm(r.eo[:, rows], keep.ctx[...], 0, 0)
+                if sizes.pad:
+                    value = value + mm(xb, gp[:, sizes.start : end], 0, 0)
+                pieces.append(value)
+            value = pieces[0] if len(pieces) == 1 else jnp.concatenate(pieces, axis=1)
+            store_grad_rows(at, y_at, value, slice(begin, end))
+
+    def back_hidden(at):
+        gp = (r.dp0, r.dp1)[at]
+        width = gp.shape[1]
+        return mm(gp[...], wa[at][:, :width], 1, 1)
+
+    grad = r.cin[...].reshape(tok, model).astype(F32)
+    dz2 = back_two(1, grad)
+    weight_grad(1, 1, kept[1].g, r.eo)
+    reduce_a(8)
+    back_up(1)
+    weight_grad(1, 0, kept[1].g, kept[1].hb)
+    reduce_a(7)
+    wait_branch = exchange(back_in(1))
+    reduce_b(8)
+    dz1, grad_ctx = back_one(1, dz2 + wait_branch())
+    reduce_b(7)
+    reduce_c(8)
+    attention_back(1, grad_ctx)
+    send_dkv(1)
+    reduce_c(7)
+    reduce_end(8)
+    take_dkv(1)
+    projection_grad(1, 0)
+    reduce_a(6)
+    wait_branch = exchange(back_hidden(1))
+    reduce_end(7)
+    reduce_b(6)
+    grad = dz1 + wait_branch()
+    dz2 = back_two(0, grad)
+    weight_grad(0, 1, kept[0].g, r.eo)
+    reduce_a(4)
+    reduce_a(5)
+    reduce_c(6)
+    back_up(0)
+    weight_grad(0, 0, kept[0].g, kept[0].hb)
+    reduce_a(2)
+    reduce_a(3)
+    wait_branch = exchange(back_in(0))
+    reduce_b(4)
+    reduce_b(5)
+    reduce_end(6)
+    dz1, grad_ctx = back_one(0, dz2 + wait_branch())
+    reduce_b(2)
+    reduce_b(3)
+    reduce_c(4)
+    attention_back(0, grad_ctx)
+    send_dkv(0)
+    reduce_c(5)
+    take_dkv(0)
+    projection_grad(0, 0)
+    reduce_a(0)
+    projection_grad(0, 1)
+    reduce_a(1)
+    total_step(r.vw, r.vl, 0, r.ws, r.wr)
+    wait_branch = exchange(back_hidden(0))
+    reduce_c(2)
+    reduce_end(4)
+    grad = dz1 + wait_branch()
+    r.gblk[...] = grad.astype(BF).reshape(r.gblk.shape)
+    collect(r.gblk, r.gland, r.zs, r.zr)
+    reduce_b(0)
+    reduce_b(1)
+    reduce_c(3)
+    reduce_end(5)
+    total_add(r.vw, r.vl, 0, r.ws, r.wr)
+    total_step(r.vw, r.vl, 1, r.ws, r.wr)
+    reduce_end(2)
+    reduce_end(3)
+    total_add(r.vw, r.vl, 1, r.ws, r.wr)
+    total_step(r.vw, r.vl, 2, r.ws, r.wr)
+    reduce_c(0)
+    total_add(r.vw, r.vl, 2, r.ws, r.wr)
+    total_step(r.vw, r.vl, 3, r.ws, r.wr)
+    reduce_c(1)
+    total_add(r.vw, r.vl, 3, r.ws, r.wr)
+    total_step(r.vw, r.vl, 4, r.ws, r.wr)
+    for i in (8, 7, 6, 4, 5, 2, 3):
+        reduce_out(i)
+    total_add(r.vw, r.vl, 4, r.ws, r.wr)
+    r.dvec[...] = r.vw[5]
+    collect_done(r.oblk, r.oland, r.ys, r.yr)
+    r.out[...] = r.oland[...]
+    reduce_end(0)
+    reduce_end(1)
+    collect_done(r.gblk, r.gland, r.zs, r.zr)
+    r.gh[...] = r.gland[...].astype(F32)
+    reduce_out(0)
+    reduce_out(1)
+    for copy in sent:
+        copy.wait_send()
+
+
+def fused_call(hid, cot, vec, shards, dims):
+    model, tok, seq = dims.model, dims.tok, dims.seq
+    block = (4, tok // 4, model)
+    vmem = pltpu.VMEM
+    dma = pltpu.SemaphoreType.DMA
+    names = ["hid", "cot", "vec", "pa0", "pf0", "pa1", "pf1"]
+    inputs = [hid, cot, vec] + list(shards)
+    outs = {
+        "out": jax.ShapeDtypeStruct(hid.shape, BF),
+        "gh": jax.ShapeDtypeStruct(hid.shape, F32),
+        "da0": jax.ShapeDtypeStruct(shards[0].shape, F32),
+        "df0": jax.ShapeDtypeStruct(shards[1].shape, F32),
+        "da1": jax.ShapeDtypeStruct(shards[2].shape, F32),
+        "df1": jax.ShapeDtypeStruct(shards[3].shape, F32),
+        "dvec": jax.ShapeDtypeStruct(vec.shape, F32),
+    }
+    rows_a = 2 * shards[0].shape[1]
+    count_a = sum(chunk[0] == "A" for chunk in dims.chunks)
+    count_f = len(dims.chunks) - count_a
+    shape_a, shape_f = (rows_a, model), (dims.rows, model // 2)
+    n = len(dims.chunks)
+    scratch = {
+        "xin": vmem(block, BF),
+        "cin": vmem(block, BF),
+        "oblk": vmem(block, BF),
+        "gblk": vmem(block, BF),
+        "oland": vmem(hid.shape, BF),
+        "gland": vmem(hid.shape, BF),
+        "vw": vmem((6,) + vec.shape, F32),
+        "vl": vmem((5,) + vec.shape, F32),
+        "xs": vmem((2, tok, model), BF),
+        "xr": vmem((2, tok, model), BF),
+        "eo": vmem((tok, model), BF),
+        "raa": vmem((count_a, 2, 2) + shape_a, BF),
+        "rba": vmem((count_a, 2, 4) + shape_a, BF),
+        "rca": vmem((count_a, 3) + shape_a, BF),
+        "raf": vmem((count_f, 2, 2) + shape_f, BF),
+        "rbf": vmem((count_f, 2, 4) + shape_f, BF),
+        "rcf": vmem((count_f, 3) + shape_f, BF),
+        "fsa": vmem((count_a, rows_a // 2, model), F32),
+        "fra": vmem((count_a, rows_a // 2, model), F32),
+        "frf": vmem((count_f,) + shape_f, F32),
+    }
+    for at, sizes in enumerate(dims.layers):
+        scratch |= {
+            f"ar{at}": vmem((rows_a // 2, sizes.wide), F32),
+            f"fr{at}": vmem((2, sizes.nr, model // 2), BF),
+            f"ga{at}": vmem((SIDE, DEPTH, SIDE, rows_a, sizes.wide), BF),
+            f"wa{at}": vmem((model, sizes.wide), BF),
+            f"w{at}": vmem((2, DEPTH, SIDE, sizes.nr, model), BF),
+            f"dw{at}": vmem((2, DEPTH, SIDE, sizes.nr, model), BF),
+            f"xb{at}": vmem((tok, model), BF),
+            f"q{at}": vmem((tok, sizes.hc), BF),
+            f"kv{at}": vmem((2, tok, 2 * sizes.hc), BF),
+            f"a{at}": vmem((sizes.heads, tok, seq), BF),
+            f"ctx{at}": vmem((tok, sizes.wide - sizes.start), BF),
+            f"n1{at}": vmem((tok, model), F32),
+            f"s1{at}": vmem((tok, 1), F32),
+            f"hb{at}": vmem((tok, model), BF),
+            f"g{at}": vmem((tok, sizes.nc), BF),
+            f"gp{at}": vmem((tok, sizes.nc), BF),
+            f"n2{at}": vmem((tok, model), F32),
+            f"s2{at}": vmem((tok, 1), F32),
+            f"dkv{at}": vmem((2, tok, 2 * sizes.hc), BF),
+            f"dkr{at}": vmem((tok, 2 * sizes.hc), BF),
+            f"dp{at}": vmem((tok, sizes.wide if sizes.pad else sizes.start), BF),
+        }
+    scratch |= {name: dma((n, 7)) for name in ("gs", "gr", "ss", "sr")}
+    scratch |= {name: dma((n,)) for name in ("fs", "fr")}
+    scratch |= {name: dma((5,)) for name in ("vs", "vr", "ws", "wr")}
+    scratch |= {name: dma((4,)) for name in ("hs", "hr", "cs", "cr", "ys", "yr", "zs", "zr")}
+    scratch |= {name: dma((4,)) for name in ("is_", "ir", "os", "ks", "kr")}
+    scratch |= {name: dma((2,)) for name in ("es", "er")}
+    names = names + list(outs) + list(scratch)
+    whole = pl.BlockSpec(memory_space=pltpu.VMEM)
+    return pl.pallas_call(
+        functools.partial(fused_kernel, dims, names),
+        out_shape=list(outs.values()),
+        in_specs=[whole] * len(inputs),
+        out_specs=[whole] * len(outs),
+        scratch_shapes=list(scratch.values()),
+        compiler_params=pltpu.CompilerParams(
+            collective_id=0, has_side_effects=True, vmem_limit_bytes=dims.vmem
+        ),
+        name="layers",
+    )(*inputs)
+
+
+def pack_layer(attn_in, attn_out, ffn_in, ffn_out, core):
+    rows, heads_width = attn_in.shape[0], attn_in.shape[1] // 3
+    first = attn_in.reshape(rows, 3, 2, heads_width // 2).transpose(2, 0, 1, 3)
+    first = first.reshape(2, rows, 3 * heads_width // 2)
+    second = attn_out.T.reshape(rows, 2, heads_width // 2).transpose(1, 0, 2)
+    attn = jnp.concatenate([first, second], axis=2).astype(F32)
+    both = jnp.stack([ffn_in.T, ffn_out])
+    both = both.reshape(2, 2, both.shape[1] // 2, both.shape[2]).transpose(1, 0, 2, 3)
+    blank = jnp.zeros_like(both)
+    left, right = jnp.where(core == 0, both, blank), jnp.where(core == 0, blank, both)
+    return attn, jnp.concatenate([left, right], axis=3)
+
+
+def unpack_layer(attn, ffn, core):
+    rows, half = attn.shape[1], attn.shape[2] // 4
+    grad_in = attn[:, :, : 3 * half].reshape(2, rows, 3, half).transpose(1, 2, 0, 3)
+    grad_out = attn[:, :, 3 * half :].transpose(0, 2, 1).reshape(2 * half, rows)
+    lanes = ffn.shape[3] // 2
+    own = jnp.where(core == 0, ffn[..., :lanes], ffn[..., lanes:])
+    own = own.transpose(1, 0, 2, 3).reshape(2, 2 * ffn.shape[2], lanes)
+    return grad_in.reshape(rows, 6 * half), grad_out, own[0].T, own[1]
+
+
+def pack_vectors(shifts, gains, sizes, model, device):
+    total = 4 * sizes.hc + 4 * model + 2 * sizes.nc
+    flat = jnp.zeros((total,), F32)
+    flat = lax.dynamic_update_slice_in_dim(flat, shifts.astype(F32), device * shifts.shape[0], 0)
+    query, value, rest = flat[: 2 * sizes.hc], flat[2 * sizes.hc : 4 * sizes.hc], flat[4 * sizes.hc :]
+    both = jnp.concatenate([query.reshape(2, sizes.hc), value.reshape(2, sizes.hc)], axis=1)
+    up = rest[2 * model : 2 * model + 2 * sizes.nc].reshape(8, 2, sizes.nr).transpose(1, 0, 2)
+    scale = jnp.zeros((2 * model,), F32)
+    scale = lax.dynamic_update_slice_in_dim(scale, gains.astype(F32), device * gains.shape[0], 0)
+    return [both.reshape(-1), rest[: 2 * model], up.reshape(-1), rest[2 * model + 2 * sizes.nc :], scale]
+
+
+def unpack_vectors(flat, sizes, model, device, shift_len, gain_len):
+    both = flat[: 4 * sizes.hc].reshape(2, 2, sizes.hc).transpose(1, 0, 2).reshape(-1)
+    rest = flat[4 * sizes.hc :]
+    up = rest[2 * model : 2 * model + 2 * sizes.nc].reshape(2, 8, sizes.nr).transpose(1, 0, 2)
+    after = rest[2 * model + 2 * sizes.nc :]
+    shifts = jnp.concatenate([both, rest[: 2 * model], up.reshape(-1), after[: 2 * model]])
+    gains = after[2 * model :]
+    return (
+        lax.dynamic_slice_in_dim(shifts, device * shift_len, shift_len),
+        lax.dynamic_slice_in_dim(gains, device * gain_len, gain_len),
+    )
+
+
+def make_dims(hidden_in, teacher, student):
+    model = hidden_in.shape[2]
+    layers = [
+        layer_sizes(model, p[0].shape[1] // 3, p[2].shape[1] * DEPTH * SIDE) for p in (teacher, student)
+    ]
+    rows = layers[1].nr
+    chunks = []
+    for at, sizes in enumerate(layers):
+        chunks += [("A", at, 0, part) for part in range(sizes.wide // model)]
+        for which in (0, 1):
+            chunks += [("F", at, which, part) for part in range(sizes.nr // rows)]
+    counts, slot = {"A": 0, "F": 0}, []
+    for chunk in chunks:
+        slot.append(counts[chunk[0]])
+        counts[chunk[0]] += 1
+    rows_of, base, at = [], [], 0
+    for sizes in layers:
+        found, count = vec_rows(model, sizes)
+        rows_of.append(found)
+        base.append(at)
+        at += count
+    return types.SimpleNamespace(
+        model=model,
+        tok=4 * hidden_in.shape[1],
+        seq=8 * hidden_in.shape[1],
+        layers=layers,
+        chunks=chunks,
+        slot=slot,
+        rows=rows,
+        rows_of=rows_of,
+        base=base,
+        length_row=at,
+        vec_rows=(at + 8) // 8 * 8,
+        vmem=63 * 2**20,
+    )
+
+
+def fast_body(
+    hidden_in,
+    cotangent,
+    lengths,
+    *params,
+):
+    teacher, student = params[:6], params[6:]
+    dims = make_dims(hidden_in, teacher, student)
+    model = dims.model
+    dp, mp = lax.axis_index("dp"), lax.axis_index("mp")
+    core = lax.rem(dp, SIDE)
+    device = dp * DEPTH * SIDE + mp
+    pieces = []
+    shards = []
+    for sizes, p in zip(dims.layers, (teacher, student)):
+        shards += list(pack_layer(*p[:4], core))
+        pieces += pack_vectors(p[4], p[5], sizes, model, device)
+    spans = jnp.zeros((dims.vec_rows * model - sum(p.shape[0] for p in pieces),), F32)
+    own = jnp.where(mp == 0, lengths.astype(F32), jnp.zeros_like(lengths, F32))
+    spans = lax.dynamic_update_slice_in_dim(spans, own, dp * lengths.shape[0], 0)
+    vec = jnp.concatenate(pieces + [spans]).reshape(dims.vec_rows, model)
+    out, grad_hidden, da0, df0, da1, df1, dvec = fused_call(hidden_in, cotangent, vec, shards, dims)
+    results = [out, grad_hidden]
+    flat = dvec.reshape(-1)
+    for at, (sizes, p, attn, ffn) in enumerate(
+        zip(dims.layers, (teacher, student), (da0, da1), (df0, df1))
+    ):
+        results += list(unpack_layer(attn, ffn, core))
+        begin = dims.base[at] * model
+        results += list(
+            unpack_vectors(flat[begin:], sizes, model, device, p[4].shape[0], p[5].shape[0])
+        )
+    return tuple(results)
+
+
+def body(axes, *args):
+    rows, tokens, model = args[0].shape
+    fits = axes["dp"] == SIDE * SIDE and axes["mp"] == DEPTH * SIDE
+    if fits and rows == 2 and tokens % 16 == 0 and model % 256 == 0:
+        return fast_body(*args)
+    return general_body(*args)
+
+
+def general_body(
     hidden_in,
     cotangent,
     lengths,
@@ -347,4 +1310,5 @@
         P(("dp", "mp")),
         P(("dp", "mp")),
     )
-    return jax.shard_map(body, mesh=mesh, in_specs=in_specs, out_specs=out_specs, check_vma=False)
+    return jax.shard_map(
+        functools.partial(body, dict(mesh.shape)), mesh=mesh, in_specs=in_specs, out_specs=out_specs, check_vma=False)

time: 1690 us -> 277 us (0.16)
  waiting for transfers between devices: 1180 us -> 0 us
  blocking collectives: 259 us -> 0 us
  Pallas kernels: 0 us -> 246 us
  matrix products: 78.8 us -> 0 us
  local copies, waits for them, and re-layouts: 96.8 us -> 20.4 us
  other arithmetic: 45.2 us -> 9.21 us
    reduce_scatter x12 -> x0, waiting for transfers between devices: 564 us -> none  [the longest x2 130 us: backward_layer(): lax.psum_scatter(value_terms.astype(jnp.bfloat16), 'mp', scatter_dimensio...]
    all_gather x9 -> x0, waiting for transfers between devices: 330 us -> none  [the longest x2 86.5 us: backward_layer(): grad_tokens = lax.all_gather(grad_down, 'mp', axis=1, tiled=True)]
    unnamed x29 -> x0, waiting for transfers between devices: 285 us -> none
    pallas_call x0 -> x1, Pallas kernels: none -> 246 us  [fused_call(): pl.pallas_call(functools.partial(fused_kernel, dims, names), out_shape=li...]
    all_gather x7 -> x0, blocking collectives: 175 us -> none  [the longest x1 75.5 us: fetch(): lax.all_gather(attn_out, ('dp', 'mp'), axis=1, tiled=True)]
    unnamed x2 -> x0, blocking collectives: 83.8 us -> none
    dot_general x36 -> x0, matrix products: 78.8 us -> none  [the longest x2 8.08 us: backward_layer(): jnp.einsum('rsd,fd->rsf', grad_tokens, ffn_second, preferred_element_type...]
    unnamed x218 -> x34, local copies, waits for them, and re-layouts: 54 us -> 2.58 us
  transfers between devices with their start and end apart: 25 -> 0, of which waited for: 24 -> 0; matrix products, arithmetic and copies ran while one was open for 7% -> 0% of each run, Pallas kernels for 0% -> 0%
where the time goes in v1:
time: 277 us
  Pallas kernels  246 us (89%)
  local copies, waits for them, and re-layouts  20.4 us (7%)
  other arithmetic  9.21 us (3%)
    pallas_call x1, Pallas kernels, fused_call(): pl.pallas_call(functools.partial(fused_kernel, dims, names), out_shape=li...  246 us

profile of v1, /device:TPU:0, one launch (start us, length us, event | category | flops | bytes accessed | tf_op | source)
XLA Modules:
  0.0 276.7 jit_solution(13996622903320088281)
XLA Ops:
  0.7 0.8 convert_dynamic-update-slice_fusion.3
  1.5 0.7 convert_dynamic-update-slice_fusion.2
  2.2 0.8 fusion.8
  3.0 0.8 reshape.219
  3.9 0.8 convert_dynamic-update-slice_fusion
  4.9 0.8 convert_dynamic-update-slice_fusion.1
  5.9 0.8 copy.102
  6.7 0.9 reshape.217
  7.7 0.1 reshape.218
  7.8 0.7 maximum_convert_fusion.1.refs_5_
  8.8 0.6 reshape.213.refs_2_
  9.5 0.1 copy.71
  9.7 0.1 reshape.215
  9.8 0.7 maximum_convert_fusion.refs_3_
  10.5 0.1 copy.67
  10.7 0.1 copy.68
  10.9 0.8 pad_maximum_fusion.2.refs_6_
  11.8 0.1 select_bitcast_fusion.1
  11.9 1.0 pad_maximum_fusion.refs_4_
  12.9 246.0 %layers.1 = (bf16[2,64,768]{2,1,0:T(8,128)(2,1)}, f32[2,64,768]{2,1,0:T(8,128)}, f32[2,24,1536]{2,1,0:T(8,128)}, f32[2,2,192,384]{3,2,1,0:T(8,128)}, f32[2,24,76...) custom-call(bf16[2,64,768]{2,1,0:T(8,128)(2,1)} %refs_0_.1, bf16[2,64,768]{2,1,0:T(8,128)(2,1)} %refs_1_.1, ...), custom_call_target="tpu_custom_call" | custom-call | tf_op jit(solution)/shard_map/layers/pallas_call | solution.py:1091
  258.9 0.8 slice_reduce_fusion
  259.9 0.7 slice.225
  260.7 0.1 reshape.226
  260.8 0.7 slice.242
  261.5 0.6 dynamic_slice.15
  262.1 0.9 fusion.11
  263.1 0.8 slice.228
  263.9 0.6 dynamic_slice.13
  264.7 0.7 fusion.4
  265.4 0.7 fusion.7
  266.0 0.9 slice_bitcast_fusion.1
  266.9 0.9 slice.230
  267.8 0.7 reshape.229
  268.6 0.1 reshape.227
  268.7 0.1 copy.79
  268.8 0.8 reshape.228
  269.6 0.6 copy.88
  270.3 0.1 reshape.220
  270.4 0.2 copy.72
  270.6 0.9 reshape.221
  271.4 0.2 fusion.1
  271.6 0.3 fusion
  272.0 0.9 copy.86
  272.9 0.9 copy.76
  273.7 0.7 fusion.10
  274.4 0.8 copy.83
  275.2 0.7 copy.125
  275.9 0.7 copy.126
  (78 shorter events, 1.6 us)
Async XLA Ops:
  0.6 8.8 %copy-start.8 = (bf16[192,192]{1,0:T(8,128)(2,1)S(1)}, bf16[192,192]{1,0:T(8,128)(2,1)}, u32[]{:S(2)}) copy-start(bf16[192,192]{1,0:T(8,128)(2,1)} %param.26) | copy-start | bytes 221188
  0.7 8.9 %copy-start.7 = (bf16[24,2304]{1,0:T(8,128)(2,1)S(1)}, bf16[24,2304]{1,0:T(8,128)(2,1)}, u32[]{:S(2)}) copy-start(bf16[24,2304]{1,0:T(8,128)(2,1)} %param.18) | copy-start | bytes 331780
  7.6 2.9 %copy-start.5 = (bf16[192,384]{1,0:T(8,128)(2,1)S(1)}, bf16[192,384]{1,0:T(8,128)(2,1)}, u32[]{:S(2)}) copy-start(bf16[192,384]{1,0:T(8,128)(2,1)} %param.20) | copy-start | bytes 442372
  7.8 2.9 %copy-start.6 = (bf16[384,192]{0,1:T(8,128)(2,1)S(1)}, bf16[384,192]{0,1:T(8,128)(2,1)}, u32[]{:S(2)}) copy-start(bf16[384,192]{0,1:T(8,128)(2,1)} %param.21) | copy-start | bytes 442372
  8.6 2.2 copy-start.9
  258.9 10.7 %copy-start.3 = (f32[2,24,1536]{2,1,0:T(8,128)S(1)}, f32[2,24,1536]{2,1,0:T(8,128)}, u32[]{:S(2)}) copy-start(f32[2,24,1536]{2,1,0:T(8,128)} %get-tuple-element.23) | copy-start | bytes 884740
  268.8 2.6 copy-start.1
  270.4 1.3 copy-start
  272.0 3.2 %copy-start.4 = (bf16[2,64,768]{2,1,0:T(8,128)(2,1)S(1)}, bf16[2,64,768]{2,1,0:T(8,128)(2,1)}, u32[]{:S(2)}) copy-start(bf16[2,64,768]{2,1,0:T(8,128)(2,1)} %get-tuple-element.104) | copy-start | bytes 589828
  272.9 3.1 %copy-start.2 = (f32[2,64,768]{2,1,0:T(8,128)S(1)}, f32[2,64,768]{2,1,0:T(8,128)}, u32[]{:S(2)}) copy-start(f32[2,64,768]{2,1,0:T(8,128)} %get-tuple-element.105) | copy-start | bytes 1179652

commit v2 on v1

--- a/solution.py
+++ b/solution.py
@@ -317,24 +317,48 @@
 
 
 def vec_rows(model, sizes):
+    lengths = dict(
+        qv=4 * sizes.hc, bo=model, beta1=model, b1=2 * sizes.nc, b2=model, beta2=model, g1=model, g2=model
+    )
     rows, at = {}, 0
-    for name, length in (
-        ("qv", 4 * sizes.hc),
-        ("bo", model),
-        ("beta1", model),
-        ("b1", 2 * sizes.nc),
-        ("b2", model),
-        ("beta2", model),
-        ("g1", model),
-        ("g2", model),
-    ):
+    for name, length in lengths.items():
         rows[name] = at
         at += length // model
-    return rows, at
-
-
-def fused_kernel(dims, names, *refs):
-    r = types.SimpleNamespace(**dict(zip(names, refs)))
+    return types.SimpleNamespace(**rows), at
+
+
+def named(tree):
+    if isinstance(tree, dict):
+        return types.SimpleNamespace(**{key: named(value) for key, value in tree.items()})
+    return [named(value) for value in tree] if isinstance(tree, list) else tree
+
+
+def fused_kernel(dims, tree, *refs):
+    given, outs, scratch, held, made = jax.tree.unflatten(tree, refs)
+    lay = [named(a | b | d) for a, b, d in zip(held["lay"], made["lay"], scratch["lay"])]
+    r = named(held | made | scratch)
+    given, outs = named(given), named(outs)
+
+    def fetch_copies():
+        pairs = []
+        for at in range(2):
+            far, near = given.lay[at], lay[at]
+            pairs += [(far.pai, near.pai), (far.pao, near.pao)]
+            if at == 0:
+                pairs += [(given.hid, r.hid)]
+            pairs += [(far.pfi, near.pfi), (far.pfo, near.pfo), (far.psh, near.psh), (far.pga, near.pga)]
+        pairs += [(given.len, r.len), (given.cot, r.cot)]
+        return [pltpu.make_async_copy(src, dst, r.ins.at[i]) for i, (src, dst) in enumerate(pairs)]
+
+    fetched = fetch_copies()
+    for copy in fetched:
+        copy.start()
+    stored = []
+
+    def store(src, dst):
+        copy = pltpu.make_async_copy(src, dst, r.outs.at[len(stored)])
+        copy.start()
+        stored.append(copy)
     model, tok, seq, layers = dims.model, dims.tok, dims.seq, dims.layers
     half_lanes = model // 2
     dp, mp = lax.axis_index("dp"), lax.axis_index("mp")
@@ -357,7 +381,6 @@
         pl.semaphore_signal(bar, inc=1, device_id={"dp": dp, "mp": other}, device_id_type=MESH)
     pl.semaphore_signal(bar, inc=1, device_id=sib, device_id_type=MESH)
     pl.semaphore_signal(bar, inc=1, device_id=yn, device_id_type=MESH)
-    pl.semaphore_wait(bar, PARTNERS)
 
     sent = []
 
@@ -369,7 +392,7 @@
     def push(src, dst, send, recv, dev):
         copy = remote(src, dst, send, recv, dev)
         copy.start()
-        sent.append(copy)
+        sent.append((None, copy))
 
     def arrived(dst, recv, send):
         remote(dst, dst, send, recv, sib).wait_recv()
@@ -432,49 +455,134 @@
                 pl.when(jnp.logical_not(local))(copy.wait_send)
 
     chunks = dims.chunks
-
-    def unit(i, grads, z_slice, x_at, y_at):
+    every, first, second = pl.ds(0, DEPTH), pl.ds(0, 2), pl.ds(2, 2)
+    both = pl.ds(0, 2)
+
+    def view(i, grads, band, z_slice, x_at, y_at):
         kind, layer, which, part = chunks[i]
+        full = dims.unit_rows[kind]
+        begin, count = {"a": (0, full - 32), "b": (full - 32, 16), "c": (full - 16, 16)}[band]
         if kind == "A":
-            ref = r.ga0 if layer == 0 else r.ga1
-            return ref.at[y_at, z_slice, x_at, :, pl.ds(part * model, model)]
-        ref = (r.dw0, r.dw1)[layer] if grads else (r.w0, r.w1)[layer]
-        lanes = pl.ds(pl.multiple_of(y_at * half_lanes, 128), half_lanes)
-        return ref.at[which, z_slice, x_at, pl.ds(part * dims.rows, dims.rows), lanes]
-
-    every, first, second = pl.ds(0, DEPTH), pl.ds(0, 2), pl.ds(2, 2)
-
-    def gather_z(i):
-        own = unit(i, False, pl.ds(z, 1), x, y)
-        for d in range(1, DEPTH):
-            push(own, own, r.gs.at[i, d - 1], r.gr.at[i, d - 1], zdev[d - 1])
-
-    def gather_xy(i):
-        for d in range(1, DEPTH):
-            got = unit(i, False, pl.ds(lax.rem(z + DEPTH - d, DEPTH), 1), x, y)
-            arrived(got, r.gr.at[i, d - 1], r.gs.at[i, d - 1])
-        own = unit(i, False, every, x, y)
-        push(own, own, r.gs.at[i, 3], r.gr.at[i, 3], xn)
-        push(own, own, r.gs.at[i, 4], r.gr.at[i, 4], yn)
-
-    def gather_on(i):
-        arrived(unit(i, False, every, 1 - x, y), r.gr.at[i, 3], r.gs.at[i, 3])
-        arrived(unit(i, False, every, x, 1 - y), r.gr.at[i, 4], r.gs.at[i, 4])
-        over_x = unit(i, False, first, x, 1 - y)
-        over_y = unit(i, False, second, 1 - x, y)
-        push(over_x, over_x, r.gs.at[i, 5], r.gr.at[i, 5], xn)
-        push(over_y, over_y, r.gs.at[i, 6], r.gr.at[i, 6], yn)
-
-    def gather_end(i):
-        arrived(unit(i, False, first, 1 - x, 1 - y), r.gr.at[i, 5], r.gs.at[i, 5])
-        arrived(unit(i, False, second, 1 - x, 1 - y), r.gr.at[i, 6], r.gs.at[i, 6])
-
-    def slots(i):
-        kind, layer, which, part = chunks[i]
-        at = dims.slot[i]
-        if kind == "A":
-            return r.raa.at[at], r.rba.at[at], r.rca.at[at]
-        return r.raf.at[at], r.rbf.at[at], r.rcf.at[at]
+            ref = lay[layer].ga
+            y_pick = both if y_at is None else y_at
+            return ref.at[y_pick, z_slice, x_at, pl.ds(begin, count), pl.ds(part * model, model)]
+        ref = lay[layer].dw if grads else lay[layer].w
+        lanes = pl.ds(0, model)
+        if y_at is not None:
+            lanes = pl.ds(pl.multiple_of(y_at * half_lanes, 128), half_lanes)
+        return ref.at[which, z_slice, x_at, pl.ds(part * full + begin, count), lanes]
+
+    UP, DOWN, FAR, RELAY = range(4)
+    z_far = lax.rem(z + 2, DEPTH)
+    z_up, z_down = lax.rem(z + 1, DEPTH), lax.rem(z + DEPTH - 1, DEPTH)
+    z_end = DEPTH - 1 - z
+    has_up, has_down = z < DEPTH - 1, z > 0
+    inner = (z == 1) | (z == 2)
+    outer = (z == 0) | (z == 3)
+    z_out = jnp.where(z == 1, 0, 3)
+    z_in = jnp.where(z == 0, 1, 2)
+
+    def push_if(cond, src, dst, send, recv, dev):
+        copy = remote(src, dst, send, recv, dev)
+        pl.when(cond)(copy.start)
+        sent.append((cond, copy))
+
+    def wait_sent():
+        for cond, copy in sent:
+            if cond is None:
+                copy.wait_send()
+            else:
+                pl.when(cond)(copy.wait_send)
+        sent.clear()
+
+    def arrived_if(cond, dst, recv, send):
+        pl.when(cond)(remote(dst, dst, send, recv, sib).wait_recv)
+
+    def at_z(zz):
+        return device(c, x, y, zz)
+
+    def line_send(part, send, recv):
+        own = part(z)
+        push_if(has_up, own, own, send(UP), recv(UP), at_z(z_up))
+        push_if(has_down, own, own, send(DOWN), recv(DOWN), at_z(z_down))
+        push(own, own, send(FAR), recv(FAR), at_z(z_far))
+
+    def line_relay(part, send, recv):
+        far = part(z_far)
+        arrived_if(inner, far, recv(FAR), send(FAR))
+        push_if(inner, far, far, send(RELAY), recv(RELAY), at_z(z_out))
+
+    def line_end(part, send, recv):
+        arrived_if(has_down, part(z_down), recv(UP), send(UP))
+        arrived_if(has_up, part(z_up), recv(DOWN), send(DOWN))
+        arrived_if(outer, part(z_far), recv(FAR), send(FAR))
+        arrived_if(outer, part(z_end), recv(RELAY), send(RELAY))
+
+    def sems(ref_send, ref_recv, i, base):
+        return (lambda k: ref_send.at[i, base + k]), (lambda k: ref_recv.at[i, base + k])
+
+    def one(zz):
+        return pl.ds(zz, 1)
+
+    def parts_of(i, grads):
+        return (
+            lambda zz: view(i, grads, "a", one(zz), x, y),
+            lambda zz: view(i, grads, "b", one(zz), both, y),
+            lambda zz: view(i, grads, "c", one(zz), x, None),
+        )
+
+    def gather_sems(i, base):
+        return sems(r.gs, r.gr, i, base)
+
+    def gather_push(i, k, piece, dev):
+        push(piece, piece, r.gs.at[i, k], r.gr.at[i, k], dev)
+
+    def gather_wait(i, k, piece):
+        arrived(piece, r.gr.at[i, k], r.gs.at[i, k])
+
+    def gather_0(i):
+        gather_push(i, 16, view(i, False, "b", one(z), x, y), xn)
+        gather_push(i, 17, view(i, False, "c", one(z), x, y), yn)
+        line_send(parts_of(i, False)[0], *gather_sems(i, 0))
+
+    def gather_1(i):
+        a, b, c_part = parts_of(i, False)
+        gather_wait(i, 16, view(i, False, "b", one(z), 1 - x, y))
+        line_send(b, *gather_sems(i, 4))
+        gather_wait(i, 17, view(i, False, "c", one(z), x, 1 - y))
+        line_send(c_part, *gather_sems(i, 8))
+        line_relay(a, *gather_sems(i, 0))
+
+    def gather_2(i):
+        a, b, c_part = parts_of(i, False)
+        line_end(a, *gather_sems(i, 0))
+        own = view(i, False, "a", every, x, y)
+        gather_push(i, 12, own, xn)
+        gather_push(i, 13, own, yn)
+        line_relay(b, *gather_sems(i, 4))
+        line_relay(c_part, *gather_sems(i, 8))
+
+    def gather_3(i):
+        a, b, c_part = parts_of(i, False)
+        line_end(b, *gather_sems(i, 4))
+        gather_push(i, 18, view(i, False, "b", every, both, y), yn)
+        line_end(c_part, *gather_sems(i, 8))
+        gather_push(i, 19, view(i, False, "c", every, x, None), xn)
+        gather_wait(i, 12, view(i, False, "a", every, 1 - x, y))
+        gather_wait(i, 13, view(i, False, "a", every, x, 1 - y))
+        gather_push(i, 14, view(i, False, "a", first, x, 1 - y), xn)
+        gather_push(i, 15, view(i, False, "a", second, 1 - x, y), yn)
+
+    def gather_4(i):
+        gather_wait(i, 14, view(i, False, "a", first, 1 - x, 1 - y))
+        gather_wait(i, 15, view(i, False, "a", second, 1 - x, 1 - y))
+        gather_wait(i, 18, view(i, False, "b", every, both, 1 - y))
+        gather_wait(i, 19, view(i, False, "c", every, 1 - x, None))
+
+    def pump(step):
+        for lag, stage in enumerate((gather_0, gather_1, gather_2, gather_3, gather_4)):
+            if 0 <= step - lag < len(chunks):
+                stage(step - lag)
 
     def add_into(ref, extra):
         total = ref[...].astype(F32)
@@ -482,59 +590,134 @@
             total = total + more[...].astype(F32)
         ref[...] = total.astype(BF)
 
-    def reduce_a(i):
-        ra, rb, rc = slots(i)
-        push(unit(i, True, first, 1 - x, 1 - y), ra.at[0], r.ss.at[i, 5], r.sr.at[i, 5], xn)
-        push(unit(i, True, second, 1 - x, 1 - y), ra.at[1], r.ss.at[i, 6], r.sr.at[i, 6], yn)
-
-    def reduce_b(i):
-        ra, rb, rc = slots(i)
-        arrived(ra.at[0], r.sr.at[i, 5], r.ss.at[i, 5])
-        add_into(unit(i, True, first, x, 1 - y), [ra.at[0]])
-        arrived(ra.at[1], r.sr.at[i, 6], r.ss.at[i, 6])
-        add_into(unit(i, True, second, 1 - x, y), [ra.at[1]])
-        push(unit(i, True, every, 1 - x, y), rb.at[0], r.ss.at[i, 3], r.sr.at[i, 3], xn)
-        push(unit(i, True, every, x, 1 - y), rb.at[1], r.ss.at[i, 4], r.sr.at[i, 4], yn)
-
-    def reduce_c(i):
-        ra, rb, rc = slots(i)
-        arrived(rb.at[0], r.sr.at[i, 3], r.ss.at[i, 3])
-        arrived(rb.at[1], r.sr.at[i, 4], r.ss.at[i, 4])
-        add_into(unit(i, True, every, x, y), [rb.at[0], rb.at[1]])
-        for d in range(1, DEPTH):
-            src = unit(i, True, pl.ds(lax.rem(z + d, DEPTH), 1), x, y)
-            push(src, rc.at[pl.ds(d - 1, 1)], r.ss.at[i, d - 1], r.sr.at[i, d - 1], zdev[d - 1])
-
-    def reduce_end(i):
+    def slots(i, name):
+        return getattr(r.red[chunks[i][0] == "F"], name).at[dims.slot[i]]
+
+    def reduce_push(i, k, src, dst, dev):
+        push(src, dst, r.ss.at[i, k], r.sr.at[i, k], dev)
+
+    def reduce_wait(i, k, dst):
+        arrived(dst, r.sr.at[i, k], r.ss.at[i, k])
+
+    def line_reduce_send(part, land, send, recv):
+        push_if(has_up, part(z_up), land.at[UP], send(UP), recv(UP), at_z(z_up))
+        push_if(has_down, part(z_down), land.at[DOWN], send(DOWN), recv(DOWN), at_z(z_down))
+        push_if(outer, part(z_end), land.at[RELAY], send(RELAY), recv(RELAY), at_z(z_in))
+        push_if(outer, part(z_far), land.at[FAR], send(FAR), recv(FAR), at_z(z_far))
+
+    def line_reduce_relay(part, land, send, recv):
+        @pl.when(inner)
+        def _():
+            arrived(land.at[RELAY], recv(RELAY), send(RELAY))
+            add_into(part(z_far), [land.at[RELAY]])
+
+        push_if(inner, part(z_far), land.at[FAR], send(FAR), recv(FAR), at_z(z_far))
+
+    def line_reduce_end(part, land, send, recv):
+        arrived(land.at[FAR], recv(FAR), send(FAR))
+
+        @pl.when(inner)
+        def _():
+            arrived(land.at[UP], recv(UP), send(UP))
+            arrived(land.at[DOWN], recv(DOWN), send(DOWN))
+            add_into(part(z), [land.at[FAR], land.at[UP], land.at[DOWN]])
+
+        @pl.when(z == 0)
+        def _():
+            arrived(land.at[DOWN], recv(DOWN), send(DOWN))
+            add_into(part(z), [land.at[FAR], land.at[DOWN]])
+
+        @pl.when(z == DEPTH - 1)
+        def _():
+            arrived(land.at[UP], recv(UP), send(UP))
+            add_into(part(z), [land.at[FAR], land.at[UP]])
+
+    def reduce_sems(i, base):
+        return sems(r.ss, r.sr, i, base)
+
+    def reduce_0(i):
+        over = slots(i, "ad")
+        reduce_push(i, 14, view(i, True, "a", first, 1 - x, 1 - y), over.at[0], xn)
+        reduce_push(i, 15, view(i, True, "a", second, 1 - x, 1 - y), over.at[1], yn)
+        reduce_push(i, 18, view(i, True, "b", every, both, 1 - y), slots(i, "by"), yn)
+        reduce_push(i, 19, view(i, True, "c", every, 1 - x, None), slots(i, "cx"), xn)
+
+    def reduce_1(i):
+        a, b, c_part = parts_of(i, True)
+        over, beside = slots(i, "ad"), slots(i, "an")
+        reduce_wait(i, 14, over.at[0])
+        add_into(view(i, True, "a", first, x, 1 - y), [over.at[0]])
+        reduce_push(i, 13, view(i, True, "a", every, x, 1 - y), beside.at[1], yn)
+        reduce_wait(i, 15, over.at[1])
+        add_into(view(i, True, "a", second, 1 - x, y), [over.at[1]])
+        reduce_push(i, 12, view(i, True, "a", every, 1 - x, y), beside.at[0], xn)
+        reduce_wait(i, 18, slots(i, "by"))
+        add_into(view(i, True, "b", every, both, y), [slots(i, "by")])
+        line_reduce_send(b, slots(i, "bz"), *reduce_sems(i, 4))
+        reduce_wait(i, 19, slots(i, "cx"))
+        add_into(view(i, True, "c", every, x, None), [slots(i, "cx")])
+        line_reduce_send(c_part, slots(i, "cz"), *reduce_sems(i, 8))
+
+    def reduce_2(i):
+        a, b, c_part = parts_of(i, True)
+        beside = slots(i, "an")
+        reduce_wait(i, 12, beside.at[0])
+        reduce_wait(i, 13, beside.at[1])
+        add_into(view(i, True, "a", every, x, y), [beside.at[0], beside.at[1]])
+        line_reduce_send(a, slots(i, "az"), *reduce_sems(i, 0))
+        line_reduce_relay(b, slots(i, "bz"), *reduce_sems(i, 4))
+        line_reduce_relay(c_part, slots(i, "cz"), *reduce_sems(i, 8))
+
+    def reduce_3(i):
+        a, b, c_part = parts_of(i, True)
+        line_reduce_end(b, slots(i, "bz"), *reduce_sems(i, 4))
+        reduce_push(i, 16, view(i, True, "b", one(z), 1 - x, y), slots(i, "bx"), xn)
+        line_reduce_end(c_part, slots(i, "cz"), *reduce_sems(i, 8))
+        reduce_push(i, 17, view(i, True, "c", one(z), x, 1 - y), slots(i, "cy"), yn)
+        line_reduce_relay(a, slots(i, "az"), *reduce_sems(i, 0))
+
+    def reduce_4(i):
         kind, layer, which, part = chunks[i]
         at = dims.slot[i]
-        ra, rb, rc = slots(i)
-        total = unit(i, True, pl.ds(z, 1), x, y)[...].astype(F32)[0]
-        for d in range(1, DEPTH):
-            arrived(rc.at[pl.ds(d - 1, 1)], r.sr.at[i, d - 1], r.ss.at[i, d - 1])
-            total = total + rc[d - 1].astype(F32)
+        line_reduce_end(parts_of(i, True)[0], slots(i, "az"), *reduce_sems(i, 0))
+        reduce_wait(i, 16, slots(i, "bx"))
+        reduce_wait(i, 17, slots(i, "cy"))
+        total = jnp.concatenate(
+            [
+                view(i, True, "a", one(z), x, y)[...].astype(F32)[0],
+                (view(i, True, "b", one(z), x, y)[...].astype(F32) + slots(i, "bx")[...].astype(F32))[0],
+                (view(i, True, "c", one(z), x, y)[...].astype(F32) + slots(i, "cy")[...].astype(F32))[0],
+            ],
+            axis=0,
+        )
         if kind == "A":
-            out = (r.da0, r.da1)[layer]
+            out = lay[layer].da
             rows = total.shape[0] // 2
             out[c, :, part * model : (part + 1) * model] = jnp.where(c == 0, total[:rows], total[rows:])
             r.fsa[at] = jnp.where(c == 0, total[rows:], total[:rows])
             push(r.fsa.at[at], r.fra.at[at], r.fs.at[i], r.fr.at[i], sib)
         else:
-            out = (r.df0, r.df1)[layer]
+            out = lay[layer].df
             rows = pl.ds(part * dims.rows, dims.rows)
-            out[c, which, rows, :] = total
-            push(out.at[c, which, rows, :], r.frf.at[at], r.fs.at[i], r.fr.at[i], sib)
+            lanes = total.shape[1] // 2
+            out[c, which, rows, :] = jnp.where(c == 0, total[:, :lanes], total[:, lanes:])
+            r.fsf[at] = jnp.where(c == 0, total[:, lanes:], total[:, :lanes])
+            push(r.fsf.at[at], r.frf.at[at], r.fs.at[i], r.fr.at[i], sib)
 
     def reduce_out(i):
         kind, layer, which, part = chunks[i]
         at = dims.slot[i]
         if kind == "A":
             arrived(r.fra.at[at], r.fr.at[i], r.fs.at[i])
-            (r.da0, r.da1)[layer][1 - c, :, part * model : (part + 1) * model] = r.fra[at]
+            lay[layer].da[1 - c, :, part * model : (part + 1) * model] = r.fra[at]
+            if part == layers[layer].wide // model - 1:
+                store(lay[layer].da, outs.lay[layer].da)
         else:
             arrived(r.frf.at[at], r.fr.at[i], r.fs.at[i])
             rows = pl.ds(part * dims.rows, dims.rows)
-            (r.df0, r.df1)[layer][1 - c, which, rows, :] = r.frf[at]
+            lay[layer].df[1 - c, which, rows, :] = r.frf[at]
+            if part == layers[layer].nr // dims.rows - 1:
+                store(lay[layer].df.at[:, which], outs.lay[layer].df.at[:, which])
 
     def total_step(work, land, step, sends, recvs):
         dev = (sib, xn, yn, zn, zfar)[step]
@@ -565,31 +748,24 @@
     def layer_vecs(at):
         sizes, rows, base = layers[at], dims.rows_of[at], dims.base[at]
         if sizes.hc * 2 == model:
-            qv = r.vw[5, pl.ds(base + rows["qv"] + c, 1), :]
+            qv = r.vw[5, pl.ds(base + rows.qv + c, 1), :]
         else:
-            both = vec_row(base + rows["qv"])
+            both = vec_row(base + rows.qv)
             qv = jnp.where(c == 0, both[:, : 2 * sizes.hc], both[:, 2 * sizes.hc :])
         span = sizes.nc // model
-        b1 = [r.vw[5, pl.ds(base + rows["b1"] + c * span + s, 1), :] for s in range(span)]
+        b1 = [r.vw[5, pl.ds(base + rows.b1 + c * span + s, 1), :] for s in range(span)]
         found = types.SimpleNamespace(bq=qv[:, : sizes.hc], bv=qv[:, sizes.hc :], b1=b1)
-        for name in ("bo", "beta1", "b2", "beta2", "g1", "g2"):
-            setattr(found, name, vec_row(base + rows[name]))
+        for name, row in vars(rows).items():
+            if not hasattr(found, name):
+                setattr(found, name, vec_row(base + row))
         return found
 
-    kept = [
-        types.SimpleNamespace(
-            **{
-                name: getattr(r, f"{name}{at}")
-                for name in ("xb", "q", "kv", "a", "ctx", "n1", "s1", "hb", "g", "gp", "n2", "s2")
-            }
-        )
-        for at in range(2)
-    ]
-    wa = (r.wa0, r.wa1)
-    weights = (r.w0, r.w1)
+    kept = lay
+    wa = [one_layer.wa for one_layer in lay]
+    weights = [one_layer.w for one_layer in lay]
 
     def order_rows(at, part):
-        gathered, whole = (r.ga0, r.ga1)[at], wa[at]
+        gathered, whole = lay[at].ga, wa[at]
         cols = slice(part * model, (part + 1) * model)
         rows = gathered.shape[3] // 2
         span = DEPTH * 2 * rows
@@ -604,7 +780,7 @@
                     whole[begin : begin + 2 * rows, cols] = both
 
     def store_grad_rows(at, y_at, value, cols):
-        blocks = (r.ga0, r.ga1)[at]
+        blocks = lay[at].ga
         rows = blocks.shape[3] // 2
         span = DEPTH * 2 * rows
         for z_at in range(DEPTH):
@@ -630,8 +806,10 @@
     def attention(at):
         sizes, keep = layers[at], kept[at]
         lane = lax.broadcasted_iota(jnp.int32, (1, model), 1)
-        row = (y * SIDE + row_core) * 2 + x
-        length = jnp.sum(jnp.where(lane == row, vec_row(dims.length_row), 0.0), axis=1, keepdims=True)
+        first_lane = (y * SIDE + row_core) * group + x
+        entry = vec_row(dims.length_row)
+        entry = jnp.where(lane == first_lane, 256.0 * entry, jnp.where(lane == first_lane + 2, entry, 0.0))
+        length = jnp.sum(entry, axis=1, keepdims=True)
         valid = lax.broadcasted_iota(jnp.int32, (1, seq), 1).astype(F32) < length
         for h in range(sizes.heads):
             q = keep.q[:, h * HEAD : (h + 1) * HEAD]
@@ -645,7 +823,7 @@
 
     def attention_back(at, grad_ctx):
         sizes, keep = layers[at], kept[at]
-        dkv, gp = (r.dkv0, r.dkv1)[at], (r.dp0, r.dp1)[at]
+        dkv, gp = lay[at].dkv, lay[at].dp
         for h in range(sizes.heads):
             q = keep.q[:, h * HEAD : (h + 1) * HEAD]
             k, v = head_kv(at, h)
@@ -687,59 +865,161 @@
 
     def weight_grad(at, which, left, right):
         sizes = layers[at]
-        dw = (r.dw0, r.dw1)[at]
+        dw = lay[at].dw
         span = model // 2
         zb = sizes.zb // 2
         for b in range(sizes.nc // span):
             value = mm(left[:, b * span : (b + 1) * span], right[...], 0, 0).astype(BF)
             dw[which, b * zb : (b + 1) * zb] = value.reshape(zb, 2, sizes.nr, model)
 
-    spread(r.hid, r.xin, r.hs, r.hr)
-    push(r.vec, r.vl.at[0], r.vs.at[0], r.vr.at[0], sib)
-    push(r.pa0.at[1 - c], r.ar0, r.is_.at[0], r.ir.at[0], sib)
-    push(r.pf0.at[1 - c], r.fr0, r.is_.at[1], r.ir.at[1], sib)
-    push(r.pa1.at[1 - c], r.ar1, r.is_.at[2], r.ir.at[2], sib)
-    push(r.pf1.at[1 - c], r.fr1, r.is_.at[3], r.ir.at[3], sib)
-
-    def prepare_a(at):
-        own_ref, land, blocks = (r.pa0, r.pa1)[at], (r.ar0, r.ar1)[at], (r.ga0, r.ga1)[at]
+
+    def pack_a(at):
+        sizes, width = layers[at], 2 * layers[at].hc
+        rows_in = lay[at].pai[...].astype(F32)
+        rows_out = lay[at].pao[...].astype(F32)
+        halves = []
+        for h in range(2):
+            own = slice(h * sizes.hc, (h + 1) * sizes.hc)
+            pieces = [rows_in[:, p * width : (p + 1) * width][:, own] for p in range(3)]
+            halves.append(jnp.concatenate(pieces + [rows_out[:, own]], axis=1))
+        send = lay[at].asend
+        send[...] = jnp.where(c == 0, halves[1], halves[0])
+        if at == 0:
+            pl.semaphore_wait(bar, PARTNERS)
+        push(send, lay[at].ar, r.is_.at[2 * at], r.ir.at[2 * at], sib)
+        return jnp.where(c == 0, halves[0], halves[1])
+
+    def pack_f(at):
+        sizes = layers[at]
+        first = lay[at].pfi[...].astype(F32).T
+        second = lay[at].pfo[...].astype(F32)
+        if dims.turned[at]:
+            second = second.T
+        send, own = lay[at].fsend, []
+        for which, value in enumerate((first, second)):
+            low_half, high_half = value[: sizes.nr], value[sizes.nr :]
+            own.append(jnp.where(c == 0, low_half, high_half))
+            send[which] = jnp.where(c == 0, high_half, low_half).astype(BF)
+        push(send, lay[at].fr, r.is_.at[2 * at + 1], r.ir.at[2 * at + 1], sib)
+        return own
+
+    def prepare_a(at, own):
+        land, blocks = lay[at].ar, lay[at].ga
         arrived(land, r.ir.at[2 * at], r.is_.at[2 * at])
-        own, other = own_ref[c], land[...]
-        both = [jnp.where(c == 0, own, other), jnp.where(c == 0, other, own)]
-        blocks[y, z, x] = jnp.concatenate(both, axis=0).astype(BF)
-
-    def prepare_f(at):
-        own_ref, land = (r.pf0, r.pf1)[at], (r.fr0, r.fr1)[at]
+        other = land[...]
+        pair = [jnp.where(c == 0, own, other), jnp.where(c == 0, other, own)]
+        blocks[y, z, x] = jnp.concatenate(pair, axis=0).astype(BF)
+
+    def prepare_f(at, own):
+        land = lay[at].fr
         arrived(land, r.ir.at[2 * at + 1], r.is_.at[2 * at + 1])
         lanes = pl.ds(pl.multiple_of(y * half_lanes, 128), half_lanes)
-        weights[at][:, z, x, :, lanes] = own_ref[c] + land[...]
-
-    prepare_a(0)
-    gather_z(0)
-    gather_z(1)
-    prepare_f(0)
-    gather_z(2)
-    arrived(r.vl.at[0], r.vr.at[0], r.vs.at[0])
-    r.vw[1] = r.vec[...] + r.vl[0]
+        for which in range(2):
+            other = land[which].astype(F32)
+            pair = [jnp.where(c == 0, own[which], other), jnp.where(c == 0, other, own[which])]
+            weights[at][which, z, x, :, lanes] = jnp.concatenate(pair, axis=1).astype(BF)
+
+    group = dims.group
+    per_row = model // group
+    index = dp * DEPTH * SIDE + mp
+
+    def targets(at_group):
+        result, begin = jnp.full_like(at_group, dims.length_row * per_row) + dp, 0
+        for at, sizes in enumerate(layers):
+            base = dims.base[at] * per_row
+            head, count_b = sizes.hc // group, sizes.nr // group
+            up_at = dims.rows_of[at].b1 * per_row
+            count = dims.shift_groups[at]
+            g = index * count + (at_group - begin)
+            w = g % (2 * head)
+            qv = (w // head) * (2 * head) + (g // (2 * head)) * head + w % head
+            b = g - up_at
+            up_to = up_at + ((b % (2 * count_b)) // count_b) * (8 * count_b)
+            up_to = up_to + (b // (2 * count_b)) * count_b + b % count_b
+            place = jnp.where(g < 4 * head, qv, jnp.where((b >= 0) & (b < 16 * count_b), up_to, g))
+            inside = (at_group >= begin) & (at_group < begin + count)
+            result = jnp.where(inside, base + place, result)
+            begin += count
+            count = dims.gain_groups[at]
+            place = dims.rows_of[at].g1 * per_row + index * count + (at_group - begin)
+            inside = (at_group >= begin) & (at_group < begin + count)
+            result = jnp.where(inside, base + place, result)
+            begin += count
+        return result // per_row, result % per_row
+
+    groups = dims.vec_rows
+    lane_group = lax.broadcasted_iota(jnp.int32, (groups, dims.lanes), 1) // group
+    lane_own = lane_group == lax.broadcasted_iota(jnp.int32, (groups, dims.lanes), 0)
+
+    def place_masks():
+        down = lax.broadcasted_iota(jnp.int32, (groups, 1), 0)
+        across = lax.broadcasted_iota(jnp.int32, (1, groups), 1)
+        row_down, place_down = targets(down)
+        row_across, _ = targets(across)
+        lane = lax.broadcasted_iota(jnp.int32, (groups, model), 1) // group
+        to_row = jnp.where(row_across == down, 1.0, 0.0).astype(BF)
+        from_row = jnp.where(row_down == across, 1.0, 0.0).astype(BF)
+        return lane == place_down, to_row, from_row
+
+    def pack_vectors():
+        lengths = r.len[...].astype(F32).reshape(1, 2) * jnp.where(mp == 0, 1.0, 0.0)
+        high = jnp.floor(lengths * (1.0 / 256.0))
+        pieces = []
+        for own in lay:
+            pieces += [own.psh[...].astype(F32).reshape(1, -1), own.pga[...].astype(F32).reshape(1, -1)]
+        pieces += [high, lengths - 256.0 * high]
+        used = sum(p.shape[1] for p in pieces)
+        values = jnp.concatenate(pieces + [jnp.zeros((1, dims.lanes - used), F32)], axis=1)
+        spread_out = jnp.where(lane_own, values, 0.0).astype(BF)
+        i = lax.broadcasted_iota(jnp.int32, (dims.lanes, model), 0) % group
+        j = lax.broadcasted_iota(jnp.int32, (dims.lanes, model), 1) % group
+        r.hot[...] = jnp.where(i == j, 1.0, 0.0).astype(BF)
+        in_place, to_row, _ = place_masks()
+        wide = jnp.where(in_place, mm(spread_out, r.hot[...], 1, 0), 0.0).astype(BF)
+        return mm(to_row, wide, 1, 0)
+
+    def unpack_vectors(values):
+        in_place, _, from_row = place_masks()
+        total, rest = None, values
+        for _ in range(3):
+            low_part = rest.astype(BF)
+            rest = rest - low_part.astype(F32)
+            wide = jnp.where(in_place, mm(from_row, low_part, 1, 0), 0.0).astype(BF)
+            term = jnp.where(lane_own, mm(wide, r.hot[...], 1, 1), 0.0)
+            total = term if total is None else total + term
+        return rowsum(total)
+
+    for copy in fetched[:2]:
+        copy.wait()
+    own_a = pack_a(0)
+    fetched[2].wait()
+    spread(r.hid, r.xin, r.hs, r.hr)
+    for copy in fetched[3:5]:
+        copy.wait()
+    own_f = pack_f(0)
+    prepare_a(0, own_a)
+    pump(0)
+    prepare_f(0, own_f)
+    pump(1)
+    for copy in fetched[5:]:
+        copy.wait()
+    r.vw[0] = pack_vectors()
+    total_step(r.vw, r.vl, 0, r.vs, r.vr)
+    own_a, own_f = pack_a(1), pack_f(1)
+    total_add(r.vw, r.vl, 0, r.vs, r.vr)
     total_step(r.vw, r.vl, 1, r.vs, r.vr)
-    spread_done(r.hid, r.xin, r.hs, r.hr, r.os.at[0], r.os.at[1])
-    gather_xy(0)
-    gather_z(3)
+    prepare_a(1, own_a)
+    prepare_f(1, own_f)
     total_add(r.vw, r.vl, 1, r.vs, r.vr)
     total_step(r.vw, r.vl, 2, r.vs, r.vr)
-    prepare_a(1)
-    prepare_f(1)
-    gather_xy(1)
-    gather_on(0)
-    gather_z(4)
+    pump(2)
+    spread_done(r.hid, r.xin, r.hs, r.hr, r.os.at[0], r.os.at[1])
     total_add(r.vw, r.vl, 2, r.vs, r.vr)
     total_step(r.vw, r.vl, 3, r.vs, r.vr)
-    gather_xy(2)
-    gather_on(1)
-    gather_z(5)
+    pump(3)
     total_add(r.vw, r.vl, 3, r.vs, r.vr)
     total_step(r.vw, r.vl, 4, r.vs, r.vr)
-    gather_end(0)
+    pump(4)
     total_add(r.vw, r.vl, 4, r.vs, r.vr)
     vecs = [layer_vecs(0), layer_vecs(1)]
 
@@ -781,65 +1061,47 @@
 
     if layers[1].pad:
         kept[1].ctx[...] = jnp.zeros_like(kept[1].ctx)
-        r.dp1[...] = jnp.zeros_like(r.dp1)
+        lay[1].dp[...] = jnp.zeros_like(lay[1].dp)
     kept[0].xb[...] = r.xin[...].reshape(tok, model)
     project(0, kept[0].xb[...], (0,))
-    gather_xy(3)
-    gather_on(2)
-    gather_z(6)
-    gather_end(1)
+    pump(5)
     project(0, kept[0].xb[...], (1,))
     send_kv(0)
     spread(r.cot, r.cin, r.cs, r.cr)
-    gather_xy(4)
-    gather_on(3)
-    gather_z(7)
-    gather_end(2)
+    pump(6)
+    pump(7)
     wait_kv(0)
     attention(0)
     wait_branch = exchange(attend_out(0))
-    gather_xy(5)
-    gather_on(4)
-    gather_z(8)
-    gather_end(3)
+    pump(8)
     normed = norm_one(0, kept[0].xb[...].astype(F32), wait_branch())
     up(0, vecs[0])
-    gather_xy(6)
-    gather_on(5)
-    gather_end(4)
     spread_done(r.cot, r.cin, r.cs, r.cr, r.os.at[2], r.os.at[3])
-    gather_xy(7)
-    gather_on(6)
-    gather_end(5)
+    pump(9)
     wait_branch = exchange(down(0))
-    gather_xy(8)
-    gather_on(7)
-    gather_end(6)
+    pump(10)
     middle = norm_two(0, normed, wait_branch())
     kept[1].xb[...] = middle.astype(BF)
     project(1, kept[1].xb[...], (0,))
     send_kv(1)
+    pump(11)
     wait_kv(1)
     attention(1)
     wait_branch = exchange(attend_out(1))
-    gather_on(8)
-    gather_end(7)
     normed = norm_one(1, middle, wait_branch())
     up(1, vecs[1])
-    gather_end(8)
+    pump(12)
     wait_branch = exchange(down(1))
     final = norm_two(1, normed, wait_branch())
     r.oblk[...] = final.astype(BF).reshape(r.oblk.shape)
     collect(r.oblk, r.oland, r.ys, r.yr)
-    for copy in sent:
-        copy.wait_send()
-    sent.clear()
+    wait_sent()
 
     r.vw[0] = jnp.zeros_like(r.vw[0])
     once = jnp.where(c == 0, 1.0, 0.0)
 
     def put_vec(at, name, value):
-        row = dims.base[at] + dims.rows_of[at][name]
+        row = dims.base[at] + getattr(dims.rows_of[at], name)
         r.vw[0, row : row + 1, :] = value * once
 
     def back_two(at, grad):
@@ -854,7 +1116,7 @@
 
     def back_up(at):
         sizes, keep = layers[at], kept[at]
-        base = dims.base[at] + dims.rows_of[at]["b1"]
+        base = dims.base[at] + dims.rows_of[at].b1
         span = sizes.nc // model
         for b in range(span):
             cols = slice(b * model, (b + 1) * model)
@@ -883,19 +1145,19 @@
         return dz1, grad_ctx
 
     def send_dkv(at):
-        dkv, land = (r.dkv0, r.dkv1)[at], (r.dkr0, r.dkr1)[at]
+        dkv, land = lay[at].dkv, lay[at].dkr
         push(dkv.at[1 - half], land, r.ks.at[2 + at], r.kr.at[2 + at], zn)
 
     def take_dkv(at):
         sizes = layers[at]
-        dkv, land, gp = (r.dkv0, r.dkv1)[at], (r.dkr0, r.dkr1)[at], (r.dp0, r.dp1)[at]
+        dkv, land, gp = lay[at].dkv, lay[at].dkr, lay[at].dp
         arrived(land, r.kr.at[2 + at], r.ks.at[2 + at])
         total = (dkv[half].astype(F32) + land[...].astype(F32)).astype(BF)
         gp[:, sizes.hc : 3 * sizes.hc] = total
         qsum = rowsum(gp[:, : sizes.hc].astype(F32))
         vsum = rowsum(total[:, sizes.hc :].astype(F32))
         both = jnp.concatenate([qsum, vsum], axis=1)
-        row = dims.base[at] + dims.rows_of[at]["qv"]
+        row = dims.base[at] + dims.rows_of[at].qv
         if 2 * sizes.hc == model:
             r.vw[0, pl.ds(row + c, 1), :] = both
         else:
@@ -904,7 +1166,7 @@
             r.vw[0, row : row + 1, :] = jnp.concatenate([left, right], axis=1)
 
     def projection_grad(at, part):
-        sizes, keep, gp = layers[at], kept[at], (r.dp0, r.dp1)[at]
+        sizes, keep, gp = layers[at], kept[at], lay[at].dp
         begin, end = part * model, (part + 1) * model
         for y_at in range(SIDE):
             rows = slice(y_at * half_lanes, (y_at + 1) * half_lanes)
@@ -922,231 +1184,281 @@
             store_grad_rows(at, y_at, value, slice(begin, end))
 
     def back_hidden(at):
-        gp = (r.dp0, r.dp1)[at]
+        gp = lay[at].dp
         width = gp.shape[1]
         return mm(gp[...], wa[at][:, :width], 1, 1)
 
     grad = r.cin[...].reshape(tok, model).astype(F32)
     dz2 = back_two(1, grad)
     weight_grad(1, 1, kept[1].g, r.eo)
-    reduce_a(8)
+    reduce_0(8)
     back_up(1)
     weight_grad(1, 0, kept[1].g, kept[1].hb)
-    reduce_a(7)
+    reduce_0(7)
     wait_branch = exchange(back_in(1))
-    reduce_b(8)
     dz1, grad_ctx = back_one(1, dz2 + wait_branch())
-    reduce_b(7)
-    reduce_c(8)
+    reduce_1(8)
     attention_back(1, grad_ctx)
     send_dkv(1)
-    reduce_c(7)
-    reduce_end(8)
+    reduce_1(7)
+    reduce_2(8)
     take_dkv(1)
     projection_grad(1, 0)
-    reduce_a(6)
+    reduce_0(6)
     wait_branch = exchange(back_hidden(1))
-    reduce_end(7)
-    reduce_b(6)
+    reduce_2(7)
+    reduce_3(8)
     grad = dz1 + wait_branch()
     dz2 = back_two(0, grad)
     weight_grad(0, 1, kept[0].g, r.eo)
-    reduce_a(4)
-    reduce_a(5)
-    reduce_c(6)
+    reduce_0(4)
+    reduce_1(6)
+    reduce_0(5)
     back_up(0)
     weight_grad(0, 0, kept[0].g, kept[0].hb)
-    reduce_a(2)
-    reduce_a(3)
+    reduce_3(7)
+    reduce_4(8)
+    reduce_0(2)
     wait_branch = exchange(back_in(0))
-    reduce_b(4)
-    reduce_b(5)
-    reduce_end(6)
+    reduce_1(4)
+    reduce_2(6)
+    reduce_0(3)
     dz1, grad_ctx = back_one(0, dz2 + wait_branch())
-    reduce_b(2)
-    reduce_b(3)
-    reduce_c(4)
+    reduce_1(5)
+    reduce_3(6)
     attention_back(0, grad_ctx)
     send_dkv(0)
-    reduce_c(5)
+    reduce_4(7)
+    reduce_2(4)
+    reduce_1(2)
+    reduce_4(6)
+    reduce_3(4)
     take_dkv(0)
     projection_grad(0, 0)
-    reduce_a(0)
+    reduce_0(0)
     projection_grad(0, 1)
-    reduce_a(1)
+    reduce_2(5)
+    reduce_0(1)
     total_step(r.vw, r.vl, 0, r.ws, r.wr)
     wait_branch = exchange(back_hidden(0))
-    reduce_c(2)
-    reduce_end(4)
+    reduce_1(3)
+    reduce_4(4)
+    reduce_3(5)
+    reduce_2(2)
     grad = dz1 + wait_branch()
     r.gblk[...] = grad.astype(BF).reshape(r.gblk.shape)
     collect(r.gblk, r.gland, r.zs, r.zr)
-    reduce_b(0)
-    reduce_b(1)
-    reduce_c(3)
-    reduce_end(5)
     total_add(r.vw, r.vl, 0, r.ws, r.wr)
     total_step(r.vw, r.vl, 1, r.ws, r.wr)
-    reduce_end(2)
-    reduce_end(3)
+    reduce_1(0)
+    reduce_4(5)
+    reduce_3(2)
+    reduce_2(3)
     total_add(r.vw, r.vl, 1, r.ws, r.wr)
     total_step(r.vw, r.vl, 2, r.ws, r.wr)
-    reduce_c(0)
+    reduce_1(1)
+    reduce_4(2)
+    reduce_3(3)
+    reduce_2(0)
     total_add(r.vw, r.vl, 2, r.ws, r.wr)
     total_step(r.vw, r.vl, 3, r.ws, r.wr)
-    reduce_c(1)
+    for i in (8, 7, 6, 4, 5):
+        reduce_out(i)
+    reduce_4(3)
+    reduce_3(0)
+    reduce_2(1)
     total_add(r.vw, r.vl, 3, r.ws, r.wr)
     total_step(r.vw, r.vl, 4, r.ws, r.wr)
-    for i in (8, 7, 6, 4, 5, 2, 3):
-        reduce_out(i)
+    reduce_out(2)
+    reduce_4(0)
+    reduce_3(1)
+    reduce_out(3)
     total_add(r.vw, r.vl, 4, r.ws, r.wr)
-    r.dvec[...] = r.vw[5]
+    r.dvec[...] = unpack_vectors(r.vw[5])
+    store(r.dvec, outs.dvec)
     collect_done(r.oblk, r.oland, r.ys, r.yr)
-    r.out[...] = r.oland[...]
-    reduce_end(0)
-    reduce_end(1)
+    store(r.oland, outs.out)
+    reduce_4(1)
     collect_done(r.gblk, r.gland, r.zs, r.zr)
-    r.gh[...] = r.gland[...].astype(F32)
+    store(r.gland, outs.gh)
     reduce_out(0)
     reduce_out(1)
-    for copy in sent:
-        copy.wait_send()
-
-
-def fused_call(hid, cot, vec, shards, dims):
+    wait_sent()
+    for copy in stored:
+        copy.wait()
+
+
+def fused_call(hid, cot, lengths, params, dims):
     model, tok, seq = dims.model, dims.tok, dims.seq
     block = (4, tok // 4, model)
     vmem = pltpu.VMEM
     dma = pltpu.SemaphoreType.DMA
-    names = ["hid", "cot", "vec", "pa0", "pf0", "pa1", "pf1"]
-    inputs = [hid, cot, vec] + list(shards)
-    outs = {
-        "out": jax.ShapeDtypeStruct(hid.shape, BF),
-        "gh": jax.ShapeDtypeStruct(hid.shape, F32),
-        "da0": jax.ShapeDtypeStruct(shards[0].shape, F32),
-        "df0": jax.ShapeDtypeStruct(shards[1].shape, F32),
-        "da1": jax.ShapeDtypeStruct(shards[2].shape, F32),
-        "df1": jax.ShapeDtypeStruct(shards[3].shape, F32),
-        "dvec": jax.ShapeDtypeStruct(vec.shape, F32),
-    }
-    rows_a = 2 * shards[0].shape[1]
+    rows_in = params[0][0].shape[0]
+    shape = jax.ShapeDtypeStruct
+    given = dict(hid=hid, cot=cot, len=lengths, lay=[])
+    outs = dict(out=shape(hid.shape, BF), gh=shape(hid.shape, BF), lay=[], dvec=shape((1, dims.lanes), F32))
+    for (ai, ao, fi, fo, sh, ga), sizes in zip(params, dims.layers):
+        given["lay"].append(dict(pai=ai, pao=ao, pfi=fi, pfo=fo, psh=sh, pga=ga))
+        outs["lay"].append(
+            dict(
+                da=shape((2, rows_in, sizes.wide), F32),
+                df=shape((2, 2, sizes.nr, model // 4), F32),
+            )
+        )
+    as_scratch = lambda tree: jax.tree.map(lambda v: vmem(v.shape, v.dtype), tree)
+    held, made = as_scratch(given), as_scratch({key: outs[key] for key in ("lay", "dvec")})
+    vec = (dims.vec_rows, model)
+    rows_a = 2 * rows_in
     count_a = sum(chunk[0] == "A" for chunk in dims.chunks)
     count_f = len(dims.chunks) - count_a
-    shape_a, shape_f = (rows_a, model), (dims.rows, model // 2)
+    half = model // 2
     n = len(dims.chunks)
-    scratch = {
-        "xin": vmem(block, BF),
-        "cin": vmem(block, BF),
-        "oblk": vmem(block, BF),
-        "gblk": vmem(block, BF),
-        "oland": vmem(hid.shape, BF),
-        "gland": vmem(hid.shape, BF),
-        "vw": vmem((6,) + vec.shape, F32),
-        "vl": vmem((5,) + vec.shape, F32),
-        "xs": vmem((2, tok, model), BF),
-        "xr": vmem((2, tok, model), BF),
-        "eo": vmem((tok, model), BF),
-        "raa": vmem((count_a, 2, 2) + shape_a, BF),
-        "rba": vmem((count_a, 2, 4) + shape_a, BF),
-        "rca": vmem((count_a, 3) + shape_a, BF),
-        "raf": vmem((count_f, 2, 2) + shape_f, BF),
-        "rbf": vmem((count_f, 2, 4) + shape_f, BF),
-        "rcf": vmem((count_f, 3) + shape_f, BF),
-        "fsa": vmem((count_a, rows_a // 2, model), F32),
-        "fra": vmem((count_a, rows_a // 2, model), F32),
-        "frf": vmem((count_f,) + shape_f, F32),
-    }
-    for at, sizes in enumerate(dims.layers):
-        scratch |= {
-            f"ar{at}": vmem((rows_a // 2, sizes.wide), F32),
-            f"fr{at}": vmem((2, sizes.nr, model // 2), BF),
-            f"ga{at}": vmem((SIDE, DEPTH, SIDE, rows_a, sizes.wide), BF),
-            f"wa{at}": vmem((model, sizes.wide), BF),
-            f"w{at}": vmem((2, DEPTH, SIDE, sizes.nr, model), BF),
-            f"dw{at}": vmem((2, DEPTH, SIDE, sizes.nr, model), BF),
-            f"xb{at}": vmem((tok, model), BF),
-            f"q{at}": vmem((tok, sizes.hc), BF),
-            f"kv{at}": vmem((2, tok, 2 * sizes.hc), BF),
-            f"a{at}": vmem((sizes.heads, tok, seq), BF),
-            f"ctx{at}": vmem((tok, sizes.wide - sizes.start), BF),
-            f"n1{at}": vmem((tok, model), F32),
-            f"s1{at}": vmem((tok, 1), F32),
-            f"hb{at}": vmem((tok, model), BF),
-            f"g{at}": vmem((tok, sizes.nc), BF),
-            f"gp{at}": vmem((tok, sizes.nc), BF),
-            f"n2{at}": vmem((tok, model), F32),
-            f"s2{at}": vmem((tok, 1), F32),
-            f"dkv{at}": vmem((2, tok, 2 * sizes.hc), BF),
-            f"dkr{at}": vmem((tok, 2 * sizes.hc), BF),
-            f"dp{at}": vmem((tok, sizes.wide if sizes.pad else sizes.start), BF),
-        }
-    scratch |= {name: dma((n, 7)) for name in ("gs", "gr", "ss", "sr")}
-    scratch |= {name: dma((n,)) for name in ("fs", "fr")}
-    scratch |= {name: dma((5,)) for name in ("vs", "vr", "ws", "wr")}
-    scratch |= {name: dma((4,)) for name in ("hs", "hr", "cs", "cr", "ys", "yr", "zs", "zr")}
-    scratch |= {name: dma((4,)) for name in ("is_", "ir", "os", "ks", "kr")}
-    scratch |= {name: dma((2,)) for name in ("es", "er")}
-    names = names + list(outs) + list(scratch)
-    whole = pl.BlockSpec(memory_space=pltpu.VMEM)
-    return pl.pallas_call(
-        functools.partial(fused_kernel, dims, names),
-        out_shape=list(outs.values()),
+    scratch = dict(
+        xin=vmem(block, BF),
+        cin=vmem(block, BF),
+        oblk=vmem(block, BF),
+        gblk=vmem(block, BF),
+        oland=vmem(hid.shape, BF),
+        gland=vmem(hid.shape, BF),
+        vw=vmem((6,) + vec, F32),
+        vl=vmem((5,) + vec, F32),
+        xs=vmem((2, tok, model), BF),
+        xr=vmem((2, tok, model), BF),
+        eo=vmem((tok, model), BF),
+        fsa=vmem((count_a, rows_in, model), F32),
+        fra=vmem((count_a, rows_in, model), F32),
+        fsf=vmem((count_f, dims.rows, half // 2), F32),
+        frf=vmem((count_f, dims.rows, half // 2), F32),
+        hot=vmem((dims.lanes, model), BF),
+        gs=dma((n, 20)),
+        gr=dma((n, 20)),
+        ss=dma((n, 20)),
+        sr=dma((n, 20)),
+        fs=dma((n,)),
+        fr=dma((n,)),
+        vs=dma((5,)),
+        vr=dma((5,)),
+        ws=dma((5,)),
+        wr=dma((5,)),
+        hs=dma((4,)),
+        hr=dma((4,)),
+        cs=dma((4,)),
+        cr=dma((4,)),
+        ys=dma((4,)),
+        yr=dma((4,)),
+        zs=dma((4,)),
+        zr=dma((4,)),
+        is_=dma((4,)),
+        ir=dma((4,)),
+        os=dma((4,)),
+        ks=dma((4,)),
+        kr=dma((4,)),
+        es=dma((2,)),
+        er=dma((2,)),
+        ins=dma((16,)),
+        outs=dma((10,)),
+        red=[],
+        lay=[],
+    )
+    for count, rows, wide, pair in (
+        (count_a, rows_a - 32, model, (2, 4, 16, model)),
+        (count_f, dims.rows - 32, half, (4, 16, model)),
+    ):
+        line = pair[:-3] + (1, 16, model)
+        scratch["red"].append(
+            dict(
+                ad=vmem((count, 2, 2, rows, wide), BF),
+                an=vmem((count, 2, 4, rows, wide), BF),
+                az=vmem((count, 4, 1, rows, wide), BF),
+                by=vmem((count, 4, 2, 16, wide), BF),
+                bz=vmem((count, 4, 1, 2, 16, wide), BF),
+                bx=vmem((count, 1, 16, wide), BF),
+                cx=vmem((count,) + pair, BF),
+                cz=vmem((count, 4) + line, BF),
+                cy=vmem((count, 1, 16, wide), BF),
+            )
+        )
+    for sizes in dims.layers:
+        scratch["lay"].append(
+            dict(
+                ar=vmem((rows_in, sizes.wide), F32),
+                asend=vmem((rows_in, sizes.wide), F32),
+                fr=vmem((2, sizes.nr, model // 4), BF),
+                fsend=vmem((2, sizes.nr, model // 4), BF),
+                ga=vmem((SIDE, DEPTH, SIDE, rows_a, sizes.wide), BF),
+                wa=vmem((model, sizes.wide), BF),
+                w=vmem((2, DEPTH, SIDE, sizes.nr, model), BF),
+                dw=vmem((2, DEPTH, SIDE, sizes.nr, model), BF),
+                xb=vmem((tok, model), BF),
+                q=vmem((tok, sizes.hc), BF),
+                kv=vmem((2, tok, 2 * sizes.hc), BF),
+                a=vmem((sizes.heads, tok, seq), BF),
+                ctx=vmem((tok, sizes.wide - sizes.start), BF),
+                n1=vmem((tok, model), F32),
+                s1=vmem((tok, 1), F32),
+                hb=vmem((tok, model), BF),
+                g=vmem((tok, sizes.nc), BF),
+                gp=vmem((tok, sizes.nc), BF),
+                n2=vmem((tok, model), F32),
+                s2=vmem((tok, 1), F32),
+                dkv=vmem((2, tok, 2 * sizes.hc), BF),
+                dkr=vmem((tok, 2 * sizes.hc), BF),
+                dp=vmem((tok, sizes.wide if sizes.pad else sizes.start), BF),
+            )
+        )
+    inputs, outputs = jax.tree.leaves(given), jax.tree.leaves(outs)
+    whole = pl.BlockSpec(memory_space=pl.ANY)
+    local = (scratch, held, made)
+    values = pl.pallas_call(
+        functools.partial(fused_kernel, dims, jax.tree.structure((given, outs) + local)),
+        out_shape=outputs,
         in_specs=[whole] * len(inputs),
-        out_specs=[whole] * len(outs),
-        scratch_shapes=list(scratch.values()),
+        out_specs=[whole] * len(outputs),
+        scratch_shapes=jax.tree.leaves(local),
         compiler_params=pltpu.CompilerParams(
             collective_id=0, has_side_effects=True, vmem_limit_bytes=dims.vmem
         ),
         name="layers",
     )(*inputs)
-
-
-def pack_layer(attn_in, attn_out, ffn_in, ffn_out, core):
-    rows, heads_width = attn_in.shape[0], attn_in.shape[1] // 3
-    first = attn_in.reshape(rows, 3, 2, heads_width // 2).transpose(2, 0, 1, 3)
-    first = first.reshape(2, rows, 3 * heads_width // 2)
-    second = attn_out.T.reshape(rows, 2, heads_width // 2).transpose(1, 0, 2)
-    attn = jnp.concatenate([first, second], axis=2).astype(F32)
-    both = jnp.stack([ffn_in.T, ffn_out])
-    both = both.reshape(2, 2, both.shape[1] // 2, both.shape[2]).transpose(1, 0, 2, 3)
-    blank = jnp.zeros_like(both)
-    left, right = jnp.where(core == 0, both, blank), jnp.where(core == 0, blank, both)
-    return attn, jnp.concatenate([left, right], axis=3)
-
-
-def unpack_layer(attn, ffn, core):
-    rows, half = attn.shape[1], attn.shape[2] // 4
-    grad_in = attn[:, :, : 3 * half].reshape(2, rows, 3, half).transpose(1, 2, 0, 3)
-    grad_out = attn[:, :, 3 * half :].transpose(0, 2, 1).reshape(2 * half, rows)
-    lanes = ffn.shape[3] // 2
-    own = jnp.where(core == 0, ffn[..., :lanes], ffn[..., lanes:])
-    own = own.transpose(1, 0, 2, 3).reshape(2, 2 * ffn.shape[2], lanes)
-    return grad_in.reshape(rows, 6 * half), grad_out, own[0].T, own[1]
-
-
-def pack_vectors(shifts, gains, sizes, model, device):
-    total = 4 * sizes.hc + 4 * model + 2 * sizes.nc
-    flat = jnp.zeros((total,), F32)
-    flat = lax.dynamic_update_slice_in_dim(flat, shifts.astype(F32), device * shifts.shape[0], 0)
-    query, value, rest = flat[: 2 * sizes.hc], flat[2 * sizes.hc : 4 * sizes.hc], flat[4 * sizes.hc :]
-    both = jnp.concatenate([query.reshape(2, sizes.hc), value.reshape(2, sizes.hc)], axis=1)
-    up = rest[2 * model : 2 * model + 2 * sizes.nc].reshape(8, 2, sizes.nr).transpose(1, 0, 2)
-    scale = jnp.zeros((2 * model,), F32)
-    scale = lax.dynamic_update_slice_in_dim(scale, gains.astype(F32), device * gains.shape[0], 0)
-    return [both.reshape(-1), rest[: 2 * model], up.reshape(-1), rest[2 * model + 2 * sizes.nc :], scale]
-
-
-def unpack_vectors(flat, sizes, model, device, shift_len, gain_len):
-    both = flat[: 4 * sizes.hc].reshape(2, 2, sizes.hc).transpose(1, 0, 2).reshape(-1)
-    rest = flat[4 * sizes.hc :]
-    up = rest[2 * model : 2 * model + 2 * sizes.nc].reshape(2, 8, sizes.nr).transpose(1, 0, 2)
-    after = rest[2 * model + 2 * sizes.nc :]
-    shifts = jnp.concatenate([both, rest[: 2 * model], up.reshape(-1), after[: 2 * model]])
-    gains = after[2 * model :]
-    return (
-        lax.dynamic_slice_in_dim(shifts, device * shift_len, shift_len),
-        lax.dynamic_slice_in_dim(gains, device * gain_len, gain_len),
-    )
+    return jax.tree.unflatten(jax.tree.structure(outs), values)
+
+
+def finish_kernel(dims, tree, *refs):
+    given, (out, gh, *results) = jax.tree.unflatten(tree, refs)
+    r = named(given)
+    out[...] = r.out[...]
+    gh[...] = r.gh[...].astype(F32)
+    begin = 0
+    for at, sizes in enumerate(dims.layers):
+        attn, ffn = r.lay[at].da, r.lay[at].df
+        to_ai, to_ao, to_fi, to_fo, to_sh, to_ga = results[6 * at : 6 * at + 6]
+        for p in range(3):
+            for h in range(2):
+                to = (2 * p + h) * sizes.hc
+                to_ai[:, to : to + sizes.hc] = attn[h, :, p * sizes.hc : (p + 1) * sizes.hc]
+        for h in range(2):
+            to_ao[:, h * sizes.hc : (h + 1) * sizes.hc] = attn[h, :, 3 * sizes.hc :]
+        down = ffn[:, 1].reshape(2 * sizes.nr, ffn.shape[3])
+        to_fo[...] = down.T if dims.turned[at] else down
+        to_fi[...] = ffn[:, 0].reshape(2 * sizes.nr, ffn.shape[3]).T
+        for ref in (to_sh, to_ga):
+            ref[...] = r.dvec[0, begin : begin + ref.shape[0]]
+            begin += ref.shape[0]
+
+
+def finish_call(given, params, dims):
+    leaves, tree = jax.tree.flatten(given)
+    outs = [jax.ShapeDtypeStruct(given["out"].shape, d) for d in (BF, F32)]
+    outs += [jax.ShapeDtypeStruct(p.shape, F32) for shards in params for p in shards]
+    whole = pl.BlockSpec(memory_space=pltpu.VMEM)
+    return pl.pallas_call(
+        functools.partial(finish_kernel, dims, jax.tree.structure((given, outs))),
+        out_shape=outs,
+        in_specs=[whole] * len(leaves),
+        out_specs=[whole] * len(outs),
+        compiler_params=pltpu.CompilerParams(vmem_limit_bytes=dims.vmem),
+        name="finish",
+    )(*leaves)
 
 
 def make_dims(hidden_in, teacher, student):
@@ -1164,6 +1476,9 @@
     for chunk in chunks:
         slot.append(counts[chunk[0]])
         counts[chunk[0]] += 1
+    group = model // (SIDE * SIDE * DEPTH * SIDE)
+    shift_groups = [p[4].shape[0] // group for p in (teacher, student)]
+    gain_groups = [p[5].shape[0] // group for p in (teacher, student)]
     rows_of, base, at = [], [], 0
     for sizes in layers:
         found, count = vec_rows(model, sizes)
@@ -1178,46 +1493,31 @@
         chunks=chunks,
         slot=slot,
         rows=rows,
+        unit_rows={"A": 2 * teacher[0].shape[0], "F": rows},
         rows_of=rows_of,
         base=base,
         length_row=at,
         vec_rows=(at + 8) // 8 * 8,
+        turned=[p[3].shape[0] > p[3].shape[1] for p in (teacher, student)],
+        group=group,
+        lanes=(sum(shift_groups + gain_groups) * group + 4 + 127) // 128 * 128,
+        shift_groups=shift_groups,
+        gain_groups=gain_groups,
         vmem=63 * 2**20,
     )
 
 
-def fast_body(
-    hidden_in,
-    cotangent,
-    lengths,
-    *params,
-):
-    teacher, student = params[:6], params[6:]
-    dims = make_dims(hidden_in, teacher, student)
-    model = dims.model
-    dp, mp = lax.axis_index("dp"), lax.axis_index("mp")
-    core = lax.rem(dp, SIDE)
-    device = dp * DEPTH * SIDE + mp
-    pieces = []
-    shards = []
-    for sizes, p in zip(dims.layers, (teacher, student)):
-        shards += list(pack_layer(*p[:4], core))
-        pieces += pack_vectors(p[4], p[5], sizes, model, device)
-    spans = jnp.zeros((dims.vec_rows * model - sum(p.shape[0] for p in pieces),), F32)
-    own = jnp.where(mp == 0, lengths.astype(F32), jnp.zeros_like(lengths, F32))
-    spans = lax.dynamic_update_slice_in_dim(spans, own, dp * lengths.shape[0], 0)
-    vec = jnp.concatenate(pieces + [spans]).reshape(dims.vec_rows, model)
-    out, grad_hidden, da0, df0, da1, df1, dvec = fused_call(hidden_in, cotangent, vec, shards, dims)
+def fast_body(hidden_in, cotangent, lengths, *shards):
+    params = (shards[:6], shards[6:])
+    dims = make_dims(hidden_in, *params)
+    turn = lambda shards, turned: (shards[0], shards[1].T, shards[2], shards[3].T if turned else shards[3])
+    params = [turn(p, turned) + p[4:] for p, turned in zip(params, dims.turned)]
+    values = fused_call(hidden_in, cotangent, lengths, params, dims)
+    out, grad_hidden, *grads = finish_call(values, params, dims)
     results = [out, grad_hidden]
-    flat = dvec.reshape(-1)
-    for at, (sizes, p, attn, ffn) in enumerate(
-        zip(dims.layers, (teacher, student), (da0, da1), (df0, df1))
-    ):
-        results += list(unpack_layer(attn, ffn, core))
-        begin = dims.base[at] * model
-        results += list(
-            unpack_vectors(flat[begin:], sizes, model, device, p[4].shape[0], p[5].shape[0])
-        )
+    for at, turned in enumerate(dims.turned):
+        own = tuple(grads[6 * at : 6 * at + 6])
+        results += turn(own, turned) + own[4:]
     return tuple(results)
 
 

time: 277 us -> 225 us (0.81)
  Pallas kernels: 246 us -> 223 us
  local copies, waits for them, and re-layouts: 20.4 us -> 0 us
  other arithmetic: 9.21 us -> 0 us
    pallas_call x1 -> x2, Pallas kernels: 246 us -> 223 us  [the longest x1 220 us: fused_call(): pl.pallas_call(functools.partial(fused_kernel, dims, jax.tree.structure((...]
    reshape x34 -> x0, local copies, waits for them, and re-layouts: 7.74 us -> none  [the longest x2 1.65 us: unpack_layer(): return (grad_in.reshape(rows, 6 * half), grad_out, own[0].T, own[1])]
    slice x21 -> x0, local copies, waits for them, and re-layouts: 5.81 us -> none  [the longest x4 1.56 us: unpack_vectors(): gains = after[2 * model:]]
    dynamic_update_slice x5 -> x0, other arithmetic: 3.87 us -> none  [the longest x2 1.56 us: pack_vectors(): lax.dynamic_update_slice_in_dim(scale, gains.astype(F32), device * gains....]
    concatenate x6 -> x0, other arithmetic: 3.29 us -> none  [the longest x2 1.89 us: pack_layer(): return (attn, jnp.concatenate([left, right], axis=3))]
where the time goes in v2:
time: 225 us; the launch traced here: 224 us
  Pallas kernels  223 us (99%)
    pallas_call x1, Pallas kernels, fused_call(): pl.pallas_call(functools.partial(fused_kernel, dims, jax.tree.structure((...  220 us

profile of v2, /device:TPU:0, one launch (start us, length us, event | category | flops | bytes accessed | tf_op | source)
XLA Modules:
  0.0 223.9 jit_solution(14941799150869121710)
XLA Ops:
  0.7 220.0 %layers.1 = (f32[1,512]{1,0:T(1,128)}, bf16[2,64,768]{2,1,0:T(8,128)(2,1)}, f32[2,24,1536]{2,1,0:T(8,128)}, f32[2,2,192,192]{3,2,1,0:T(8,128)}, f32[2,24,768]{2,...) custom-call(bf16[2,64,768]{2,1,0:T(8,128)(2,1)} %refs_0_.1, bf16[2,64,768]{2,1,0:T(8,128)(2,1)} %refs_1_.1, ...), custom_call_target="tpu_custom_call" | custom-call | tf_op jit(solution)/shard_map/layers/pallas_call | solution.py:1412
  220.7 3.0 %finish.1 = (bf16[2,64,768]{2,1,0:T(8,128)(2,1)}, f32[2,64,768]{2,1,0:T(8,128)}, f32[24,2304]{1,0:T(8,128)}, f32[24,768]{1,0:T(8,128)}, f32[192,384]{1,0:T(8,128...) custom-call(f32[1,512]{1,0:T(1,128)} %get-tuple-element.35.refs_0_, ...), custom_call_target="tpu_custom_call" | custom-call | tf_op jit(solution)/shard_map/finish/pallas_call | solution.py:1454

commit v3 on v2

--- a/solution.py
+++ b/solution.py
@@ -301,7 +301,7 @@
     return scale * (grad - jnp.mean(grad, axis=-1, keepdims=True) - normed * along)
 
 
-def layer_sizes(model, heads_width, hidden):
+def layer_sizes(model, heads_width, hidden, pair):
     half = heads_width // 2
     start = 3 * half // 128 * 128
     return types.SimpleNamespace(
@@ -312,6 +312,10 @@
         pad=3 * half - start,
         nr=hidden // 16,
         nc=hidden // 2,
+        nl=hidden // 4 if pair else hidden // 2,
+        pair=pair,
+        sides=2 if pair else 1,
+        zs=2 if pair else DEPTH,
         zb=model * 8 // hidden,
     )
 
@@ -461,6 +465,10 @@
     def view(i, grads, band, z_slice, x_at, y_at):
         kind, layer, which, part = chunks[i]
         full = dims.unit_rows[kind]
+        if kind == "P":
+            ref = lay[layer].dw if grads else lay[layer].w
+            lanes = pl.ds(pl.multiple_of(y_at * half_lanes, 128), half_lanes)
+            return ref.at[which, z_slice, x_at, :, lanes]
         begin, count = {"a": (0, full - 32), "b": (full - 32, 16), "c": (full - 16, 16)}[band]
         if kind == "A":
             ref = lay[layer].ga
@@ -540,6 +548,30 @@
     def gather_wait(i, k, piece):
         arrived(piece, r.gr.at[i, k], r.gs.at[i, k])
 
+    z_own, z_other = z // 2, 1 - z // 2
+
+    def pair_view(i, grads, z_slice, x_at, y_at):
+        return view(i, grads, None, z_slice, x_at, y_at)
+
+    def pair_0(i):
+        gather_push(i, 0, pair_view(i, False, one(z_own), x, y), zfar)
+
+    def pair_1(i):
+        gather_wait(i, 0, pair_view(i, False, one(z_other), x, y))
+        own = pair_view(i, False, both, x, y)
+        gather_push(i, 1, own, xn)
+        gather_push(i, 2, own, yn)
+
+    def pair_2(i):
+        gather_wait(i, 1, pair_view(i, False, both, 1 - x, y))
+        gather_wait(i, 2, pair_view(i, False, both, x, 1 - y))
+        gather_push(i, 3, pair_view(i, False, one(0), x, 1 - y), xn)
+        gather_push(i, 4, pair_view(i, False, one(1), 1 - x, y), yn)
+
+    def pair_3(i):
+        gather_wait(i, 3, pair_view(i, False, one(0), 1 - x, 1 - y))
+        gather_wait(i, 4, pair_view(i, False, one(1), 1 - x, 1 - y))
+
     def gather_0(i):
         gather_push(i, 16, view(i, False, "b", one(z), x, y), xn)
         gather_push(i, 17, view(i, False, "c", one(z), x, y), yn)
@@ -579,10 +611,16 @@
         gather_wait(i, 18, view(i, False, "b", every, both, 1 - y))
         gather_wait(i, 19, view(i, False, "c", every, 1 - x, None))
 
+    band_stages = (gather_0, gather_1, gather_2, gather_3, gather_4)
+    pair_stages = (pair_0, pair_1, pair_2, pair_3)
+
     def pump(step):
-        for lag, stage in enumerate((gather_0, gather_1, gather_2, gather_3, gather_4)):
-            if 0 <= step - lag < len(chunks):
-                stage(step - lag)
+        for lag in range(5):
+            i = step - lag
+            if 0 <= i < len(chunks):
+                stages = pair_stages if chunks[i][0] == "P" else band_stages
+                if lag < len(stages):
+                    stages[lag](i)
 
     def add_into(ref, extra):
         total = ref[...].astype(F32)
@@ -591,7 +629,7 @@
         ref[...] = total.astype(BF)
 
     def slots(i, name):
-        return getattr(r.red[chunks[i][0] == "F"], name).at[dims.slot[i]]
+        return getattr(r.red["AFP".index(chunks[i][0])], name).at[dims.slot[i]]
 
     def reduce_push(i, k, src, dst, dev):
         push(src, dst, r.ss.at[i, k], r.sr.at[i, k], dev)
@@ -635,14 +673,14 @@
     def reduce_sems(i, base):
         return sems(r.ss, r.sr, i, base)
 
-    def reduce_0(i):
+    def band_reduce_0(i):
         over = slots(i, "ad")
         reduce_push(i, 14, view(i, True, "a", first, 1 - x, 1 - y), over.at[0], xn)
         reduce_push(i, 15, view(i, True, "a", second, 1 - x, 1 - y), over.at[1], yn)
         reduce_push(i, 18, view(i, True, "b", every, both, 1 - y), slots(i, "by"), yn)
         reduce_push(i, 19, view(i, True, "c", every, 1 - x, None), slots(i, "cx"), xn)
 
-    def reduce_1(i):
+    def band_reduce_1(i):
         a, b, c_part = parts_of(i, True)
         over, beside = slots(i, "ad"), slots(i, "an")
         reduce_wait(i, 14, over.at[0])
@@ -658,7 +696,7 @@
         add_into(view(i, True, "c", every, x, None), [slots(i, "cx")])
         line_reduce_send(c_part, slots(i, "cz"), *reduce_sems(i, 8))
 
-    def reduce_2(i):
+    def band_reduce_2(i):
         a, b, c_part = parts_of(i, True)
         beside = slots(i, "an")
         reduce_wait(i, 12, beside.at[0])
@@ -668,7 +706,7 @@
         line_reduce_relay(b, slots(i, "bz"), *reduce_sems(i, 4))
         line_reduce_relay(c_part, slots(i, "cz"), *reduce_sems(i, 8))
 
-    def reduce_3(i):
+    def band_reduce_3(i):
         a, b, c_part = parts_of(i, True)
         line_reduce_end(b, slots(i, "bz"), *reduce_sems(i, 4))
         reduce_push(i, 16, view(i, True, "b", one(z), 1 - x, y), slots(i, "bx"), xn)
@@ -676,9 +714,7 @@
         reduce_push(i, 17, view(i, True, "c", one(z), x, 1 - y), slots(i, "cy"), yn)
         line_reduce_relay(a, slots(i, "az"), *reduce_sems(i, 0))
 
-    def reduce_4(i):
-        kind, layer, which, part = chunks[i]
-        at = dims.slot[i]
+    def band_reduce_4(i):
         line_reduce_end(parts_of(i, True)[0], slots(i, "az"), *reduce_sems(i, 0))
         reduce_wait(i, 16, slots(i, "bx"))
         reduce_wait(i, 17, slots(i, "cy"))
@@ -690,34 +726,71 @@
             ],
             axis=0,
         )
+        reduce_store(i, total)
+
+    def pair_reduce_0(i):
+        over = slots(i, "ad")
+        reduce_push(i, 3, pair_view(i, True, one(0), 1 - x, 1 - y), over.at[0], xn)
+        reduce_push(i, 4, pair_view(i, True, one(1), 1 - x, 1 - y), over.at[1], yn)
+
+    def pair_reduce_1(i):
+        over, beside = slots(i, "ad"), slots(i, "an")
+        reduce_wait(i, 3, over.at[0])
+        add_into(pair_view(i, True, one(0), x, 1 - y), [over.at[0]])
+        reduce_push(i, 2, pair_view(i, True, both, x, 1 - y), beside.at[1], yn)
+        reduce_wait(i, 4, over.at[1])
+        add_into(pair_view(i, True, one(1), 1 - x, y), [over.at[1]])
+        reduce_push(i, 1, pair_view(i, True, both, 1 - x, y), beside.at[0], xn)
+
+    def pair_reduce_2(i):
+        beside = slots(i, "an")
+        reduce_wait(i, 1, beside.at[0])
+        reduce_wait(i, 2, beside.at[1])
+        add_into(pair_view(i, True, both, x, y), [beside.at[0], beside.at[1]])
+        reduce_push(i, 0, pair_view(i, True, one(z_other), x, y), slots(i, "az"), zfar)
+
+    def pair_reduce_3(i):
+        far = slots(i, "az")
+        reduce_wait(i, 0, far)
+        own = pair_view(i, True, one(z_own), x, y)
+        reduce_store(i, (own[...].astype(F32) + far[...].astype(F32))[0])
+
+    def reduce_store(i, total):
+        kind, layer, which, part = chunks[i]
+        send, land = slots(i, "fsend"), slots(i, "fland")
         if kind == "A":
-            out = lay[layer].da
             rows = total.shape[0] // 2
-            out[c, :, part * model : (part + 1) * model] = jnp.where(c == 0, total[:rows], total[rows:])
-            r.fsa[at] = jnp.where(c == 0, total[rows:], total[:rows])
-            push(r.fsa.at[at], r.fra.at[at], r.fs.at[i], r.fr.at[i], sib)
+            cols = slice(part * model, (part + 1) * model)
+            lay[layer].da[c, :, cols] = jnp.where(c == 0, total[:rows], total[rows:])
+            send[...] = jnp.where(c == 0, total[rows:], total[:rows])
         else:
-            out = lay[layer].df
-            rows = pl.ds(part * dims.rows, dims.rows)
-            lanes = total.shape[1] // 2
-            out[c, which, rows, :] = jnp.where(c == 0, total[:, :lanes], total[:, lanes:])
-            r.fsf[at] = jnp.where(c == 0, total[:, lanes:], total[:, :lanes])
-            push(r.fsf.at[at], r.frf.at[at], r.fs.at[i], r.fr.at[i], sib)
+            full = dims.unit_rows[kind]
+            rows, lanes = pl.ds(part * full, full), total.shape[1] // 2
+            lay[layer].df[c, which, rows, :] = jnp.where(c == 0, total[:, :lanes], total[:, lanes:])
+            send[...] = jnp.where(c == 0, total[:, lanes:], total[:, :lanes])
+        push(send, land, r.fs.at[i], r.fr.at[i], sib)
 
     def reduce_out(i):
         kind, layer, which, part = chunks[i]
-        at = dims.slot[i]
+        land = slots(i, "fland")
+        arrived(land, r.fr.at[i], r.fs.at[i])
         if kind == "A":
-            arrived(r.fra.at[at], r.fr.at[i], r.fs.at[i])
-            lay[layer].da[1 - c, :, part * model : (part + 1) * model] = r.fra[at]
-            if part == layers[layer].wide // model - 1:
+            lay[layer].da[1 - c, :, part * model : (part + 1) * model] = land[...]
+            if part == 0:
                 store(lay[layer].da, outs.lay[layer].da)
         else:
-            arrived(r.frf.at[at], r.fr.at[i], r.fs.at[i])
-            rows = pl.ds(part * dims.rows, dims.rows)
-            lay[layer].df[1 - c, which, rows, :] = r.frf[at]
-            if part == layers[layer].nr // dims.rows - 1:
+            full = dims.unit_rows[kind]
+            lay[layer].df[1 - c, which, pl.ds(part * full, full), :] = land[...]
+            if part == layers[layer].nr // full - 1:
                 store(lay[layer].df.at[:, which], outs.lay[layer].df.at[:, which])
+
+    band_reduces = (band_reduce_0, band_reduce_1, band_reduce_2, band_reduce_3, band_reduce_4)
+    pair_reduces = (pair_reduce_0, pair_reduce_1, pair_reduce_2, pair_reduce_3)
+
+    def reduce(i, stage):
+        stages = pair_reduces if chunks[i][0] == "P" else band_reduces
+        if stage < len(stages):
+            stages[stage](i)
 
     def total_step(work, land, step, sends, recvs):
         dev = (sib, xn, yn, zn, zfar)[step]
@@ -739,6 +812,39 @@
         def finish():
             copy.wait()
             return r.xs[slot].astype(F32) + r.xr[slot].astype(F32)
+
+        return finish
+
+    quarter = tok // 2
+    own_rows = pl.ds(pl.multiple_of(c * quarter, 16), quarter)
+    other_rows = pl.ds(pl.multiple_of((1 - c) * quarter, 16), quarter)
+
+    def share(ref, k):
+        piece = ref.at[half, own_rows]
+        push(piece, piece, r.ps.at[k, 0], r.pr.at[k, 0], zn)
+
+        def finish():
+            got = ref.at[1 - half, own_rows]
+            arrived(got, r.pr.at[k, 0], r.ps.at[k, 0])
+            push(got, got, r.ps.at[k, 1], r.pr.at[k, 1], sib)
+            arrived(ref.at[1 - half, other_rows], r.pr.at[k, 1], r.ps.at[k, 1])
+
+        return finish
+
+    def fold(make, k):
+        r.px[...] = make(1 - half).astype(BF)
+        push(r.px.at[other_rows], r.prx.at[k], r.ps.at[k, 2], r.pr.at[k, 2], sib)
+        own = exchange(make(half))
+        arrived(r.prx.at[k], r.pr.at[k, 2], r.ps.at[k, 2])
+        r.pz[k] = (r.px[own_rows, :].astype(F32) + r.prx[k].astype(F32)).astype(BF)
+        push(r.pz.at[k], r.pzr.at[k, c], r.ps.at[k, 3], r.pr.at[k, 3], zn)
+
+        def finish():
+            got = r.pzr.at[k, c]
+            arrived(got, r.pr.at[k, 3], r.ps.at[k, 3])
+            push(got, got, r.ps.at[k, 4], r.pr.at[k, 4], sib)
+            arrived(r.pzr.at[k, 1 - c], r.pr.at[k, 4], r.ps.at[k, 4])
+            return own() + r.pzr[k].reshape(tok, model).astype(F32)
 
         return finish
 
@@ -754,6 +860,9 @@
             qv = jnp.where(c == 0, both[:, : 2 * sizes.hc], both[:, 2 * sizes.hc :])
         span = sizes.nc // model
         b1 = [r.vw[5, pl.ds(base + rows.b1 + c * span + s, 1), :] for s in range(span)]
+        if sizes.pair:
+            cut = 2 * sizes.nr
+            b1 = [jnp.concatenate([jnp.where(half == 0, v[:, :cut], v[:, cut:]) for v in b1], axis=1)]
         found = types.SimpleNamespace(bq=qv[:, : sizes.hc], bv=qv[:, sizes.hc :], b1=b1)
         for name, row in vars(rows).items():
             if not hasattr(found, name):
@@ -834,7 +943,8 @@
             da = mm(dc, v, 1, 1)
             inner = jnp.sum(a * da, axis=1, keepdims=True)
             ds = (0.125 * a * (da - inner)).astype(BF)
-            gp[:, h * HEAD : (h + 1) * HEAD] = mm(ds, k, 1, 0).astype(BF)
+            at_q = 2 * sizes.hc + h * HEAD
+            gp[:, at_q : at_q + HEAD] = mm(ds, k, 1, 0).astype(BF)
             dk = mm(ds, q, 0, 0).astype(BF).reshape(2, tok, HEAD)
             dv = mm(low, dc, 0, 0).astype(BF).reshape(2, tok, HEAD)
             dkv[:, :, h * HEAD : (h + 1) * HEAD] = dk
@@ -845,32 +955,34 @@
         w = weights[at][which, b * sizes.zb : (b + 1) * sizes.zb]
         return w.reshape(model, model)
 
-    def up(at, vecs):
+    def up(at, side):
         sizes, keep = layers[at], kept[at]
-        for b in range(sizes.nc // model):
+        for b in range(sizes.nl // model):
             cols = slice(b * model, (b + 1) * model)
-            u = mm(keep.hb[...], block(at, 0, b), 1, 1) + vecs.b1[b]
+            u = mm(keep.hb[side], block(at, 0, b), 1, 1) + vecs[at].b1[b]
             phi = 0.5 * (1.0 + lax.erf(u * 0.7071067811865476))
-            keep.g[:, cols] = (u * phi).astype(BF)
+            keep.g[side, :, cols] = (u * phi).astype(BF)
             density = jnp.exp(u * u * -0.5) * 0.3989422804014327
-            keep.gp[:, cols] = (phi + u * density).astype(BF)
-
-    def down(at):
+            keep.gp[side, :, cols] = (phi + u * density).astype(BF)
+
+    def times_block(at, which, side):
         sizes, keep = layers[at], kept[at]
         total = None
-        for b in range(sizes.nc // model):
-            term = mm(keep.g[:, b * model : (b + 1) * model], block(at, 1, b), 1, 0)
+        for b in range(sizes.nl // model):
+            term = mm(keep.g[side, :, b * model : (b + 1) * model], block(at, which, b), 1, 0)
             total = term if total is None else total + term
         return total
 
-    def weight_grad(at, which, left, right):
-        sizes = layers[at]
-        dw = lay[at].dw
+    def weight_grad(at, which, right):
+        sizes, keep = layers[at], kept[at]
         span = model // 2
         zb = sizes.zb // 2
-        for b in range(sizes.nc // span):
-            value = mm(left[:, b * span : (b + 1) * span], right[...], 0, 0).astype(BF)
-            dw[which, b * zb : (b + 1) * zb] = value.reshape(zb, 2, sizes.nr, model)
+        rows = sizes.sides * tok
+        wide = right[...].reshape(rows, model)
+        for b in range(sizes.nl // span):
+            left = keep.g[:, :, b * span : (b + 1) * span].reshape(rows, span)
+            value = mm(left, wide, 0, 0).astype(BF)
+            keep.dw[which, b * zb : (b + 1) * zb] = value.reshape(zb, 2, sizes.nr, model)
 
 
     def pack_a(at):
@@ -880,7 +992,7 @@
         halves = []
         for h in range(2):
             own = slice(h * sizes.hc, (h + 1) * sizes.hc)
-            pieces = [rows_in[:, p * width : (p + 1) * width][:, own] for p in range(3)]
+            pieces = [rows_in[:, p * width : (p + 1) * width][:, own] for p in (1, 2, 0)]
             halves.append(jnp.concatenate(pieces + [rows_out[:, own]], axis=1))
         send = lay[at].asend
         send[...] = jnp.where(c == 0, halves[1], halves[0])
@@ -917,7 +1029,7 @@
         for which in range(2):
             other = land[which].astype(F32)
             pair = [jnp.where(c == 0, own[which], other), jnp.where(c == 0, other, own[which])]
-            weights[at][which, z, x, :, lanes] = jnp.concatenate(pair, axis=1).astype(BF)
+            weights[at][which, z_own if layers[at].pair else z, x, :, lanes] = jnp.concatenate(pair, axis=1).astype(BF)
 
     group = dims.group
     per_row = model // group
@@ -1029,16 +1141,16 @@
             order_rows(at, part)
         if sizes.wide == model:
             p = mm(hidden_low, wa[at][...], 1, 0)
-            keep.q[...] = (p[:, : sizes.hc] + vecs[at].bq).astype(BF)
-            keep.kv[half, :, : sizes.hc] = p[:, sizes.hc : 2 * sizes.hc].astype(BF)
-            keep.kv[half, :, sizes.hc :] = (p[:, 2 * sizes.hc : 3 * sizes.hc] + vecs[at].bv).astype(BF)
+            kv, q = p[:, : 2 * sizes.hc], p[:, 2 * sizes.hc : 3 * sizes.hc]
         elif parts == (0,):
-            p = mm(hidden_low, wa[at][:, : 2 * sizes.hc], 1, 0)
-            keep.q[...] = (p[:, : sizes.hc] + vecs[at].bq).astype(BF)
-            keep.kv[half, :, : sizes.hc] = p[:, sizes.hc :].astype(BF)
+            kv, q = mm(hidden_low, wa[at][:, : 2 * sizes.hc], 1, 0), None
         else:
-            p = mm(hidden_low, wa[at][:, 2 * sizes.hc : 3 * sizes.hc], 1, 0)
-            keep.kv[half, :, sizes.hc :] = (p + vecs[at].bv).astype(BF)
+            kv, q = None, mm(hidden_low, wa[at][:, 2 * sizes.hc : 3 * sizes.hc], 1, 0)
+        if q is not None:
+            keep.q[...] = (q + vecs[at].bq).astype(BF)
+        if kv is not None:
+            keep.kv[half, :, : sizes.hc] = kv[:, : sizes.hc].astype(BF)
+            keep.kv[half, :, sizes.hc :] = (kv[:, sizes.hc :] + vecs[at].bv).astype(BF)
 
     def attend_out(at):
         return mm(kept[at].ctx[...], wa[at][:, layers[at].start :], 1, 1)
@@ -1049,7 +1161,7 @@
         keep.n1[...] = normed
         keep.s1[...] = scale
         result = normed * v.g1 + v.beta1
-        keep.hb[...] = result.astype(BF)
+        keep.hb[half if layers[at].pair else 0] = result.astype(BF)
         return result
 
     def norm_two(at, base, branch):
@@ -1064,34 +1176,35 @@
         lay[1].dp[...] = jnp.zeros_like(lay[1].dp)
     kept[0].xb[...] = r.xin[...].reshape(tok, model)
     project(0, kept[0].xb[...], (0,))
+    send_kv(0)
     pump(5)
     project(0, kept[0].xb[...], (1,))
-    send_kv(0)
     spread(r.cot, r.cin, r.cs, r.cr)
-    pump(6)
-    pump(7)
     wait_kv(0)
     attention(0)
     wait_branch = exchange(attend_out(0))
+    pump(6)
+    normed = norm_one(0, kept[0].xb[...].astype(F32), wait_branch())
+    wait_share = share(kept[0].hb, 0)
+    up(0, half)
+    pump(7)
+    wait_share()
+    up(0, 1 - half)
+    wait_branch = fold(lambda side: times_block(0, 1, side), 0)
+    spread_done(r.cot, r.cin, r.cs, r.cr, r.os.at[2], r.os.at[3])
     pump(8)
-    normed = norm_one(0, kept[0].xb[...].astype(F32), wait_branch())
-    up(0, vecs[0])
-    spread_done(r.cot, r.cin, r.cs, r.cr, r.os.at[2], r.os.at[3])
-    pump(9)
-    wait_branch = exchange(down(0))
-    pump(10)
     middle = norm_two(0, normed, wait_branch())
     kept[1].xb[...] = middle.astype(BF)
     project(1, kept[1].xb[...], (0,))
     send_kv(1)
-    pump(11)
+    pump(9)
     wait_kv(1)
     attention(1)
     wait_branch = exchange(attend_out(1))
     normed = norm_one(1, middle, wait_branch())
-    up(1, vecs[1])
-    pump(12)
-    wait_branch = exchange(down(1))
+    up(1, 0)
+    pump(10)
+    wait_branch = exchange(times_block(1, 1, 0))
     final = norm_two(1, normed, wait_branch())
     r.oblk[...] = final.astype(BF).reshape(r.oblk.shape)
     collect(r.oblk, r.oland, r.ys, r.yr)
@@ -1110,28 +1223,35 @@
         put_vec(at, "g2", rowsum(grad * n2))
         put_vec(at, "beta2", rowsum(grad))
         dz2 = normalize_back(grad * v.g2, n2, keep.s2[...])
-        r.eo[...] = dz2.astype(BF)
-        put_vec(at, "b2", rowsum(r.eo[...].astype(F32)))
+        low_dz2 = dz2.astype(BF)
+        keep.eo[half if layers[at].pair else 0] = low_dz2
+        put_vec(at, "b2", rowsum(low_dz2.astype(F32)))
         return dz2
 
     def back_up(at):
         sizes, keep = layers[at], kept[at]
         base = dims.base[at] + dims.rows_of[at].b1
-        span = sizes.nc // model
-        for b in range(span):
+        span, sums = sizes.nc // model, []
+        for b in range(sizes.nl // model):
             cols = slice(b * model, (b + 1) * model)
-            dg = mm(r.eo[...], block(at, 1, b), 1, 1)
-            du = (dg * keep.gp[:, cols].astype(F32)).astype(BF)
-            keep.g[:, cols] = du
-            r.vw[0, pl.ds(base + c * span + b, 1), :] = rowsum(du.astype(F32))
-
-    def back_in(at):
-        sizes, keep = layers[at], kept[at]
-        total = None
-        for b in range(sizes.nc // model):
-            term = mm(keep.g[:, b * model : (b + 1) * model], block(at, 0, b), 1, 0)
-            total = term if total is None else total + term
-        return total
+            total = None
+            for side in range(sizes.sides):
+                dg = mm(keep.eo[side], block(at, 1, b), 1, 1)
+                du = (dg * keep.gp[side, :, cols].astype(F32)).astype(BF)
+                keep.g[side, :, cols] = du
+                term = rowsum(du.astype(F32))
+                total = term if total is None else total + term
+            sums.append(total)
+        if sizes.pair:
+            cut = 2 * sizes.nr
+            blank = jnp.zeros((1, cut), F32)
+            pieces = [sums[0][:, b * cut : (b + 1) * cut] for b in range(span)]
+            sums = [
+                jnp.concatenate([jnp.where(half == 0, p, blank), jnp.where(half == 0, blank, p)], axis=1)
+                for p in pieces
+            ]
+        for b, total in enumerate(sums):
+            r.vw[0, pl.ds(base + c * span + b, 1), :] = total
 
     def back_one(at, grad):
         keep, v = kept[at], vecs[at]
@@ -1153,8 +1273,8 @@
         dkv, land, gp = lay[at].dkv, lay[at].dkr, lay[at].dp
         arrived(land, r.kr.at[2 + at], r.ks.at[2 + at])
         total = (dkv[half].astype(F32) + land[...].astype(F32)).astype(BF)
-        gp[:, sizes.hc : 3 * sizes.hc] = total
-        qsum = rowsum(gp[:, : sizes.hc].astype(F32))
+        gp[:, : 2 * sizes.hc] = total
+        qsum = rowsum(gp[:, 2 * sizes.hc : 3 * sizes.hc].astype(F32))
         vsum = rowsum(total[:, sizes.hc :].astype(F32))
         both = jnp.concatenate([qsum, vsum], axis=1)
         row = dims.base[at] + dims.rows_of[at].qv
@@ -1190,99 +1310,88 @@
 
     grad = r.cin[...].reshape(tok, model).astype(F32)
     dz2 = back_two(1, grad)
-    weight_grad(1, 1, kept[1].g, r.eo)
-    reduce_0(8)
+    weight_grad(1, 1, kept[1].eo)
+    reduce(6, 0)
     back_up(1)
-    weight_grad(1, 0, kept[1].g, kept[1].hb)
-    reduce_0(7)
-    wait_branch = exchange(back_in(1))
+    weight_grad(1, 0, kept[1].hb)
+    reduce(5, 0)
+    wait_branch = exchange(times_block(1, 0, 0))
     dz1, grad_ctx = back_one(1, dz2 + wait_branch())
-    reduce_1(8)
+    reduce(6, 1)
     attention_back(1, grad_ctx)
     send_dkv(1)
-    reduce_1(7)
-    reduce_2(8)
+    reduce(5, 1)
+    reduce(6, 2)
     take_dkv(1)
     projection_grad(1, 0)
-    reduce_0(6)
+    reduce(4, 0)
     wait_branch = exchange(back_hidden(1))
-    reduce_2(7)
-    reduce_3(8)
+    reduce(5, 2)
+    reduce(6, 3)
     grad = dz1 + wait_branch()
     dz2 = back_two(0, grad)
-    weight_grad(0, 1, kept[0].g, r.eo)
-    reduce_0(4)
-    reduce_1(6)
-    reduce_0(5)
+    wait_share = share(kept[0].eo, 1)
+    reduce(4, 1)
+    reduce(5, 3)
+    reduce(6, 4)
+    wait_share()
+    weight_grad(0, 1, kept[0].eo)
+    reduce(3, 0)
     back_up(0)
-    weight_grad(0, 0, kept[0].g, kept[0].hb)
-    reduce_3(7)
-    reduce_4(8)
-    reduce_0(2)
-    wait_branch = exchange(back_in(0))
-    reduce_1(4)
-    reduce_2(6)
-    reduce_0(3)
+    wait_branch = fold(lambda side: times_block(0, 0, side), 1)
+    weight_grad(0, 0, kept[0].hb)
+    reduce(2, 0)
+    reduce(4, 2)
     dz1, grad_ctx = back_one(0, dz2 + wait_branch())
-    reduce_1(5)
-    reduce_3(6)
+    reduce(3, 1)
+    reduce(5, 4)
     attention_back(0, grad_ctx)
     send_dkv(0)
-    reduce_4(7)
-    reduce_2(4)
-    reduce_1(2)
-    reduce_4(6)
-    reduce_3(4)
+    projection_grad(0, 1)
+    reduce(1, 0)
+    reduce(2, 1)
+    reduce(4, 3)
+    reduce(3, 2)
     take_dkv(0)
     projection_grad(0, 0)
-    reduce_0(0)
-    projection_grad(0, 1)
-    reduce_2(5)
-    reduce_0(1)
+    reduce(0, 0)
     total_step(r.vw, r.vl, 0, r.ws, r.wr)
     wait_branch = exchange(back_hidden(0))
-    reduce_1(3)
-    reduce_4(4)
-    reduce_3(5)
-    reduce_2(2)
+    reduce(1, 1)
+    reduce(2, 2)
+    reduce(4, 4)
+    reduce(3, 3)
     grad = dz1 + wait_branch()
     r.gblk[...] = grad.astype(BF).reshape(r.gblk.shape)
     collect(r.gblk, r.gland, r.zs, r.zr)
     total_add(r.vw, r.vl, 0, r.ws, r.wr)
     total_step(r.vw, r.vl, 1, r.ws, r.wr)
-    reduce_1(0)
-    reduce_4(5)
-    reduce_3(2)
-    reduce_2(3)
+    reduce(0, 1)
+    reduce(1, 2)
+    reduce(2, 3)
     total_add(r.vw, r.vl, 1, r.ws, r.wr)
     total_step(r.vw, r.vl, 2, r.ws, r.wr)
-    reduce_1(1)
-    reduce_4(2)
-    reduce_3(3)
-    reduce_2(0)
+    for i in (6, 5, 4, 3):
+        reduce_out(i)
     total_add(r.vw, r.vl, 2, r.ws, r.wr)
     total_step(r.vw, r.vl, 3, r.ws, r.wr)
-    for i in (8, 7, 6, 4, 5):
-        reduce_out(i)
-    reduce_4(3)
-    reduce_3(0)
-    reduce_2(1)
+    reduce(0, 2)
+    reduce(1, 3)
     total_add(r.vw, r.vl, 3, r.ws, r.wr)
     total_step(r.vw, r.vl, 4, r.ws, r.wr)
     reduce_out(2)
-    reduce_4(0)
-    reduce_3(1)
-    reduce_out(3)
+    reduce(0, 3)
+    reduce(1, 4)
     total_add(r.vw, r.vl, 4, r.ws, r.wr)
     r.dvec[...] = unpack_vectors(r.vw[5])
     store(r.dvec, outs.dvec)
     collect_done(r.oblk, r.oland, r.ys, r.yr)
     store(r.oland, outs.out)
-    reduce_4(1)
+    reduce_out(1)
+    reduce(0, 4)
     collect_done(r.gblk, r.gland, r.zs, r.zr)
     store(r.gland, outs.gh)
     reduce_out(0)
-    reduce_out(1)
     wait_sent()
     for copy in stored:
         copy.wait()
@@ -1309,8 +1418,7 @@
     held, made = as_scratch(given), as_scratch({key: outs[key] for key in ("lay", "dvec")})
     vec = (dims.vec_rows, model)
     rows_a = 2 * rows_in
-    count_a = sum(chunk[0] == "A" for chunk in dims.chunks)
-    count_f = len(dims.chunks) - count_a
+    counts = [sum(chunk[0] == kind for chunk in dims.chunks) for kind in "AFP"]
     half = model // 2
     n = len(dims.chunks)
     scratch = dict(
@@ -1325,10 +1433,12 @@
         xs=vmem((2, tok, model), BF),
         xr=vmem((2, tok, model), BF),
         eo=vmem((tok, model), BF),
-        fsa=vmem((count_a, rows_in, model), F32),
-        fra=vmem((count_a, rows_in, model), F32),
-        fsf=vmem((count_f, dims.rows, half // 2), F32),
-        frf=vmem((count_f, dims.rows, half // 2), F32),
+        px=vmem((tok, model), BF),
+        prx=vmem((2, tok // 2, model), BF),
+        pz=vmem((2, tok // 2, model), BF),
+        pzr=vmem((2, 2, tok // 2, model), BF),
+        ps=dma((2, 5)),
+        pr=dma((2, 5)),
         hot=vmem((dims.lanes, model), BF),
         gs=dma((n, 20)),
         gr=dma((n, 20)),
@@ -1360,9 +1470,10 @@
         red=[],
         lay=[],
     )
-    for count, rows, wide, pair in (
-        (count_a, rows_a - 32, model, (2, 4, 16, model)),
-        (count_f, dims.rows - 32, half, (4, 16, model)),
+    rows_f, rows_p = dims.unit_rows["F"], dims.unit_rows["P"]
+    for count, rows, wide, pair, shard in (
+        (counts[0], rows_a - 32, model, (2, 4, 16, model), (rows_in, model)),
+        (counts[1], rows_f - 32, half, (4, 16, model), (rows_f, half // 2)),
     ):
         line = pair[:-3] + (1, 16, model)
         scratch["red"].append(
@@ -1376,8 +1487,19 @@
                 cx=vmem((count,) + pair, BF),
                 cz=vmem((count, 4) + line, BF),
                 cy=vmem((count, 1, 16, wide), BF),
+                fsend=vmem((count,) + shard, F32),
+                fland=vmem((count,) + shard, F32),
             )
         )
+    scratch["red"].append(
+        dict(
+            ad=vmem((counts[2], 2, 1, rows_p, half), BF),
+            an=vmem((counts[2], 2, 2, rows_p, half), BF),
+            az=vmem((counts[2], 1, rows_p, half), BF),
+            fsend=vmem((counts[2], rows_p, half // 2), F32),
+            fland=vmem((counts[2], rows_p, half // 2), F32),
+        )
+    )
     for sizes in dims.layers:
         scratch["lay"].append(
             dict(
@@ -1387,8 +1509,8 @@
                 fsend=vmem((2, sizes.nr, model // 4), BF),
                 ga=vmem((SIDE, DEPTH, SIDE, rows_a, sizes.wide), BF),
                 wa=vmem((model, sizes.wide), BF),
-                w=vmem((2, DEPTH, SIDE, sizes.nr, model), BF),
-                dw=vmem((2, DEPTH, SIDE, sizes.nr, model), BF),
+                w=vmem((2, sizes.zs, SIDE, sizes.nr, model), BF),
+                dw=vmem((2, sizes.zs, SIDE, sizes.nr, model), BF),
                 xb=vmem((tok, model), BF),
                 q=vmem((tok, sizes.hc), BF),
                 kv=vmem((2, tok, 2 * sizes.hc), BF),
@@ -1396,9 +1518,10 @@
                 ctx=vmem((tok, sizes.wide - sizes.start), BF),
                 n1=vmem((tok, model), F32),
                 s1=vmem((tok, 1), F32),
-                hb=vmem((tok, model), BF),
-                g=vmem((tok, sizes.nc), BF),
-                gp=vmem((tok, sizes.nc), BF),
+                hb=vmem((sizes.sides, tok, model), BF),
+                eo=vmem((sizes.sides, tok, model), BF),
+                g=vmem((sizes.sides, tok, sizes.nl), BF),
+                gp=vmem((sizes.sides, tok, sizes.nl), BF),
                 n2=vmem((tok, model), F32),
                 s2=vmem((tok, 1), F32),
                 dkv=vmem((2, tok, 2 * sizes.hc), BF),
@@ -1434,7 +1557,7 @@
         to_ai, to_ao, to_fi, to_fo, to_sh, to_ga = results[6 * at : 6 * at + 6]
         for p in range(3):
             for h in range(2):
-                to = (2 * p + h) * sizes.hc
+                to = (2 * ((p + 1) % 3) + h) * sizes.hc
                 to_ai[:, to : to + sizes.hc] = attn[h, :, p * sizes.hc : (p + 1) * sizes.hc]
         for h in range(2):
             to_ao[:, h * sizes.hc : (h + 1) * sizes.hc] = attn[h, :, 3 * sizes.hc :]
@@ -1464,15 +1587,17 @@
 def make_dims(hidden_in, teacher, student):
     model = hidden_in.shape[2]
     layers = [
-        layer_sizes(model, p[0].shape[1] // 3, p[2].shape[1] * DEPTH * SIDE) for p in (teacher, student)
+        layer_sizes(model, p[0].shape[1] // 3, p[2].shape[1] * DEPTH * SIDE, pair)
+        for p, pair in ((teacher, True), (student, False))
     ]
     rows = layers[1].nr
     chunks = []
     for at, sizes in enumerate(layers):
         chunks += [("A", at, 0, part) for part in range(sizes.wide // model)]
         for which in (0, 1):
-            chunks += [("F", at, which, part) for part in range(sizes.nr // rows)]
-    counts, slot = {"A": 0, "F": 0}, []
+            kind, count = ("P", 1) if sizes.pair else ("F", sizes.nr // rows)
+            chunks += [(kind, at, which, part) for part in range(count)]
+    counts, slot = {"A": 0, "F": 0, "P": 0}, []
     for chunk in chunks:
         slot.append(counts[chunk[0]])
         counts[chunk[0]] += 1
@@ -1493,7 +1618,7 @@
         chunks=chunks,
         slot=slot,
         rows=rows,
-        unit_rows={"A": 2 * teacher[0].shape[0], "F": rows},
+        unit_rows={"A": 2 * teacher[0].shape[0], "F": rows, "P": layers[0].nr},
         rows_of=rows_of,
         base=base,
         length_row=at,
@@ -1523,7 +1648,8 @@
 
 def body(axes, *args):
     rows, tokens, model = args[0].shape
-    fits = axes["dp"] == SIDE * SIDE and axes["mp"] == DEPTH * SIDE
+    pair_fits = args[3 + 2].shape[1] * 2 == model
+    fits = pair_fits and axes["dp"] == SIDE * SIDE and axes["mp"] == DEPTH * SIDE
     if fits and rows == 2 and tokens % 16 == 0 and model % 256 == 0:
         return fast_body(*args)
     return general_body(*args)

time: 225 us -> 210 us (0.933)
  Pallas kernels: 223 us -> 207 us
    pallas_call x1, Pallas kernels: 220 us -> 204 us  [fused_call(): pl.pallas_call(functools.partial(fused_kernel, dims, jax.tree.structure((...]
where the time goes in v3:
time: 210 us; the launch traced here: 208 us
  Pallas kernels  207 us (99%)
    pallas_call x1, Pallas kernels, fused_call(): pl.pallas_call(functools.partial(fused_kernel, dims, jax.tree.structure((...  204 us

profile of v3, /device:TPU:0, one launch (start us, length us, event | category | flops | bytes accessed | tf_op | source)
XLA Modules:
  0.0 207.8 jit_solution(3807849199558717852)
XLA Ops:
  0.7 203.9 %layers.1 = (f32[1,512]{1,0:T(1,128)}, bf16[2,64,768]{2,1,0:T(8,128)(2,1)}, f32[2,24,1536]{2,1,0:T(8,128)}, f32[2,2,192,192]{3,2,1,0:T(8,128)}, f32[2,24,768]{2,...) custom-call(bf16[2,64,768]{2,1,0:T(8,128)(2,1)} %refs_0_.1, bf16[2,64,768]{2,1,0:T(8,128)(2,1)} %refs_1_.1, ...), custom_call_target="tpu_custom_call" | custom-call | tf_op jit(solution)/shard_map/layers/pallas_call | solution.py:1535
  204.6 3.0 %finish.1 = (bf16[2,64,768]{2,1,0:T(8,128)(2,1)}, f32[2,64,768]{2,1,0:T(8,128)}, f32[24,2304]{1,0:T(8,128)}, f32[24,768]{1,0:T(8,128)}, f32[192,384]{1,0:T(8,128...) custom-call(f32[1,512]{1,0:T(1,128)} %get-tuple-element.35.refs_0_, ...), custom_call_target="tpu_custom_call" | custom-call | tf_op jit(solution)/shard_map/finish/pallas_call | solution.py:1577

commit v4 on v3

--- a/solution.py
+++ b/solution.py
@@ -309,6 +309,7 @@
         heads=half // HEAD,
         wide=4 * half,
         start=start,
+        qw=-(-half // 128) * 128,
         pad=3 * half - start,
         nr=hidden // 16,
         nc=hidden // 2,
@@ -414,7 +415,7 @@
             pl.when(local)(pltpu.make_async_copy(src.at[j], land.at[block], recvs.at[block]).start)
             pl.when(jnp.logical_not(local))(copy.start)
 
-    def spread_done(src, land, sends, recvs, on_chip_send, on_chip_recv):
+    def spread_turn(src, land, sends, recvs, on_chip_send, on_chip_recv):
         target = 2 * c + z // 2
         for j in range(2):
             local = (x == j) & (z == target)
@@ -427,11 +428,11 @@
             for block in range(4):
                 arrived(land.at[block], recvs.at[block], sends.at[0])
             whole.start()
-            whole.wait_send()
-
-        @pl.when(jnp.logical_not(mine))
-        def _():
-            whole.wait_recv()
+
+    def spread_end(land, on_chip_send, on_chip_recv):
+        whole = remote(land, land, on_chip_send, on_chip_recv, sib)
+        pl.when(mine)(whole.wait_send)
+        pl.when(jnp.logical_not(mine))(whole.wait_recv)
 
     def collect(src, land, sends, recvs):
         @pl.when(mine)
@@ -614,13 +615,9 @@
     band_stages = (gather_0, gather_1, gather_2, gather_3, gather_4)
     pair_stages = (pair_0, pair_1, pair_2, pair_3)
 
-    def pump(step):
-        for lag in range(5):
-            i = step - lag
-            if 0 <= i < len(chunks):
-                stages = pair_stages if chunks[i][0] == "P" else band_stages
-                if lag < len(stages):
-                    stages[lag](i)
+    def gather(i, stage):
+        stages = pair_stages if chunks[i][0] == "P" else band_stages
+        stages[stage](i)
 
     def add_into(ref, extra):
         total = ref[...].astype(F32)
@@ -819,34 +816,49 @@
     own_rows = pl.ds(pl.multiple_of(c * quarter, 16), quarter)
     other_rows = pl.ds(pl.multiple_of((1 - c) * quarter, 16), quarter)
 
-    def share(ref, k):
-        piece = ref.at[half, own_rows]
-        push(piece, piece, r.ps.at[k, 0], r.pr.at[k, 0], zn)
-
-        def finish():
-            got = ref.at[1 - half, own_rows]
+    class Share:
+        def __init__(self, ref, k):
+            blocks = len(ref.shape) == 4
+            self.own = pl.ds(2 * c, 2) if blocks else own_rows
+            self.other = pl.ds(2 - 2 * c, 2) if blocks else other_rows
+            self.ref, self.k = ref, k
+            piece = ref.at[half, self.own]
+            push(piece, piece, r.ps.at[k, 0], r.pr.at[k, 0], zn)
+
+        def turn(self):
+            got, k = self.ref.at[1 - half, self.own], self.k
             arrived(got, r.pr.at[k, 0], r.ps.at[k, 0])
             push(got, got, r.ps.at[k, 1], r.pr.at[k, 1], sib)
-            arrived(ref.at[1 - half, other_rows], r.pr.at[k, 1], r.ps.at[k, 1])
-
-        return finish
-
-    def fold(make, k):
-        r.px[...] = make(1 - half).astype(BF)
-        push(r.px.at[other_rows], r.prx.at[k], r.ps.at[k, 2], r.pr.at[k, 2], sib)
-        own = exchange(make(half))
-        arrived(r.prx.at[k], r.pr.at[k, 2], r.ps.at[k, 2])
-        r.pz[k] = (r.px[own_rows, :].astype(F32) + r.prx[k].astype(F32)).astype(BF)
-        push(r.pz.at[k], r.pzr.at[k, c], r.ps.at[k, 3], r.pr.at[k, 3], zn)
-
-        def finish():
+
+        def end(self):
+            k = self.k
+            arrived(self.ref.at[1 - half, self.other], r.pr.at[k, 1], r.ps.at[k, 1])
+
+    class Fold:
+        def __init__(self, make, k):
+            self.make, self.k = make, k
+            r.px[k] = make(1 - half, False).astype(BF)
+            push(r.px.at[k, other_rows], r.prx.at[k], r.ps.at[k, 2], r.pr.at[k, 2], sib)
+
+        def keep(self):
+            self.own = exchange(self.make(half, True))
+
+        def cross(self):
+            k = self.k
+            arrived(r.prx.at[k], r.pr.at[k, 2], r.ps.at[k, 2])
+            r.pz[k] = (r.px[k, own_rows, :].astype(F32) + r.prx[k].astype(F32)).astype(BF)
+            push(r.pz.at[k], r.pzr.at[k, c], r.ps.at[k, 3], r.pr.at[k, 3], zn)
+
+        def turn(self):
+            k = self.k
             got = r.pzr.at[k, c]
             arrived(got, r.pr.at[k, 3], r.ps.at[k, 3])
             push(got, got, r.ps.at[k, 4], r.pr.at[k, 4], sib)
+
+        def end(self):
+            k = self.k
             arrived(r.pzr.at[k, 1 - c], r.pr.at[k, 4], r.ps.at[k, 4])
-            return own() + r.pzr[k].reshape(tok, model).astype(F32)
-
-        return finish
+            return self.own() + r.pzr[k].reshape(tok, model).astype(F32)
 
     def vec_row(row):
         return r.vw[5, row : row + 1, :]
@@ -898,14 +910,6 @@
                 both = [value[begin : begin + rows], value[span + begin : span + begin + rows]]
                 blocks[y_at, z_at, x_at, :, cols] = jnp.concatenate(both, axis=0).astype(BF)
 
-    def send_kv(at):
-        kv = kept[at].kv
-        push(kv.at[half], kv.at[half], r.ks.at[at], r.kr.at[at], zn)
-
-    def wait_kv(at):
-        kv = kept[at].kv
-        arrived(kv.at[1 - half], r.kr.at[at], r.ks.at[at])
-
     def head_kv(at, h):
         sizes, kv = layers[at], kept[at].kv
         k = kv[:, :, h * HEAD : (h + 1) * HEAD].reshape(seq, HEAD)
@@ -932,7 +936,7 @@
 
     def attention_back(at, grad_ctx):
         sizes, keep = layers[at], kept[at]
-        dkv, gp = lay[at].dkv, lay[at].dp
+        dkv, dq = lay[at].dkv, lay[at].dq
         for h in range(sizes.heads):
             q = keep.q[:, h * HEAD : (h + 1) * HEAD]
             k, v = head_kv(at, h)
@@ -943,8 +947,7 @@
             da = mm(dc, v, 1, 1)
             inner = jnp.sum(a * da, axis=1, keepdims=True)
             ds = (0.125 * a * (da - inner)).astype(BF)
-            at_q = 2 * sizes.hc + h * HEAD
-            gp[:, at_q : at_q + HEAD] = mm(ds, k, 1, 0).astype(BF)
+            dq[:, h * HEAD : (h + 1) * HEAD] = mm(ds, k, 1, 0).astype(BF)
             dk = mm(ds, q, 0, 0).astype(BF).reshape(2, tok, HEAD)
             dv = mm(low, dc, 0, 0).astype(BF).reshape(2, tok, HEAD)
             dkv[:, :, h * HEAD : (h + 1) * HEAD] = dk
@@ -1101,56 +1104,22 @@
             total = term if total is None else total + term
         return rowsum(total)
 
-    for copy in fetched[:2]:
-        copy.wait()
-    own_a = pack_a(0)
-    fetched[2].wait()
-    spread(r.hid, r.xin, r.hs, r.hr)
-    for copy in fetched[3:5]:
-        copy.wait()
-    own_f = pack_f(0)
-    prepare_a(0, own_a)
-    pump(0)
-    prepare_f(0, own_f)
-    pump(1)
-    for copy in fetched[5:]:
-        copy.wait()
-    r.vw[0] = pack_vectors()
-    total_step(r.vw, r.vl, 0, r.vs, r.vr)
-    own_a, own_f = pack_a(1), pack_f(1)
-    total_add(r.vw, r.vl, 0, r.vs, r.vr)
-    total_step(r.vw, r.vl, 1, r.vs, r.vr)
-    prepare_a(1, own_a)
-    prepare_f(1, own_f)
-    total_add(r.vw, r.vl, 1, r.vs, r.vr)
-    total_step(r.vw, r.vl, 2, r.vs, r.vr)
-    pump(2)
-    spread_done(r.hid, r.xin, r.hs, r.hr, r.os.at[0], r.os.at[1])
-    total_add(r.vw, r.vl, 2, r.vs, r.vr)
-    total_step(r.vw, r.vl, 3, r.vs, r.vr)
-    pump(3)
-    total_add(r.vw, r.vl, 3, r.vs, r.vr)
-    total_step(r.vw, r.vl, 4, r.vs, r.vr)
-    pump(4)
-    total_add(r.vw, r.vl, 4, r.vs, r.vr)
-    vecs = [layer_vecs(0), layer_vecs(1)]
-
-    def project(at, hidden_low, parts):
+    vecs = []
+    block_shape = (4, tok // 4, model)
+
+    def tokens(at, side):
+        return kept[at].xb[side].reshape(tok, model)
+
+    def project_kv(at, side):
         sizes, keep = layers[at], kept[at]
-        for part in parts:
-            order_rows(at, part)
-        if sizes.wide == model:
-            p = mm(hidden_low, wa[at][...], 1, 0)
-            kv, q = p[:, : 2 * sizes.hc], p[:, 2 * sizes.hc : 3 * sizes.hc]
-        elif parts == (0,):
-            kv, q = mm(hidden_low, wa[at][:, : 2 * sizes.hc], 1, 0), None
-        else:
-            kv, q = None, mm(hidden_low, wa[at][:, 2 * sizes.hc : 3 * sizes.hc], 1, 0)
-        if q is not None:
-            keep.q[...] = (q + vecs[at].bq).astype(BF)
-        if kv is not None:
-            keep.kv[half, :, : sizes.hc] = kv[:, : sizes.hc].astype(BF)
-            keep.kv[half, :, sizes.hc :] = (kv[:, sizes.hc :] + vecs[at].bv).astype(BF)
+        kv = mm(tokens(at, side), wa[at][:, : 2 * sizes.hc], 1, 0)
+        keep.kv[side, :, : sizes.hc] = kv[:, : sizes.hc].astype(BF)
+        keep.kv[side, :, sizes.hc :] = (kv[:, sizes.hc :] + vecs[at].bv).astype(BF)
+
+    def project_q(at):
+        sizes, keep = layers[at], kept[at]
+        q = mm(tokens(at, half), wa[at][:, 2 * sizes.hc : 2 * sizes.hc + sizes.qw], 1, 0)
+        keep.q[...] = (q[:, : sizes.hc] + vecs[at].bq).astype(BF)
 
     def attend_out(at):
         return mm(kept[at].ctx[...], wa[at][:, layers[at].start :], 1, 1)
@@ -1173,39 +1142,112 @@
 
     if layers[1].pad:
         kept[1].ctx[...] = jnp.zeros_like(kept[1].ctx)
-        lay[1].dp[...] = jnp.zeros_like(lay[1].dp)
-    kept[0].xb[...] = r.xin[...].reshape(tok, model)
-    project(0, kept[0].xb[...], (0,))
-    send_kv(0)
-    pump(5)
-    project(0, kept[0].xb[...], (1,))
+        lay[1].dq[...] = jnp.zeros_like(lay[1].dq)
+    for copy in fetched[:2]:
+        copy.wait()
+    own_a0 = pack_a(0)
+    fetched[2].wait()
+    spread(r.hid, kept[0].xb.at[lax.rem(z // 2, 2)], r.hs, r.hr)
+    for copy in fetched[3:5]:
+        copy.wait()
+    own_f0 = pack_f(0)
+    prepare_f(0, own_f0)
+    gather(2, 0)
+    spread_turn(r.hid, kept[0].xb.at[half], r.hs, r.hr, r.os.at[0], r.os.at[1])
+    for copy in fetched[5:]:
+        copy.wait()
+    r.vw[0] = pack_vectors()
+    own_a1 = pack_a(1)
+    spread_end(kept[0].xb.at[half], r.os.at[0], r.os.at[1])
+    gather(3, 0)
+    prepare_a(0, own_a0)
+    share_hid = Share(kept[0].xb, 2)
+    total_step(r.vw, r.vl, 0, r.vs, r.vr)
+    gather(2, 1)
+    gather(0, 0)
+    total_add(r.vw, r.vl, 0, r.vs, r.vr)
+    gather(1, 0)
+    gather(2, 2)
+    total_step(r.vw, r.vl, 1, r.vs, r.vr)
+    gather(0, 1)
+    gather(3, 1)
+    total_add(r.vw, r.vl, 1, r.vs, r.vr)
+    own_f1 = pack_f(1)
+    prepare_f(1, own_f1)
+    gather(1, 1)
+    total_step(r.vw, r.vl, 2, r.vs, r.vr)
+    prepare_a(1, own_a1)
+    share_hid.turn()
+    gather(0, 2)
+    total_add(r.vw, r.vl, 2, r.vs, r.vr)
+    total_step(r.vw, r.vl, 3, r.vs, r.vr)
+    share_hid.end()
+    gather(4, 0)
+    gather(1, 2)
+    gather(6, 0)
+    gather(2, 3)
+    gather(0, 3)
+    total_add(r.vw, r.vl, 3, r.vs, r.vr)
+    total_step(r.vw, r.vl, 4, r.vs, r.vr)
+    gather(1, 3)
+    gather(6, 1)
+    total_add(r.vw, r.vl, 4, r.vs, r.vr)
+    vecs.extend([layer_vecs(0), layer_vecs(1)])
+    gather(0, 4)
+    gather(4, 1)
+    order_rows(0, 0)
+    project_kv(0, half)
+    gather(3, 2)
+    gather(6, 2)
+    project_kv(0, 1 - half)
+    gather(1, 4)
+    gather(5, 0)
+    order_rows(0, 1)
+    project_q(0)
+    attention(0)
+    branch = exchange(attend_out(0))
+    gather(4, 2)
+    branch = branch()
+    normed = norm_one(0, tokens(0, half).astype(F32), branch)
+    share_normed = Share(kept[0].hb, 0)
+    gather(3, 3)
+    gather(4, 3)
+    gather(6, 3)
     spread(r.cot, r.cin, r.cs, r.cr)
-    wait_kv(0)
-    attention(0)
-    wait_branch = exchange(attend_out(0))
-    pump(6)
-    normed = norm_one(0, kept[0].xb[...].astype(F32), wait_branch())
-    wait_share = share(kept[0].hb, 0)
+    gather(5, 1)
+    share_normed.turn()
     up(0, half)
-    pump(7)
-    wait_share()
+    share_normed.end()
     up(0, 1 - half)
-    wait_branch = fold(lambda side: times_block(0, 1, side), 0)
-    spread_done(r.cot, r.cin, r.cs, r.cr, r.os.at[2], r.os.at[3])
-    pump(8)
-    middle = norm_two(0, normed, wait_branch())
-    kept[1].xb[...] = middle.astype(BF)
-    project(1, kept[1].xb[...], (0,))
-    send_kv(1)
-    pump(9)
-    wait_kv(1)
+    down = Fold(lambda side, own: times_block(0, 1, side), 0)
+    down.keep()
+    down.cross()
+    gather(5, 2)
+    gather(4, 4)
+    down.turn()
+    branch = down.end()
+    middle = norm_two(0, normed, branch)
+    kept[1].xb[half] = middle.astype(BF).reshape(block_shape)
+    share_middle = Share(kept[1].xb, 3)
+    order_rows(1, 0)
+    project_kv(1, half)
+    project_q(1)
+    gather(5, 3)
+    gather(6, 4)
+    spread_turn(r.cot, r.cin, r.cs, r.cr, r.os.at[2], r.os.at[3])
+    share_middle.turn()
+    spread_end(r.cin, r.os.at[2], r.os.at[3])
+    share_middle.end()
+    project_kv(1, 1 - half)
     attention(1)
-    wait_branch = exchange(attend_out(1))
-    normed = norm_one(1, middle, wait_branch())
+    branch = exchange(attend_out(1))
+    gather(5, 4)
+    branch = branch()
+    normed = norm_one(1, middle, branch)
     up(1, 0)
-    pump(10)
-    wait_branch = exchange(times_block(1, 1, 0))
-    final = norm_two(1, normed, wait_branch())
+    branch = exchange(times_block(1, 1, 0))
+    branch = branch()
+    final = norm_two(1, normed, branch)
     r.oblk[...] = final.astype(BF).reshape(r.oblk.shape)
     collect(r.oblk, r.oland, r.ys, r.yr)
     wait_sent()
@@ -1264,18 +1306,10 @@
         grad_ctx = mm(r.eo[...], wa[at][:, layers[at].start :], 1, 0).astype(BF)
         return dz1, grad_ctx
 
-    def send_dkv(at):
-        dkv, land = lay[at].dkv, lay[at].dkr
-        push(dkv.at[1 - half], land, r.ks.at[2 + at], r.kr.at[2 + at], zn)
-
-    def take_dkv(at):
-        sizes = layers[at]
-        dkv, land, gp = lay[at].dkv, lay[at].dkr, lay[at].dp
-        arrived(land, r.kr.at[2 + at], r.ks.at[2 + at])
-        total = (dkv[half].astype(F32) + land[...].astype(F32)).astype(BF)
-        gp[:, : 2 * sizes.hc] = total
-        qsum = rowsum(gp[:, 2 * sizes.hc : 3 * sizes.hc].astype(F32))
-        vsum = rowsum(total[:, sizes.hc :].astype(F32))
+    def bias_sums(at):
+        sizes, dkv, dq = layers[at], lay[at].dkv, lay[at].dq
+        qsum = rowsum(dq[:, : sizes.hc].astype(F32))
+        vsum = rowsum(dkv[:, :, sizes.hc :].reshape(seq, sizes.hc).astype(F32))
         both = jnp.concatenate([qsum, vsum], axis=1)
         row = dims.base[at] + dims.rows_of[at].qv
         if 2 * sizes.hc == model:
@@ -1286,112 +1320,131 @@
             r.vw[0, row : row + 1, :] = jnp.concatenate([left, right], axis=1)
 
     def projection_grad(at, part):
-        sizes, keep, gp = layers[at], kept[at], lay[at].dp
+        sizes, keep = layers[at], kept[at]
         begin, end = part * model, (part + 1) * model
         for y_at in range(SIDE):
             rows = slice(y_at * half_lanes, (y_at + 1) * half_lanes)
             pieces = []
-            xb = keep.xb[:, rows]
-            split = min(end, sizes.start)
-            if begin < split:
-                pieces.append(mm(xb, gp[:, begin:split], 0, 0))
-            if end > sizes.start:
-                value = mm(r.eo[:, rows], keep.ctx[...], 0, 0)
+            if begin == 0:
+                every_token = keep.xb[:, :, :, rows].reshape(seq, half_lanes)
+                grads = keep.dkv[...].reshape(seq, 2 * sizes.hc)
+                pieces.append(mm(every_token, grads, 0, 0))
+            if end > 2 * sizes.hc:
+                own = keep.xb[half, :, :, rows].reshape(tok, half_lanes)
+                query = mm(own, keep.dq[...], 0, 0)
+                output = mm(r.eo[:, rows], keep.ctx[...], 0, 0)
                 if sizes.pad:
-                    value = value + mm(xb, gp[:, sizes.start : end], 0, 0)
-                pieces.append(value)
+                    apart = sizes.start - 2 * sizes.hc
+                    pieces += [query[:, :apart], query[:, apart:] + output]
+                else:
+                    pieces += [query, output]
             value = pieces[0] if len(pieces) == 1 else jnp.concatenate(pieces, axis=1)
             store_grad_rows(at, y_at, value, slice(begin, end))
 
-    def back_hidden(at):
-        gp = lay[at].dp
-        width = gp.shape[1]
-        return mm(gp[...], wa[at][:, :width], 1, 1)
+    def back_hidden(at, side, own):
+        sizes, keep = layers[at], kept[at]
+        total = mm(keep.dkv[side], wa[at][:, : 2 * sizes.hc], 1, 1)
+        if own:
+            begin = 2 * sizes.hc
+            total = total + mm(keep.dq[...], wa[at][:, begin : begin + keep.dq.shape[1]], 1, 1)
+        return total
 
     grad = r.cin[...].reshape(tok, model).astype(F32)
     dz2 = back_two(1, grad)
     weight_grad(1, 1, kept[1].eo)
     reduce(6, 0)
     back_up(1)
+    branch = exchange(times_block(1, 0, 0))
+    branch = branch()
+    dz1, grad_ctx = back_one(1, dz2 + branch)
+    attention_back(1, grad_ctx)
+    reduce(6, 1)
+    down = Fold(lambda side, own: back_hidden(1, side, own), 2)
+    down.keep()
+    down.cross()
+    projection_grad(1, 0)
+    bias_sums(1)
+    reduce(4, 0)
     weight_grad(1, 0, kept[1].hb)
+    down.turn()
     reduce(5, 0)
-    wait_branch = exchange(times_block(1, 0, 0))
-    dz1, grad_ctx = back_one(1, dz2 + wait_branch())
-    reduce(6, 1)
-    attention_back(1, grad_ctx)
-    send_dkv(1)
+    branch = down.end()
+    dz2 = back_two(0, dz1 + branch)
+    share_grad = Share(kept[0].eo, 1)
+    reduce(4, 1)
     reduce(5, 1)
-    reduce(6, 2)
-    take_dkv(1)
-    projection_grad(1, 0)
-    reduce(4, 0)
-    wait_branch = exchange(back_hidden(1))
-    reduce(5, 2)
-    reduce(6, 3)
-    grad = dz1 + wait_branch()
-    dz2 = back_two(0, grad)
-    wait_share = share(kept[0].eo, 1)
-    reduce(4, 1)
-    reduce(5, 3)
-    reduce(6, 4)
-    wait_share()
+    share_grad.turn()
+    share_grad.end()
     weight_grad(0, 1, kept[0].eo)
     reduce(3, 0)
     back_up(0)
-    wait_branch = fold(lambda side: times_block(0, 0, side), 1)
+    up_back = Fold(lambda side, own: times_block(0, 0, side), 1)
     weight_grad(0, 0, kept[0].hb)
     reduce(2, 0)
+    up_back.keep()
+    up_back.cross()
+    reduce(6, 2)
     reduce(4, 2)
-    dz1, grad_ctx = back_one(0, dz2 + wait_branch())
+    reduce(5, 2)
     reduce(3, 1)
-    reduce(5, 4)
+    up_back.turn()
+    collect_done(r.oblk, r.oland, r.ys, r.yr)
+    store(r.oland, outs.out)
+    branch = up_back.end()
+    reduce(2, 1)
+    dz1, grad_ctx = back_one(0, dz2 + branch)
     attention_back(0, grad_ctx)
-    send_dkv(0)
+    reduce(3, 2)
+    to_hidden = Fold(lambda side, own: back_hidden(0, side, own), 3)
     projection_grad(0, 1)
     reduce(1, 0)
-    reduce(2, 1)
+    to_hidden.keep()
+    to_hidden.cross()
+    reduce(5, 3)
+    reduce(2, 2)
     reduce(4, 3)
-    reduce(3, 2)
-    take_dkv(0)
     projection_grad(0, 0)
+    bias_sums(0)
     reduce(0, 0)
     total_step(r.vw, r.vl, 0, r.ws, r.wr)
-    wait_branch = exchange(back_hidden(0))
+    total_add(r.vw, r.vl, 0, r.ws, r.wr)
     reduce(1, 1)
-    reduce(2, 2)
-    reduce(4, 4)
-    reduce(3, 3)
-    grad = dz1 + wait_branch()
-    r.gblk[...] = grad.astype(BF).reshape(r.gblk.shape)
-    collect(r.gblk, r.gland, r.zs, r.zr)
-    total_add(r.vw, r.vl, 0, r.ws, r.wr)
     total_step(r.vw, r.vl, 1, r.ws, r.wr)
+    reduce(6, 3)
+    reduce(5, 4)
+    reduce(1, 2)
     reduce(0, 1)
-    reduce(1, 2)
-    reduce(2, 3)
     total_add(r.vw, r.vl, 1, r.ws, r.wr)
     total_step(r.vw, r.vl, 2, r.ws, r.wr)
-    for i in (6, 5, 4, 3):
-        reduce_out(i)
+    to_hidden.turn()
+    reduce(3, 3)
     total_add(r.vw, r.vl, 2, r.ws, r.wr)
+    reduce(4, 4)
+    reduce_out(3)
     total_step(r.vw, r.vl, 3, r.ws, r.wr)
+    branch = to_hidden.end()
+    reduce(6, 4)
+    reduce(2, 3)
+    reduce(1, 3)
     reduce(0, 2)
-    reduce(1, 3)
+    reduce_out(5)
     total_add(r.vw, r.vl, 3, r.ws, r.wr)
+    reduce(1, 4)
+    reduce(0, 3)
+    reduce_out(2)
     total_step(r.vw, r.vl, 4, r.ws, r.wr)
-    reduce_out(2)
-    reduce(0, 3)
-    reduce(1, 4)
+    reduce(0, 4)
+    reduce_out(1)
+    reduce_out(6)
+    reduce_out(4)
+    r.gblk[...] = (dz1 + branch).astype(BF).reshape(r.gblk.shape)
+    collect(r.gblk, r.gland, r.zs, r.zr)
+    reduce_out(0)
     total_add(r.vw, r.vl, 4, r.ws, r.wr)
     r.dvec[...] = unpack_vectors(r.vw[5])
     store(r.dvec, outs.dvec)
-    collect_done(r.oblk, r.oland, r.ys, r.yr)
-    store(r.oland, outs.out)
-    reduce_out(1)
-    reduce(0, 4)
     collect_done(r.gblk, r.gland, r.zs, r.zr)
     store(r.gland, outs.gh)
-    reduce_out(0)
     wait_sent()
     for copy in stored:
         copy.wait()
@@ -1422,7 +1475,6 @@
     half = model // 2
     n = len(dims.chunks)
     scratch = dict(
-        xin=vmem(block, BF),
         cin=vmem(block, BF),
         oblk=vmem(block, BF),
         gblk=vmem(block, BF),
@@ -1433,12 +1485,12 @@
         xs=vmem((2, tok, model), BF),
         xr=vmem((2, tok, model), BF),
         eo=vmem((tok, model), BF),
-        px=vmem((tok, model), BF),
-        prx=vmem((2, tok // 2, model), BF),
-        pz=vmem((2, tok // 2, model), BF),
-        pzr=vmem((2, 2, tok // 2, model), BF),
-        ps=dma((2, 5)),
-        pr=dma((2, 5)),
+        px=vmem((4, tok, model), BF),
+        prx=vmem((4, tok // 2, model), BF),
+        pz=vmem((4, tok // 2, model), BF),
+        pzr=vmem((4, 2, tok // 2, model), BF),
+        ps=dma((4, 5)),
+        pr=dma((4, 5)),
         hot=vmem((dims.lanes, model), BF),
         gs=dma((n, 20)),
         gr=dma((n, 20)),
@@ -1461,8 +1513,6 @@
         is_=dma((4,)),
         ir=dma((4,)),
         os=dma((4,)),
-        ks=dma((4,)),
-        kr=dma((4,)),
         es=dma((2,)),
         er=dma((2,)),
         ins=dma((16,)),
@@ -1511,7 +1561,7 @@
                 wa=vmem((model, sizes.wide), BF),
                 w=vmem((2, sizes.zs, SIDE, sizes.nr, model), BF),
                 dw=vmem((2, sizes.zs, SIDE, sizes.nr, model), BF),
-                xb=vmem((tok, model), BF),
+                xb=vmem((2,) + block, BF),
                 q=vmem((tok, sizes.hc), BF),
                 kv=vmem((2, tok, 2 * sizes.hc), BF),
                 a=vmem((sizes.heads, tok, seq), BF),
@@ -1525,8 +1575,7 @@
                 n2=vmem((tok, model), F32),
                 s2=vmem((tok, 1), F32),
                 dkv=vmem((2, tok, 2 * sizes.hc), BF),
-                dkr=vmem((tok, 2 * sizes.hc), BF),
-                dp=vmem((tok, sizes.wide if sizes.pad else sizes.start), BF),
+                dq=vmem((tok, 2 * sizes.hc if sizes.pad else sizes.hc), BF),
             )
         )
     inputs, outputs = jax.tree.leaves(given), jax.tree.leaves(outs)

time: 210 us -> 197 us (0.938); the launches traced: 208 us -> 197 us
  Pallas kernels: 207 us -> 196 us
    pallas_call x1, Pallas kernels: 204 us -> 193 us  [fused_call(): pl.pallas_call(functools.partial(fused_kernel, dims, jax.tree.structure((...]
where the time goes in v4:
time: 197 us
  Pallas kernels  196 us (99%)
    pallas_call x1, Pallas kernels, fused_call(): pl.pallas_call(functools.partial(fused_kernel, dims, jax.tree.structure((...  193 us

profile of v4, /device:TPU:0, one launch (start us, length us, event | category | flops | bytes accessed | tf_op | source)
XLA Modules:
  0.0 197.0 jit_solution(4187383569025447193)
XLA Ops:
  0.7 193.1 %layers.1 = (f32[1,512]{1,0:T(1,128)}, bf16[2,64,768]{2,1,0:T(8,128)(2,1)}, f32[2,24,1536]{2,1,0:T(8,128)}, f32[2,2,192,192]{3,2,1,0:T(8,128)}, f32[2,24,768]{2,...) custom-call(bf16[2,64,768]{2,1,0:T(8,128)(2,1)} %refs_0_.1, bf16[2,64,768]{2,1,0:T(8,128)(2,1)} %refs_1_.1, ...), custom_call_target="tpu_custom_call" | custom-call | tf_op jit(solution)/shard_map/layers/pallas_call | solution.py:1584
  193.8 3.0 %finish.1 = (bf16[2,64,768]{2,1,0:T(8,128)(2,1)}, f32[2,64,768]{2,1,0:T(8,128)}, f32[24,2304]{1,0:T(8,128)}, f32[24,768]{1,0:T(8,128)}, f32[192,384]{1,0:T(8,128...) custom-call(f32[1,512]{1,0:T(1,128)} %get-tuple-element.35.refs_0_, ...), custom_call_target="tpu_custom_call" | custom-call | tf_op jit(solution)/shard_map/finish/pallas_call | solution.py:1626

commit v5 on v4

--- a/solution.py
+++ b/solution.py
@@ -470,7 +470,10 @@
             ref = lay[layer].dw if grads else lay[layer].w
             lanes = pl.ds(pl.multiple_of(y_at * half_lanes, 128), half_lanes)
             return ref.at[which, z_slice, x_at, :, lanes]
-        begin, count = {"a": (0, full - 32), "b": (full - 32, 16), "c": (full - 16, 16)}[band]
+        if grads:
+            begin, count = {"a": (0, full - 32), "b": (full - 32, 16), "c": (full - 16, 16)}[band]
+        else:
+            begin, count = 0, full
         if kind == "A":
             ref = lay[layer].ga
             y_pick = both if y_at is None else y_at
@@ -573,44 +576,33 @@
         gather_wait(i, 3, pair_view(i, False, one(0), 1 - x, 1 - y))
         gather_wait(i, 4, pair_view(i, False, one(1), 1 - x, 1 - y))
 
+    def whole(i, z_slice, x_at, y_at):
+        return view(i, False, None, z_slice, x_at, y_at)
+
+    def line(i):
+        return (lambda zz: whole(i, one(zz), x, y)), *gather_sems(i, 0)
+
     def gather_0(i):
-        gather_push(i, 16, view(i, False, "b", one(z), x, y), xn)
-        gather_push(i, 17, view(i, False, "c", one(z), x, y), yn)
-        line_send(parts_of(i, False)[0], *gather_sems(i, 0))
+        line_send(*line(i))
 
     def gather_1(i):
-        a, b, c_part = parts_of(i, False)
-        gather_wait(i, 16, view(i, False, "b", one(z), 1 - x, y))
-        line_send(b, *gather_sems(i, 4))
-        gather_wait(i, 17, view(i, False, "c", one(z), x, 1 - y))
-        line_send(c_part, *gather_sems(i, 8))
-        line_relay(a, *gather_sems(i, 0))
+        line_relay(*line(i))
 
     def gather_2(i):
-        a, b, c_part = parts_of(i, False)
-        line_end(a, *gather_sems(i, 0))
-        own = view(i, False, "a", every, x, y)
-        gather_push(i, 12, own, xn)
-        gather_push(i, 13, own, yn)
-        line_relay(b, *gather_sems(i, 4))
-        line_relay(c_part, *gather_sems(i, 8))
+        line_end(*line(i))
+        own = whole(i, every, x, y)
+        gather_push(i, 4, own, xn)
+        gather_push(i, 5, own, yn)
 
     def gather_3(i):
-        a, b, c_part = parts_of(i, False)
-        line_end(b, *gather_sems(i, 4))
-        gather_push(i, 18, view(i, False, "b", every, both, y), yn)
-        line_end(c_part, *gather_sems(i, 8))
-        gather_push(i, 19, view(i, False, "c", every, x, None), xn)
-        gather_wait(i, 12, view(i, False, "a", every, 1 - x, y))
-        gather_wait(i, 13, view(i, False, "a", every, x, 1 - y))
-        gather_push(i, 14, view(i, False, "a", first, x, 1 - y), xn)
-        gather_push(i, 15, view(i, False, "a", second, 1 - x, y), yn)
+        gather_wait(i, 4, whole(i, every, 1 - x, y))
+        gather_wait(i, 5, whole(i, every, x, 1 - y))
+        gather_push(i, 6, whole(i, first, x, 1 - y), xn)
+        gather_push(i, 7, whole(i, second, 1 - x, y), yn)
 
     def gather_4(i):
-        gather_wait(i, 14, view(i, False, "a", first, 1 - x, 1 - y))
-        gather_wait(i, 15, view(i, False, "a", second, 1 - x, 1 - y))
-        gather_wait(i, 18, view(i, False, "b", every, both, 1 - y))
-        gather_wait(i, 19, view(i, False, "c", every, 1 - x, None))
+        gather_wait(i, 6, whole(i, first, 1 - x, 1 - y))
+        gather_wait(i, 7, whole(i, second, 1 - x, 1 - y))
 
     band_stages = (gather_0, gather_1, gather_2, gather_3, gather_4)
     pair_stages = (pair_0, pair_1, pair_2, pair_3)
@@ -1146,105 +1138,105 @@
     for copy in fetched[:2]:
         copy.wait()
     own_a0 = pack_a(0)
-    fetched[2].wait()
-    spread(r.hid, kept[0].xb.at[lax.rem(z // 2, 2)], r.hs, r.hr)
+    prepare_a(0, own_a0)
+    gather(0, 0)
     for copy in fetched[3:5]:
         copy.wait()
     own_f0 = pack_f(0)
-    prepare_f(0, own_f0)
-    gather(2, 0)
-    spread_turn(r.hid, kept[0].xb.at[half], r.hs, r.hr, r.os.at[0], r.os.at[1])
     for copy in fetched[5:]:
         copy.wait()
+    own_a1 = pack_a(1)
     r.vw[0] = pack_vectors()
-    own_a1 = pack_a(1)
+    gather(0, 1)
+    fetched[2].wait()
+    spread(r.hid, kept[0].xb.at[lax.rem(z // 2, 2)], r.hs, r.hr)
+    prepare_f(0, own_f0)
+    prepare_a(1, own_a1)
+    gather(1, 0)
+    gather(0, 2)
+    own_f1 = pack_f(1)
+    total_step(r.vw, r.vl, 0, r.vs, r.vr)
+    spread_turn(r.hid, kept[0].xb.at[half], r.hs, r.hr, r.os.at[0], r.os.at[1])
+    gather(1, 1)
     spread_end(kept[0].xb.at[half], r.os.at[0], r.os.at[1])
-    gather(3, 0)
-    prepare_a(0, own_a0)
+    total_add(r.vw, r.vl, 0, r.vs, r.vr)
+    total_step(r.vw, r.vl, 1, r.vs, r.vr)
+    gather(2, 0)
+    prepare_f(1, own_f1)
+    gather(4, 0)
     share_hid = Share(kept[0].xb, 2)
-    total_step(r.vw, r.vl, 0, r.vs, r.vr)
-    gather(2, 1)
-    gather(0, 0)
-    total_add(r.vw, r.vl, 0, r.vs, r.vr)
-    gather(1, 0)
-    gather(2, 2)
-    total_step(r.vw, r.vl, 1, r.vs, r.vr)
-    gather(0, 1)
-    gather(3, 1)
+    gather(1, 2)
     total_add(r.vw, r.vl, 1, r.vs, r.vr)
-    own_f1 = pack_f(1)
-    prepare_f(1, own_f1)
-    gather(1, 1)
     total_step(r.vw, r.vl, 2, r.vs, r.vr)
-    prepare_a(1, own_a1)
-    share_hid.turn()
-    gather(0, 2)
+    gather(0, 3)
     total_add(r.vw, r.vl, 2, r.vs, r.vr)
     total_step(r.vw, r.vl, 3, r.vs, r.vr)
-    share_hid.end()
-    gather(4, 0)
-    gather(1, 2)
-    gather(6, 0)
-    gather(2, 3)
-    gather(0, 3)
+    gather(2, 1)
+    gather(3, 0)
     total_add(r.vw, r.vl, 3, r.vs, r.vr)
+    gather(1, 3)
+    share_hid.turn()
     total_step(r.vw, r.vl, 4, r.vs, r.vr)
-    gather(1, 3)
-    gather(6, 1)
     total_add(r.vw, r.vl, 4, r.vs, r.vr)
     vecs.extend([layer_vecs(0), layer_vecs(1)])
+    gather(5, 0)
     gather(0, 4)
-    gather(4, 1)
+    share_hid.end()
+    spread(r.cot, r.cin, r.cs, r.cr)
+    gather(3, 1)
     order_rows(0, 0)
     project_kv(0, half)
-    gather(3, 2)
-    gather(6, 2)
-    project_kv(0, 1 - half)
     gather(1, 4)
-    gather(5, 0)
     order_rows(0, 1)
     project_q(0)
+    gather(4, 1)
+    project_kv(0, 1 - half)
     attention(0)
+    gather(2, 2)
+    gather(6, 0)
     branch = exchange(attend_out(0))
-    gather(4, 2)
     branch = branch()
+    gather(3, 2)
     normed = norm_one(0, tokens(0, half).astype(F32), branch)
     share_normed = Share(kept[0].hb, 0)
+    gather(5, 1)
+    gather(4, 2)
     gather(3, 3)
-    gather(4, 3)
-    gather(6, 3)
-    spread(r.cot, r.cin, r.cs, r.cr)
-    gather(5, 1)
     share_normed.turn()
+    gather(2, 3)
+    gather(6, 1)
     up(0, half)
+    gather(5, 2)
     share_normed.end()
     up(0, 1 - half)
     down = Fold(lambda side, own: times_block(0, 1, side), 0)
     down.keep()
     down.cross()
-    gather(5, 2)
-    gather(4, 4)
+    gather(4, 3)
+    gather(6, 2)
     down.turn()
     branch = down.end()
     middle = norm_two(0, normed, branch)
     kept[1].xb[half] = middle.astype(BF).reshape(block_shape)
     share_middle = Share(kept[1].xb, 3)
+    gather(4, 4)
+    spread_turn(r.cot, r.cin, r.cs, r.cr, r.os.at[2], r.os.at[3])
     order_rows(1, 0)
     project_kv(1, half)
     project_q(1)
     gather(5, 3)
-    gather(6, 4)
-    spread_turn(r.cot, r.cin, r.cs, r.cr, r.os.at[2], r.os.at[3])
     share_middle.turn()
-    spread_end(r.cin, r.os.at[2], r.os.at[3])
     share_middle.end()
     project_kv(1, 1 - half)
+    gather(6, 3)
     attention(1)
     branch = exchange(attend_out(1))
     gather(5, 4)
+    spread_end(r.cin, r.os.at[2], r.os.at[3])
     branch = branch()
     normed = norm_one(1, middle, branch)
     up(1, 0)
+    gather(6, 4)
     branch = exchange(times_block(1, 1, 0))
     branch = branch()
     final = norm_two(1, normed, branch)

time: 197 us -> 188 us (0.954)
  Pallas kernels: 196 us -> 187 us
    pallas_call x1, Pallas kernels: 193 us -> 184 us  [fused_call(): pl.pallas_call(functools.partial(fused_kernel, dims, jax.tree.structure((...]
where the time goes in v5:
time: 188 us
  Pallas kernels  187 us (99%)
    pallas_call x1, Pallas kernels, fused_call(): pl.pallas_call(functools.partial(fused_kernel, dims, jax.tree.structure((...  184 us

profile of v5, /device:TPU:0, one launch (start us, length us, event | category | flops | bytes accessed | tf_op | source)
XLA Modules:
  0.0 188.0 jit_solution(18065722458093084299)
XLA Ops:
  0.7 184.1 %layers.1 = (f32[1,512]{1,0:T(1,128)}, bf16[2,64,768]{2,1,0:T(8,128)(2,1)}, f32[2,24,1536]{2,1,0:T(8,128)}, f32[2,2,192,192]{3,2,1,0:T(8,128)}, f32[2,24,768]{2,...) custom-call(bf16[2,64,768]{2,1,0:T(8,128)(2,1)} %refs_0_.1, bf16[2,64,768]{2,1,0:T(8,128)(2,1)} %refs_1_.1, ...), custom_call_target="tpu_custom_call" | custom-call | tf_op jit(solution)/shard_map/layers/pallas_call | solution.py:1576
  184.8 3.0 %finish.1 = (bf16[2,64,768]{2,1,0:T(8,128)(2,1)}, f32[2,64,768]{2,1,0:T(8,128)}, f32[24,2304]{1,0:T(8,128)}, f32[24,768]{1,0:T(8,128)}, f32[192,384]{1,0:T(8,128...) custom-call(f32[1,512]{1,0:T(1,128)} %get-tuple-element.35.refs_0_, ...), custom_call_target="tpu_custom_call" | custom-call | tf_op jit(solution)/shard_map/finish/pallas_call | solution.py:1618

commit v6 on v5

--- a/solution.py
+++ b/solution.py
@@ -470,7 +470,7 @@
             ref = lay[layer].dw if grads else lay[layer].w
             lanes = pl.ds(pl.multiple_of(y_at * half_lanes, 128), half_lanes)
             return ref.at[which, z_slice, x_at, :, lanes]
-        if grads:
+        if band:
             begin, count = {"a": (0, full - 32), "b": (full - 32, 16), "c": (full - 16, 16)}[band]
         else:
             begin, count = 0, full
@@ -717,6 +717,39 @@
         )
         reduce_store(i, total)
 
+    def line_reduce(i):
+        return (lambda zz: view(i, True, None, one(zz), x, y)), slots(i, "az"), *reduce_sems(i, 0)
+
+    def whole_reduce_0(i):
+        over = slots(i, "ad")
+        reduce_push(i, 4, view(i, True, None, first, 1 - x, 1 - y), over.at[0], xn)
+        reduce_push(i, 5, view(i, True, None, second, 1 - x, 1 - y), over.at[1], yn)
+
+    def whole_reduce_1(i):
+        over, beside = slots(i, "ad"), slots(i, "an")
+        reduce_wait(i, 4, over.at[0])
+        add_into(view(i, True, None, first, x, 1 - y), [over.at[0]])
+        reduce_push(i, 6, view(i, True, None, every, x, 1 - y), beside.at[1], yn)
+        reduce_wait(i, 5, over.at[1])
+        add_into(view(i, True, None, second, 1 - x, y), [over.at[1]])
+        reduce_push(i, 7, view(i, True, None, every, 1 - x, y), beside.at[0], xn)
+
+    def whole_reduce_2(i):
+        beside = slots(i, "an")
+        reduce_wait(i, 6, beside.at[1])
+        reduce_wait(i, 7, beside.at[0])
+        add_into(view(i, True, None, every, x, y), [beside.at[0], beside.at[1]])
+        line_reduce_send(*line_reduce(i))
+
+    def whole_reduce_3(i):
+        line_reduce_relay(*line_reduce(i))
+
+    def whole_reduce_4(i):
+        line_reduce_end(*line_reduce(i))
+        reduce_store(i, view(i, True, None, one(z), x, y)[...].astype(F32)[0])
+
+    whole_reduces = (whole_reduce_0, whole_reduce_1, whole_reduce_2, whole_reduce_3, whole_reduce_4)
+
     def pair_reduce_0(i):
         over = slots(i, "ad")
         reduce_push(i, 3, pair_view(i, True, one(0), 1 - x, 1 - y), over.at[0], xn)
@@ -778,6 +811,8 @@
 
     def reduce(i, stage):
         stages = pair_reduces if chunks[i][0] == "P" else band_reduces
+        if chunks[i][0] in dims.whole:
+            stages = whole_reduces
         if stage < len(stages):
             stages[stage](i)
 
@@ -1150,77 +1185,77 @@
     gather(0, 1)
     fetched[2].wait()
     spread(r.hid, kept[0].xb.at[lax.rem(z // 2, 2)], r.hs, r.hr)
-    prepare_f(0, own_f0)
+    total_step(r.vw, r.vl, 0, r.vs, r.vr)
+    total_add(r.vw, r.vl, 0, r.vs, r.vr)
+    total_step(r.vw, r.vl, 1, r.vs, r.vr)
     prepare_a(1, own_a1)
     gather(1, 0)
     gather(0, 2)
+    gather(1, 1)
+    total_add(r.vw, r.vl, 1, r.vs, r.vr)
+    prepare_f(0, own_f0)
     own_f1 = pack_f(1)
-    total_step(r.vw, r.vl, 0, r.vs, r.vr)
     spread_turn(r.hid, kept[0].xb.at[half], r.hs, r.hr, r.os.at[0], r.os.at[1])
-    gather(1, 1)
     spread_end(kept[0].xb.at[half], r.os.at[0], r.os.at[1])
-    total_add(r.vw, r.vl, 0, r.vs, r.vr)
-    total_step(r.vw, r.vl, 1, r.vs, r.vr)
+    total_step(r.vw, r.vl, 2, r.vs, r.vr)
     gather(2, 0)
+    gather(1, 2)
+    share_hid = Share(kept[0].xb, 2)
+    total_add(r.vw, r.vl, 2, r.vs, r.vr)
+    gather(0, 3)
     prepare_f(1, own_f1)
+    gather(3, 0)
+    total_step(r.vw, r.vl, 3, r.vs, r.vr)
+    gather(1, 3)
+    total_add(r.vw, r.vl, 3, r.vs, r.vr)
+    gather(2, 1)
+    total_step(r.vw, r.vl, 4, r.vs, r.vr)
+    share_hid.turn()
+    gather(3, 1)
     gather(4, 0)
-    share_hid = Share(kept[0].xb, 2)
-    gather(1, 2)
-    total_add(r.vw, r.vl, 1, r.vs, r.vr)
-    total_step(r.vw, r.vl, 2, r.vs, r.vr)
-    gather(0, 3)
-    total_add(r.vw, r.vl, 2, r.vs, r.vr)
-    total_step(r.vw, r.vl, 3, r.vs, r.vr)
-    gather(2, 1)
-    gather(3, 0)
-    total_add(r.vw, r.vl, 3, r.vs, r.vr)
-    gather(1, 3)
-    share_hid.turn()
-    total_step(r.vw, r.vl, 4, r.vs, r.vr)
+    share_hid.end()
+    gather(0, 4)
     total_add(r.vw, r.vl, 4, r.vs, r.vr)
     vecs.extend([layer_vecs(0), layer_vecs(1)])
-    gather(5, 0)
-    gather(0, 4)
-    share_hid.end()
-    spread(r.cot, r.cin, r.cs, r.cr)
-    gather(3, 1)
     order_rows(0, 0)
     project_kv(0, half)
     gather(1, 4)
     order_rows(0, 1)
     project_q(0)
+    project_kv(0, 1 - half)
+    gather(5, 0)
+    attention(0)
     gather(4, 1)
-    project_kv(0, 1 - half)
-    attention(0)
+    spread(r.cot, r.cin, r.cs, r.cr)
     gather(2, 2)
-    gather(6, 0)
     branch = exchange(attend_out(0))
     branch = branch()
-    gather(3, 2)
+    gather(5, 1)
     normed = norm_one(0, tokens(0, half).astype(F32), branch)
     share_normed = Share(kept[0].hb, 0)
-    gather(5, 1)
+    gather(3, 2)
+    gather(2, 3)
+    gather(6, 0)
     gather(4, 2)
+    up(0, half)
+    share_normed.turn()
     gather(3, 3)
-    share_normed.turn()
-    gather(2, 3)
-    gather(6, 1)
-    up(0, half)
-    gather(5, 2)
     share_normed.end()
     up(0, 1 - half)
+    gather(6, 1)
+    gather(5, 2)
     down = Fold(lambda side, own: times_block(0, 1, side), 0)
     down.keep()
     down.cross()
     gather(4, 3)
+    down.turn()
+    spread_turn(r.cot, r.cin, r.cs, r.cr, r.os.at[2], r.os.at[3])
     gather(6, 2)
-    down.turn()
     branch = down.end()
     middle = norm_two(0, normed, branch)
     kept[1].xb[half] = middle.astype(BF).reshape(block_shape)
     share_middle = Share(kept[1].xb, 3)
     gather(4, 4)
-    spread_turn(r.cot, r.cin, r.cs, r.cr, r.os.at[2], r.os.at[3])
     order_rows(1, 0)
     project_kv(1, half)
     project_q(1)
@@ -1228,12 +1263,12 @@
     share_middle.turn()
     share_middle.end()
     project_kv(1, 1 - half)
+    spread_end(r.cin, r.os.at[2], r.os.at[3])
+    attention(1)
     gather(6, 3)
-    attention(1)
     branch = exchange(attend_out(1))
+    branch = branch()
     gather(5, 4)
-    spread_end(r.cin, r.os.at[2], r.os.at[3])
-    branch = branch()
     normed = norm_one(1, middle, branch)
     up(1, 0)
     gather(6, 4)
@@ -1347,90 +1382,90 @@
     reduce(6, 0)
     back_up(1)
     branch = exchange(times_block(1, 0, 0))
+    weight_grad(1, 0, kept[1].hb)
+    reduce(5, 0)
     branch = branch()
     dz1, grad_ctx = back_one(1, dz2 + branch)
     attention_back(1, grad_ctx)
-    reduce(6, 1)
     down = Fold(lambda side, own: back_hidden(1, side, own), 2)
     down.keep()
     down.cross()
+    reduce(6, 1)
     projection_grad(1, 0)
     bias_sums(1)
     reduce(4, 0)
-    weight_grad(1, 0, kept[1].hb)
     down.turn()
-    reduce(5, 0)
     branch = down.end()
     dz2 = back_two(0, dz1 + branch)
     share_grad = Share(kept[0].eo, 1)
+    reduce(5, 1)
     reduce(4, 1)
-    reduce(5, 1)
     share_grad.turn()
     share_grad.end()
     weight_grad(0, 1, kept[0].eo)
     reduce(3, 0)
     back_up(0)
-    up_back = Fold(lambda side, own: times_block(0, 0, side), 1)
     weight_grad(0, 0, kept[0].hb)
     reduce(2, 0)
+    up_back = Fold(lambda side, own: times_block(0, 0, side), 1)
     up_back.keep()
+    reduce(3, 1)
     up_back.cross()
+    reduce(2, 1)
     reduce(6, 2)
-    reduce(4, 2)
     reduce(5, 2)
-    reduce(3, 1)
     up_back.turn()
     collect_done(r.oblk, r.oland, r.ys, r.yr)
     store(r.oland, outs.out)
     branch = up_back.end()
-    reduce(2, 1)
     dz1, grad_ctx = back_one(0, dz2 + branch)
     attention_back(0, grad_ctx)
+    reduce(6, 3)
+    projection_grad(0, 1)
+    reduce(1, 0)
+    projection_grad(0, 0)
+    bias_sums(0)
+    total_step(r.vw, r.vl, 0, r.ws, r.wr)
+    reduce(4, 2)
+    reduce(0, 0)
+    total_add(r.vw, r.vl, 0, r.ws, r.wr)
     reduce(3, 2)
     to_hidden = Fold(lambda side, own: back_hidden(0, side, own), 3)
-    projection_grad(0, 1)
-    reduce(1, 0)
+    reduce(6, 4)
+    total_step(r.vw, r.vl, 1, r.ws, r.wr)
     to_hidden.keep()
     to_hidden.cross()
-    reduce(5, 3)
-    reduce(2, 2)
-    reduce(4, 3)
-    projection_grad(0, 0)
-    bias_sums(0)
-    reduce(0, 0)
-    total_step(r.vw, r.vl, 0, r.ws, r.wr)
-    total_add(r.vw, r.vl, 0, r.ws, r.wr)
     reduce(1, 1)
-    total_step(r.vw, r.vl, 1, r.ws, r.wr)
-    reduce(6, 3)
-    reduce(5, 4)
-    reduce(1, 2)
-    reduce(0, 1)
     total_add(r.vw, r.vl, 1, r.ws, r.wr)
     total_step(r.vw, r.vl, 2, r.ws, r.wr)
+    reduce(2, 2)
     to_hidden.turn()
-    reduce(3, 3)
+    reduce(0, 1)
+    reduce(5, 3)
+    reduce(1, 2)
     total_add(r.vw, r.vl, 2, r.ws, r.wr)
-    reduce(4, 4)
-    reduce_out(3)
-    total_step(r.vw, r.vl, 3, r.ws, r.wr)
-    branch = to_hidden.end()
-    reduce(6, 4)
+    reduce(4, 3)
     reduce(2, 3)
     reduce(1, 3)
+    reduce(3, 3)
+    total_step(r.vw, r.vl, 3, r.ws, r.wr)
     reduce(0, 2)
-    reduce_out(5)
+    reduce(0, 3)
+    branch = to_hidden.end()
+    reduce(1, 4)
     total_add(r.vw, r.vl, 3, r.ws, r.wr)
-    reduce(1, 4)
-    reduce(0, 3)
+    reduce_out(6)
+    reduce(5, 4)
+    reduce_out(1)
+    reduce(4, 4)
     reduce_out(2)
     total_step(r.vw, r.vl, 4, r.ws, r.wr)
-    reduce(0, 4)
-    reduce_out(1)
-    reduce_out(6)
+    reduce_out(5)
+    reduce_out(3)
     reduce_out(4)
     r.gblk[...] = (dz1 + branch).astype(BF).reshape(r.gblk.shape)
     collect(r.gblk, r.gland, r.zs, r.zr)
+    reduce(0, 4)
     reduce_out(0)
     total_add(r.vw, r.vl, 4, r.ws, r.wr)
     r.dvec[...] = unpack_vectors(r.vw[5])
@@ -1513,11 +1548,12 @@
         lay=[],
     )
     rows_f, rows_p = dims.unit_rows["F"], dims.unit_rows["P"]
-    for count, rows, wide, pair, shard in (
-        (counts[0], rows_a - 32, model, (2, 4, 16, model), (rows_in, model)),
-        (counts[1], rows_f - 32, half, (4, 16, model), (rows_f, half // 2)),
+    for count, rows, wide, pair, shard, kind in (
+        (counts[0], rows_a, model, (2, 4, 16, model), (rows_in, model), "A"),
+        (counts[1], rows_f, half, (4, 16, model), (rows_f, half // 2), "F"),
     ):
         line = pair[:-3] + (1, 16, model)
+        rows -= 0 if kind in dims.whole else 32
         scratch["red"].append(
             dict(
                 ad=vmem((count, 2, 2, rows, wide), BF),
@@ -1659,6 +1695,7 @@
         chunks=chunks,
         slot=slot,
         rows=rows,
+        whole='A',
         unit_rows={"A": 2 * teacher[0].shape[0], "F": rows, "P": layers[0].nr},
         rows_of=rows_of,
         base=base,

time: 188 us -> 186 us (0.989)
  Pallas kernels: 187 us -> 184 us
    pallas_call x1, Pallas kernels: 184 us -> 181 us  [fused_call(): pl.pallas_call(functools.partial(fused_kernel, dims, jax.tree.structure((...]
where the time goes in v6:
time: 186 us; the launch traced here: 185 us
  Pallas kernels  184 us (99%)
    pallas_call x1, Pallas kernels, fused_call(): pl.pallas_call(functools.partial(fused_kernel, dims, jax.tree.structure((...  181 us

profile of v6, /device:TPU:0, one launch (start us, length us, event | category | flops | bytes accessed | tf_op | source)
XLA Modules:
  0.0 185.1 jit_solution(1079636453869424038)
XLA Ops:
  0.7 181.2 %layers.1 = (f32[1,512]{1,0:T(1,128)}, bf16[2,64,768]{2,1,0:T(8,128)(2,1)}, f32[2,24,1536]{2,1,0:T(8,128)}, f32[2,2,192,192]{3,2,1,0:T(8,128)}, f32[2,24,768]{2,...) custom-call(bf16[2,64,768]{2,1,0:T(8,128)(2,1)} %refs_0_.1, bf16[2,64,768]{2,1,0:T(8,128)(2,1)} %refs_1_.1, ...), custom_call_target="tpu_custom_call" | custom-call | tf_op jit(solution)/shard_map/layers/pallas_call | solution.py:1612
  181.9 3.0 %finish.1 = (bf16[2,64,768]{2,1,0:T(8,128)(2,1)}, f32[2,64,768]{2,1,0:T(8,128)}, f32[24,2304]{1,0:T(8,128)}, f32[24,768]{1,0:T(8,128)}, f32[192,384]{1,0:T(8,128...) custom-call(f32[1,512]{1,0:T(1,128)} %get-tuple-element.35.refs_0_, ...), custom_call_target="tpu_custom_call" | custom-call | tf_op jit(solution)/shard_map/finish/pallas_call | solution.py:1654

commit v7 on v6

--- a/solution.py
+++ b/solution.py
@@ -956,7 +956,7 @@
             k, v = head_kv(at, h)
             scores = jnp.where(valid, mm(q, k, 1, 1) * 0.125, NEGATIVE)
             exponent = jnp.exp(scores - jnp.max(scores, axis=1, keepdims=True))
-            low = (exponent / jnp.sum(exponent, axis=1, keepdims=True)).astype(BF)
+            low = (exponent * (1.0 / jnp.sum(exponent, axis=1, keepdims=True))).astype(BF)
             keep.a[h] = low
             begin = sizes.pad + h * HEAD
             keep.ctx[:, begin : begin + HEAD] = mm(low, v, 1, 0).astype(BF)

time: 186 us -> 186 us (level)
  no operation moved by 1% of the time
where the time goes in v7:
time: 186 us; the launch traced here: 185 us
  Pallas kernels  184 us (99%)
    pallas_call x1, Pallas kernels, fused_call(): pl.pallas_call(functools.partial(fused_kernel, dims, jax.tree.structure((...  181 us

profile of v7, /device:TPU:0, one launch (start us, length us, event | category | flops | bytes accessed | tf_op | source)
XLA Modules:
  0.0 185.1 jit_solution(1079636453869424038)
XLA Ops:
  0.7 181.2 %layers.1 = (f32[1,512]{1,0:T(1,128)}, bf16[2,64,768]{2,1,0:T(8,128)(2,1)}, f32[2,24,1536]{2,1,0:T(8,128)}, f32[2,2,192,192]{3,2,1,0:T(8,128)}, f32[2,24,768]{2,...) custom-call(bf16[2,64,768]{2,1,0:T(8,128)(2,1)} %refs_0_.1, bf16[2,64,768]{2,1,0:T(8,128)(2,1)} %refs_1_.1, ...), custom_call_target="tpu_custom_call" | custom-call | tf_op jit(solution)/shard_map/layers/pallas_call | solution.py:1612
  181.9 3.0 %finish.1 = (bf16[2,64,768]{2,1,0:T(8,128)(2,1)}, f32[2,64,768]{2,1,0:T(8,128)}, f32[24,2304]{1,0:T(8,128)}, f32[24,768]{1,0:T(8,128)}, f32[192,384]{1,0:T(8,128...) custom-call(f32[1,512]{1,0:T(1,128)} %get-tuple-element.35.refs_0_, ...), custom_call_target="tpu_custom_call" | custom-call | tf_op jit(solution)/shard_map/finish/pallas_call | solution.py:1654
